TPU v7x, 32 devices: a whole 2x2x4 slice. The times are simulated.
32 devices in a mesh: tm: 4 (over y, x), tile: 8 (over z, core).
Axes of the slice: x: 2, y: 2, z: 4, core: 2. Of those that a mesh axis runs over, the one named last changes fastest.
Arguments:
- features: bfloat16 [8, 64, 16, 512], P('tm', None, 'tile'), may hold values from -6 to 6
- aligned: bfloat16 [8, 128, 16, 512], P('tm', None, 'tile'), may hold values from -6 to 6
- cotangent: bfloat16 [8, 64, 16, 512], P('tm', None, 'tile'), may hold values from -6 to 6
- weight: bfloat16 [9, 64, 192], replicated, may hold values from -0.15625 to 0.15625
- src_tile: int32 [8, 64, 2], P('tm', 'tile'), may hold values from 0 to 7, all different within a row; in each aligned block of 8 rows (0 to 7, 8 to 15, ..., all dimensions but the last counted through in order) at most 4 rows name the same one
- src_blk: int32 [8, 64, 2], P('tm', 'tile'), may hold values from 0 to 7
Outputs:
- grad_weight: float32 [9, 64, 192], replicated
- grad_feat: bfloat16 [8, 64, 16, 512], P('tm', None, 'tile')
- grad_prop: bfloat16 [8, 64, 16, 512], P('tm', None, 'tile')
Inputs may be any that keep to these rules, and one draw needn't show every extreme that they name: `src_tile`: within one frame, the 8 blocks of one band name no source band more than 4 times over both orders, and the two orders of a block name different bands.
All inputs are finite; a program needn't handle non-finite values.
Results may differ from a plain program's by a relative error of at most 0.0057.
Values may be sent and summed in bfloat16 or wider, within the bound.
No kernel may reach another device: no remote copies, remote signals or barrier semaphores. Data moves between devices by JAX's collectives and lax.ppermute only.
A program may use at most 64 MiB of HBM per device.

v0:
```python
import math

import jax
import jax.numpy as jnp
from jax import lax
from jax.sharding import PartitionSpec as P


def with_halo(cells, sides, width):
    for axis, dim in sides:
        count = lax.axis_size(axis)
        ends = count - 1
        head = lax.slice_in_dim(cells, 0, width, axis=dim)
        tail = lax.slice_in_dim(cells, cells.shape[dim] - width, cells.shape[dim], axis=dim)
        cells = jnp.concatenate(
            [
                lax.ppermute(tail, axis, [(i, (i + 1) % count) for i in range(ends)]),
                cells,
                lax.ppermute(head, axis, [((i + 1) % count, i) for i in range(ends)]),
            ],
            axis=dim,
        )
    return cells


def passed_along(block, axis, distance):
    devices = range(lax.axis_size(axis))
    route = [(i - distance, i) for i in devices if i - distance in devices]
    return lax.ppermute(block, axis, route)


def pad_columns(values):
    return jnp.pad(values, ((0, 0), (0, 0), (0, 0), (1, 1)))


def act_slope(preact):
    return 0.1 + 0.9 * jax.nn.sigmoid(preact)


def conv_forward(weight, padded_input, height):
    columns = padded_input.shape[3] - 2
    summed = jnp.zeros((padded_input.shape[0], weight.shape[1], height, columns), jnp.float32)
    for row_tap in range(3):
        for col_tap in range(3):
            window = padded_input[:, :, row_tap : row_tap + height, col_tap : col_tap + columns]
            summed = summed + jnp.einsum(
                "oi,firc->forc",
                weight[3 * row_tap + col_tap],
                window,
                preferred_element_type=jnp.float32,
            )
    return summed


def conv_transpose(weight, padded_input, height):
    columns = padded_input.shape[3] - 2
    summed = jnp.zeros((padded_input.shape[0], weight.shape[2], height, columns), jnp.float32)
    for row_tap in range(3):
        for col_tap in range(3):
            window = padded_input[
                :, :, 2 - row_tap : 2 - row_tap + height, 2 - col_tap : 2 - col_tap + columns
            ]
            summed = summed + jnp.einsum(
                "oi,forc->firc",
                weight[3 * row_tap + col_tap],
                window,
                preferred_element_type=jnp.float32,
            )
    return summed.astype(jnp.bfloat16)


def weight_grad(padded_input, cot_pre):
    height = cot_pre.shape[2]
    columns = cot_pre.shape[3]
    term_list = []
    for row_tap in range(3):
        for col_tap in range(3):
            window = padded_input[:, :, row_tap : row_tap + height, col_tap : col_tap + columns]
            term_list.append(
                jnp.einsum("forc,firc->oi", cot_pre, window, preferred_element_type=jnp.float32)
            )
    return jnp.stack(term_list)


def build_slots(aligned_grad, tiles, blocks, tile_count, capacity):
    frames, stacked, height, columns = aligned_grad.shape
    block_count = tiles.shape[1]
    pixels = height * columns // block_count
    pieces = aligned_grad.reshape(frames, 2, stacked // 2, block_count, pixels)
    row_ids = jnp.arange(2 * block_count, dtype=jnp.int32)
    destination = jnp.swapaxes(tiles, 1, 2).reshape(frames, 2 * block_count)
    target_code = (
        jnp.swapaxes(blocks, 1, 2).reshape(frames, 2 * block_count)
        + (row_ids // block_count * block_count)[None, :]
    )
    tile_hit_count = (
        destination[:, :, None] == jnp.arange(tile_count, dtype=jnp.int32)[None, None, :]
    ).astype(jnp.int32)
    earlier = jnp.cumsum(tile_hit_count, axis=1) - tile_hit_count
    slot_ids = destination * capacity + jnp.sum(tile_hit_count * earlier, axis=2)
    source_selector = (
        slot_ids[:, None, :] == jnp.arange(tile_count * capacity, dtype=jnp.int32)[None, :, None]
    ).astype(jnp.bfloat16)
    target_onehot = (target_code[:, :, None] == row_ids[None, None, :]).astype(jnp.bfloat16)
    placing = jnp.einsum(
        "anu,auo->ano", source_selector, target_onehot, preferred_element_type=jnp.float32
    ).astype(jnp.bfloat16)
    select_split = source_selector.reshape(frames, tile_count * capacity, 2, block_count)
    payload = jnp.einsum(
        "fsob,focbp->fscp", select_split, pieces, preferred_element_type=jnp.float32
    ).astype(jnp.bfloat16)
    return (payload, placing)


def place_blocks(received):
    payload, placing = received
    return jnp.einsum("fsb,fscp->fcbp", placing, payload, preferred_element_type=jnp.float32)


def deliver(aligned_grad, tiles, blocks, tile_count, capacity):
    payload, placing = build_slots(aligned_grad, tiles, blocks, tile_count, capacity)
    return place_blocks(
        (
            lax.all_to_all(payload, "tile", split_axis=1, concat_axis=1, tiled=True),
            lax.all_to_all(placing, "tile", split_axis=1, concat_axis=1, tiled=True),
        )
    )


def body(features, aligned, cotangent, weight, src_tile, src_blk):
    frames, channels, height, columns = features.shape
    inputs = jnp.concatenate((features, aligned), axis=1)
    padded_in = pad_columns(with_halo(inputs, (("tile", 2),), 1))
    preact = conv_forward(weight, padded_in, height)
    cot_pre = (cotangent * act_slope(preact)).astype(jnp.bfloat16)
    padded_cot = pad_columns(with_halo(cot_pre, (("tile", 2),), 1))
    tile_count = lax.axis_size("tile")
    block_count = src_tile.shape[1]
    capacity = max(2, (4 * block_count + tile_count - 1) // tile_count)
    input_grad = conv_transpose(weight, padded_cot, height)
    local_weight = weight_grad(padded_in, cot_pre)
    feat_grad = input_grad[:, :channels]
    aligned_grad = input_grad[:, channels:]
    arrived = deliver(aligned_grad, src_tile, src_blk, tile_count, capacity)
    landed = arrived.reshape(frames, channels, 2, height, columns)
    extended = jnp.pad(landed[:, :, 0], ((1, 1), (0, 0), (0, 0), (0, 0))) + jnp.pad(
        landed[:, :, 1], ((0, 2), (0, 0), (0, 0), (0, 0))
    )
    arriving = passed_along(extended[:2], "tm", -1)
    resident = extended[2:]
    resident = jnp.concatenate((resident[: frames - 2], resident + arriving), axis=0)
    total_weight = lax.psum(local_weight, ("tm", "tile"))
    pixels = frames * lax.axis_size("tm") * height * tile_count * columns
    grad_weight = total_weight * (1.0 / math.sqrt(pixels))
    return (grad_weight, feat_grad, resident.astype(jnp.bfloat16))


def solution(mesh):
    in_specs = (
        P("tm", None, "tile", None),
        P("tm", None, "tile", None),
        P("tm", None, "tile", None),
        P(),
        P("tm", "tile", None),
        P("tm", "tile", None),
    )
    out_specs = (P(), P("tm", None, "tile", None), P("tm", None, "tile", None))
    return jax.shard_map(body, mesh=mesh, in_specs=in_specs, out_specs=out_specs, check_vma=False)
```

profile of v0, /device:TPU:0, one launch (start us, length us, event | category | flops | bytes accessed | tf_op | source)
XLA Modules:
  0.0 229.3 jit_solution(3724605691295087058)
XLA Ops:
  8.2 1.1 copy_dynamic-update-slice_fusion
  9.3 1.3 collective-permute-start.1
  10.6 3.1 %collective-permute-start = (bf16[2,192,1,512]{3,1,2,0:T(8,128)(2,1)S(1)}, bf16[2,192,1,512]{3,1,2,0:T(8,128)(2,1)S(1)}, u32[]{:S(2)}, u32[]{:S(2)}) collective-permute-start(bf16[2,192,1,512]{3,1,2,0:T(8,128)(2,1)S(1)} %get-tuple-element.14), channel_id=1, source_target_pairs={{0,1},{1,2},{2,3},{3,4},{4,5},{5,6},{6,7},{8,9},{9,10},{10,11},{11... | collective-permute-start | bytes 1179656 | tf_op jit(solution)/shard_map/ppermute | solution.py:17
  15.1 6.3 %all-to-all-start.1 = ((bf16[2,32,16]{2,0,1:T(2,128)(2,1)}), bf16[2,32,16]{2,0,1:T(2,128)(2,1)S(1)}, u32[]{:S(2)}, u32[]{:S(2)}) async-start(bf16[2,32,16]{2,0,1:T(2,128)(2,1)} %copy.28), calls=%async_computation.1 | async-start | bytes 32768 | tf_op jit(solution)/shard_map/all_to_all | solution.py:125
  23.2 1.1 fusion.5
  27.7 2.4 %collective-permute-start.2 = (bf16[2,64,1,512]{3,1,2,0:T(8,128)(2,1)S(1)}, bf16[2,64,1,512]{3,1,2,0:T(8,128)(2,1)S(1)}, u32[]{:S(2)}, u32[]{:S(2)}) collective-permute-start(bf16[2,64,1,512]{3,1,2,0:T(8,128)(2,1)S(1)} %get-tuple-element.17), channel_id=1, source_target_pairs={{0,1},{1,2},{2,3},{3,4},{4,5},{5,6},{6,7},{8,9},{9,10},{10,11},{11... | collective-permute-start | bytes 393224 | tf_op jit(solution)/shard_map/ppermute | solution.py:17
  30.1 1.3 collective-permute-start.3
  31.8 2.7 %collective-permute-done.3 = bf16[2,64,1,512]{3,1,2,0:T(8,128)(2,1)S(1)} collective-permute-done((bf16[2,64,1,512]{3,1,2,0:T(8,128)(2,1)S(1)}, bf16[2,64,1,512]{3,1,2,0:T(8,128)(2,1)S(1)}, u32[]{:S(2)}, u32[]{:S(2)}) %collective-permute-start.3) | collective-permute-done | bytes 131104 | tf_op jit(solution)/shard_map/ppermute | solution.py:19
  37.9 1.7 fusion.32
  40.6 1.3 copy.25
  41.9 1.4 reshape.60
  43.3 1.2 bitcast_convert_fusion
  44.5 1.4 copy.27
  45.9 6.9 %all-to-all-start = ((bf16[2,32,64,128]{3,2,0,1:T(8,128)(2,1)}), bf16[2,32,64,128]{3,2,0,1:T(8,128)(2,1)}, u32[]{:S(2)}, u32[]{:S(2)}) async-start(bf16[2,32,64,128]{3,2,0,1:T(8,128)(2,1)} %copy.27), calls=%async_computation | async-start | bytes 2097152 | tf_op jit(solution)/shard_map/all_to_all | solution.py:124
  55.1 1.1 fusion.28
  61.2 18.5 %all-to-all-done = bf16[2,32,64,128]{3,2,0,1:T(8,128)(2,1)} async-done(((bf16[2,32,64,128]{3,2,0,1:T(8,128)(2,1)}), bf16[2,32,64,128]{3,2,0,1:T(8,128)(2,1)}, u32[]{:S(2)}, u32[]{:S(2)}) %all-to-all-start) | async-done | bytes 1048608 | tf_op jit(solution)/shard_map/all_to_all | solution.py:124
  79.7 2.9 %convolution_bitcast_fusion = f32[2,64,16,128]{3,2,1,0:T(8,128)} fusion(bf16[2,32,64,128]{3,2,0,1:T(8,128)(2,1)} %all-to-all-done, bf16[2,32,16,1]{2,0,1,3:T(2,128)(2,1)S(1)} %bitcast.202), kind=kOutput, calls=%fused_computation.12 | convolution fusion | flops 16777216 | bytes 2099200 | tf_op jit(solution)/shard_map/fsb,fscp->fcbp/dot_general | solution.py:117
  82.6 2.7 %reshape.62 = f32[2,64,2,2,512]{4,3,2,1,0:T(2,128)} reshape(f32[2,64,16,128]{3,2,1,0:T(8,128)} %convolution_bitcast_fusion) | data formatting | bytes 2097152 | tf_op jit(solution)/shard_map/reshape | solution.py:145
  85.4 1.6 slice_bitcast_fusion.1
  88.0 1.3 collective-permute-start.4
  89.3 1.1 fusion.22
  91.3 127.3 %all-reduce.6.cloned.1.call-done = f32[9,64,192]{2,1,0:T(8,128)} async-done(((f32[9,64,192]{2,1,0:T(8,128)}), f32[9,64,192]{2,1,0:T(8,128)}) %all-reduce.6.cloned.1.call-update) | async-done | bytes 442384 | tf_op jit(solution)/shard_map/psum | solution.py:152
  218.6 1.9 broadcast_multiply_fusion
  220.5 2.0 fusion.56
  (69 shorter events, 21.5 us)
Async XLA Ops:
  7.2 6.6 %copy-start.6 = (s32[2,8,2]{1,2,0:T(2,128)S(1)}, s32[2,8,2]{1,2,0:T(2,128)}, u32[]{:S(2)}) copy-start(s32[2,8,2]{1,2,0:T(2,128)} %param.10) | copy-start | bytes 388
  7.2 6.9 %copy-start.7 = (s32[2,8,2]{1,2,0:T(2,128)S(1)}, s32[2,8,2]{1,2,0:T(2,128)}, u32[]{:S(2)}) copy-start(s32[2,8,2]{1,2,0:T(2,128)} %param.11) | copy-start | bytes 388
  9.3 13.8 %collective-permute-start.1 = (bf16[2,192,1,512]{3,1,2,0:T(8,128)(2,1)S(1)}, bf16[2,192,1,512]{3,1,2,0:T(8,128)(2,1)S(1)}, u32[]{:S(2)}, u32[]{:S(2)}) collective-permute-start(bf16[2,192,1,512]{3,1,2,0:T(8,128)(2,1)S(1)} %get-tuple-element.15), channel_id=1, source_target_pairs={{1,0},{2,1},{3,2},{4,3},{5,4},{6,5},{7,6},{9,8},{10,9},{11,10},{12... | collective-permute-start | bytes 1179656 | tf_op jit(solution)/shard_map/ppermute | solution.py:19
  10.6 12.5 %collective-permute-start = (bf16[2,192,1,512]{3,1,2,0:T(8,128)(2,1)S(1)}, bf16[2,192,1,512]{3,1,2,0:T(8,128)(2,1)S(1)}, u32[]{:S(2)}, u32[]{:S(2)}) collective-permute-start(bf16[2,192,1,512]{3,1,2,0:T(8,128)(2,1)S(1)} %get-tuple-element.14), channel_id=1, source_target_pairs={{0,1},{1,2},{2,3},{3,4},{4,5},{5,6},{6,7},{8,9},{9,10},{10,11},{11... | collective-permute-start | bytes 1179656 | tf_op jit(solution)/shard_map/ppermute | solution.py:17
  15.1 30.8 %all-to-all-start.1 = ((bf16[2,32,16]{2,0,1:T(2,128)(2,1)}), bf16[2,32,16]{2,0,1:T(2,128)(2,1)S(1)}, u32[]{:S(2)}, u32[]{:S(2)}) async-start(bf16[2,32,16]{2,0,1:T(2,128)(2,1)} %copy.28), calls=%async_computation.1 | async-start | bytes 32768 | tf_op jit(solution)/shard_map/all_to_all | solution.py:125
  23.1 1.2 copy-start.5
  23.1 3.1 %copy-start.1 = (bf16[2,192,1,512]{3,1,2,0:T(8,128)(2,1)}, bf16[2,192,1,512]{3,1,2,0:T(8,128)(2,1)S(1)}, u32[]{:S(2)}) copy-start(bf16[2,192,1,512]{3,1,2,0:T(8,128)(2,1)S(1)} %collective-permute-done.1) | copy-start | bytes 1179652
  23.1 2.5 %copy-start.3 = (bf16[2,192,1,512]{3,1,2,0:T(8,128)(2,1)}, bf16[2,192,1,512]{3,1,2,0:T(8,128)(2,1)S(1)}, u32[]{:S(2)}) copy-start(bf16[2,192,1,512]{3,1,2,0:T(8,128)(2,1)S(1)} %collective-permute-done) | copy-start | bytes 1179652
  26.2 1.0 copy-start.8
  27.7 4.1 %collective-permute-start.2 = (bf16[2,64,1,512]{3,1,2,0:T(8,128)(2,1)S(1)}, bf16[2,64,1,512]{3,1,2,0:T(8,128)(2,1)S(1)}, u32[]{:S(2)}, u32[]{:S(2)}) collective-permute-start(bf16[2,64,1,512]{3,1,2,0:T(8,128)(2,1)S(1)} %get-tuple-element.17), channel_id=1, source_target_pairs={{0,1},{1,2},{2,3},{3,4},{4,5},{5,6},{6,7},{8,9},{9,10},{10,11},{11... | collective-permute-start | bytes 393224 | tf_op jit(solution)/shard_map/ppermute | solution.py:17
  30.1 4.4 %collective-permute-start.3 = (bf16[2,64,1,512]{3,1,2,0:T(8,128)(2,1)S(1)}, bf16[2,64,1,512]{3,1,2,0:T(8,128)(2,1)S(1)}, u32[]{:S(2)}, u32[]{:S(2)}) collective-permute-start(bf16[2,64,1,512]{3,1,2,0:T(8,128)(2,1)S(1)} %get-tuple-element.16), channel_id=1, source_target_pairs={{1,0},{2,1},{3,2},{4,3},{5,4},{6,5},{7,6},{9,8},{10,9},{11,10},{12... | collective-permute-start | bytes 393224 | tf_op jit(solution)/shard_map/ppermute | solution.py:19
  39.6 0.9 copy-start
  45.9 8.2 %copy-start.4 = (bf16[2,192,1,512]{3,1,2,0:T(8,128)(2,1)S(1)}, bf16[2,192,1,512]{3,1,2,0:T(8,128)(2,1)}, u32[]{:S(2)}) copy-start(bf16[2,192,1,512]{3,1,2,0:T(8,128)(2,1)} %copy-done.3) | copy-start | bytes 1179652
  45.9 33.8 %all-to-all-start = ((bf16[2,32,64,128]{3,2,0,1:T(8,128)(2,1)}), bf16[2,32,64,128]{3,2,0,1:T(8,128)(2,1)}, u32[]{:S(2)}, u32[]{:S(2)}) async-start(bf16[2,32,64,128]{3,2,0,1:T(8,128)(2,1)} %copy.27), calls=%async_computation | async-start | bytes 2097152 | tf_op jit(solution)/shard_map/all_to_all | solution.py:124
  52.8 165.8 %all-reduce.6.cloned.1.call-start = ((), (), s32[]{:S(2)}) async-start(), calls=%async_computation.2 | async-start | bytes 1179648 | tf_op jit(solution)/shard_map/psum | solution.py:152
  57.1 3.1 %copy-start.2 = (bf16[2,192,1,512]{3,1,2,0:T(8,128)(2,1)S(1)}, bf16[2,192,1,512]{3,1,2,0:T(8,128)(2,1)}, u32[]{:S(2)}) copy-start(bf16[2,192,1,512]{3,1,2,0:T(8,128)(2,1)} %copy-done.1) | copy-start | bytes 1179652
  86.9 3.4 %slice-start = ((bf16[2,192,2,512]{3,1,2,0:T(8,128)(2,1)}), bf16[2,64,2,512]{3,1,2,0:T(8,128)(2,1)S(1)}, s32[]{:S(2)}) async-start(bf16[2,192,2,512]{3,1,2,0:T(8,128)(2,1)} %copy-done), calls=%async_computation.3 | async-start | bytes 524288 | tf_op jit(solution)/shard_map/slice | solution.py:142
  88.0 132.6 %collective-permute-start.4 = (f32[2,64,2,512]{3,2,1,0:T(2,128)}, f32[2,64,2,512]{3,2,1,0:T(2,128)}, u32[]{:S(2)}, u32[]{:S(2)}) collective-permute-start(f32[2,64,2,512]{3,2,1,0:T(2,128)} %pad_add_fusion), channel_id=1, source_target_pairs={{8,0},{16,8},{24,16},{9,1},{17,9},{25,17},{10,2},{18,10},{26,18},{... | collective-permute-start | bytes 1572872 | tf_op jit(solution)/shard_map/ppermute | solution.py:29
Sparse Core Ops, SparseCore 0:
  90.5 128.0 all-reduce.5
where the time goes:
time: 230 us; the launch traced here: 229 us
  waiting for transfers between devices  148 us (64%)
  starting transfers between devices  22.8 us (10%)
  matrix products  22.3 us (10%)
  between operations  14.4 us (6%)
  local copies, waits for them, and re-layouts  14.1 us (6%)
  other arithmetic  7.26 us (3%)
    psum x1, waiting for transfers between devices, body(): total_weight = lax.psum(local_weight, ('tm', 'tile'))  127 us
    all_to_all x1, waiting for transfers between devices, deliver(): lax.all_to_all(payload, 'tile', split_axis=1, concat_axis=1, tiled=True)  18.5 us
    dot_general x9, matrix products, weight_grad(): jnp.einsum('forc,firc->oi', cot_pre, window, preferred_element_type=jnp.f...  9.24 us
    all_to_all x1, starting transfers between devices, deliver(): lax.all_to_all(payload, 'tile', split_axis=1, concat_axis=1, tiled=True)  6.92 us
    all_to_all x1, starting transfers between devices, deliver(): lax.all_to_all(placing, 'tile', split_axis=1, concat_axis=1, tiled=True)  6.33 us
    ppermute x2, starting transfers between devices, with_halo(): lax.ppermute(tail, axis, [(i, (i + 1) % count) for i in range(ends)])  5.47 us
    dot_general x9, matrix products, conv_transpose(): jnp.einsum('oi,forc->firc', weight[3 * row_tap + col_tap], window, prefer...  5.1 us
  transfers between devices with their start and end apart: 8, of which 3 were waited for; matrix products, arithmetic and copies ran while one was open for 13% of the time, Pallas kernels for 0%

commit v1 on v0

--- a/solution.py
+++ b/solution.py
@@ -3,7 +3,359 @@
 import jax
 import jax.numpy as jnp
 from jax import lax
+from jax.experimental import pallas as pl
+from jax.experimental.pallas import tpu as pltpu
 from jax.sharding import PartitionSpec as P
+
+F32 = jnp.float32
+BF16 = jnp.bfloat16
+
+
+def act_slope(preact):
+    return 0.1 + 0.9 * jax.nn.sigmoid(preact)
+
+
+TABLE_ROWS = 16
+
+
+def full(memory_space=pltpu.VMEM):
+    return pl.BlockSpec(memory_space=memory_space)
+
+
+def call(kernel, out_shapes, args, scalars, scratch=(), flops=0, nbytes=1 << 20):
+    specs = [full(pltpu.SMEM)] * scalars + [full()] * (len(args) - scalars)
+    return pl.pallas_call(
+        kernel,
+        out_shape=out_shapes,
+        in_specs=specs,
+        out_specs=[full()] * len(out_shapes),
+        scratch_shapes=list(scratch),
+        cost_estimate=pl.CostEstimate(flops=flops, bytes_accessed=nbytes, transcendentals=0),
+        compiler_params=pltpu.CompilerParams(vmem_limit_bytes=48 << 20),
+    )(*args)
+
+
+def from_left(values):
+    lane = lax.broadcasted_iota(jnp.int32, values.shape, 1)
+    return jnp.where(lane == 0, 0.0, pltpu.roll(values, 1, 1))
+
+
+def from_right(values):
+    columns = values.shape[1]
+    lane = lax.broadcasted_iota(jnp.int32, values.shape, 1)
+    return jnp.where(lane == columns - 1, 0.0, pltpu.roll(values, columns - 1, 1))
+
+
+def taps_of(row):
+    wide = row.astype(F32)
+    return (from_right(wide).astype(BF16), row, from_left(wide).astype(BF16))
+
+
+def forward_kernel(pos, u, rin, rout, cot, w3, tab, msg0, msg1, g3, edge, halo):
+    core = pos[0]
+    ch = cot.shape[2]
+    halo[core] = rout[...]
+    halo[1 - core] = rin[...]
+    for f, msg in ((0, msg0), (1, msg1)):
+        rows = (halo.at[0, f], u.at[f, 0], u.at[f, 1], halo.at[1, f])
+        for r in range(2):
+            taps = jnp.dot(w3[0], rows[r][...], preferred_element_type=F32)
+            taps += jnp.dot(w3[1], rows[r + 1][...], preferred_element_type=F32)
+            taps += jnp.dot(w3[2], rows[r + 2][...], preferred_element_type=F32)
+            z = taps[ch : 2 * ch] + from_left(taps[:ch]) + from_right(taps[2 * ch :])
+            g = (cot[f, r].astype(F32) * act_slope(z)).astype(BF16)
+            msg[r * ch : (r + 1) * ch] = g
+            for k, part in enumerate(taps_of(g)):
+                g3[f, r, k * ch : (k + 1) * ch] = part
+            if f == 0:
+
+                @pl.when(core == r)
+                def _():
+                    edge[...] = g
+
+        msg[2 * ch :] = tab[f]
+
+
+def taps_kernel(pos, u, rin, rout, g3, keep, send, halo, total):
+    core = pos[0]
+    size = g3.shape[2]
+    half = keep.shape[0]
+    halo[core] = rout[...]
+    halo[1 - core] = rin[...]
+    for ky in range(3):
+        acc = jnp.zeros((size, u.shape[2]), F32)
+        for f in range(2):
+            rows = (halo.at[0, f], u.at[f, 0], u.at[f, 1], halo.at[1, f])
+            for r in range(2):
+                acc += lax.dot_general(
+                    g3[f, r], rows[r + ky][...], (((1,), (1,)), ((), ())), preferred_element_type=F32
+                )
+        total[ky * size : (ky + 1) * size] = acc
+    keep[...] = total[pl.ds(pl.multiple_of(core * half, 8), half)]
+    send[...] = total[pl.ds(pl.multiple_of((1 - core) * half, 8), half)]
+
+
+def shares_kernel(pos, keep, got, own, *others):
+    group = pos[2]
+    part = own.shape[0]
+    for k, out in enumerate((own, *others)):
+        at = pl.ds(pl.multiple_of((group ^ k) * part, 8), part)
+        out[...] = keep[at] + got[at]
+
+
+def assemble_kernel(pos, mine, theirs, out):
+    core, group = pos[0], pos[2]
+    part = mine.shape[1]
+    parts = mine.shape[0]
+    for source, side in ((mine, core), (theirs, 1 - core)):
+        for k in range(parts):
+            at = (side * parts + (group ^ k)) * part
+            out[pl.ds(pl.multiple_of(at, 8), part)] = source[k]
+
+
+def collect(pos, own, near, far, g3, tabs):
+    core, chip, chips = pos[0], pos[1], len(near) + 1
+    ch = g3.shape[1] // 3
+    step = 1 - 2 * core
+    entries = [(own, chip, core)]
+    entries += [(ref, chip - step * (k + 1), core) for k, ref in enumerate(near)]
+    entries += [(ref, chip + step * (k + 1), 1 - core) for k, ref in enumerate(far)]
+    zero = jnp.zeros(g3.shape[1:], BF16)
+    g3[0] = zero
+    g3[g3.shape[0] - 1] = zero
+    for ref, where, first in entries:
+
+        @pl.when((where >= 0) & (where < chips))
+        def _(ref=ref, where=where, first=first):
+            for h in range(2):
+                band = 2 * where + (first if h == 0 else 1 - first)
+                for r in range(2):
+                    row = 2 * band + r + 1
+                    for k, part in enumerate(taps_of(ref[h, r * ch : (r + 1) * ch])):
+                        g3[row, k * ch : (k + 1) * ch] = part
+                codes = ref[h, 2 * ch : 2 * ch + TABLE_ROWS, :128].astype(F32).astype(jnp.int32)
+                tabs[pl.ds(band, 1)] = codes[:1]
+
+
+def spread(me, g3, wt, codes, gu, first, second):
+    ch = wt.shape[0] // 2
+    size = g3.shape[1]
+    columns = g3.shape[2]
+
+    def one_row(r, _):
+        window = g3[pl.ds(r, 3)].reshape(3 * size, columns)
+        gu[...] = jnp.dot(wt[...], window, preferred_element_type=F32).astype(BF16).astype(F32)
+        for j in range(4):
+            for q, sums in ((0, first), (1, second)):
+                code = codes[r // 2, ((r % 2) * 4 + j) * 2 + q]
+
+                @pl.when(code // 8 == me)
+                def _(j=j, q=q, sums=sums, code=code):
+                    sums[code % 8] += gu[q * ch : (q + 1) * ch, 128 * j : 128 * (j + 1)]
+
+        return 0
+
+    lax.fori_loop(0, g3.shape[0] - 2, one_row, 0)
+
+
+def earlier_kernel(chips, pos, *refs):
+    n = chips - 1
+    own, near, far = refs[0], refs[1 : 1 + n], refs[1 + n : 1 + 2 * n]
+    msg0, other0, zhalo, wt = refs[1 + 2 * n : 5 + 2 * n]
+    local, passed, feat, g3, rows4, tabs, codes, gu, acc, sem = refs[5 + 2 * n :]
+    core, chip = pos[0], pos[1]
+    me = 2 * chip + core
+    ch = local.shape[1]
+    size = 3 * ch
+    collect(pos, own, near, far, g3, tabs)
+    copy = pltpu.make_async_copy(tabs, codes, sem)
+    copy.start()
+    local[...] = jnp.zeros(local.shape, F32)
+    acc[...] = jnp.zeros(acc.shape, F32)
+    columns = g3.shape[2]
+    for k, part in enumerate(taps_of(zhalo[...])):
+        rows4[3 * core, k * ch : (k + 1) * ch] = part
+    for k, part in enumerate(taps_of(other0[pl.ds(pl.multiple_of(core * ch, ch), ch)])):
+        rows4[3 * (1 - core), k * ch : (k + 1) * ch] = part
+    for r in range(2):
+        for k, part in enumerate(taps_of(msg0[r * ch : (r + 1) * ch])):
+            rows4[1 + r, k * ch : (k + 1) * ch] = part
+    for r in range(2):
+        window = rows4[r : r + 3].reshape(3 * size, columns)
+        feat[0, r] = jnp.dot(wt[:ch], window, preferred_element_type=F32).astype(BF16)
+        window = g3[pl.ds(2 * me + r, 3)].reshape(3 * size, columns)
+        feat[1, r] = jnp.dot(wt[:ch], window, preferred_element_type=F32).astype(BF16)
+    copy.wait()
+    spread(me, g3, wt.at[ch:], codes, gu, local, acc)
+    passed[...] = acc[...].astype(BF16)
+
+
+def later_kernel(chips, pos, *refs):
+    n = chips - 1
+    own, near, far = refs[0], refs[1 : 1 + n], refs[1 + n : 1 + 2 * n]
+    local, passed, wt = refs[1 + 2 * n : 4 + 2 * n]
+    prop, g3, tabs, codes, gu, sums0, sums1, sem = refs[4 + 2 * n :]
+    core, chip = pos[0], pos[1]
+    me = 2 * chip + core
+    ch = local.shape[1]
+    collect(pos, own, near, far, g3, tabs)
+    copy = pltpu.make_async_copy(tabs, codes, sem)
+    copy.start()
+    sums0[...] = local[...]
+    sums1[...] = passed[...].astype(F32)
+    copy.wait()
+    spread(me, g3, wt.at[ch:], codes, gu, sums1, sums0)
+    for s, sums in ((0, sums0), (1, sums1)):
+        for b in range(8):
+            j = b % 4
+            prop[s, b // 4, :, 128 * j : 128 * (j + 1)] = sums[b].astype(BF16)
+
+
+def total_over(parts):
+    first = parts[0]
+    for part in parts[1:]:
+        first = first + part
+    return first
+
+
+def few_bands(features, aligned, cotangent, weight, src_tile, src_blk):
+    frames, channels, height, columns = features.shape
+    inner = channels + aligned.shape[1]
+    tiles = lax.axis_size("tile")
+    groups = lax.axis_size("tm")
+    chips = tiles // 2
+    tile = lax.axis_index("tile")
+    group = lax.axis_index("tm")
+    core = tile % 2
+    pos = jnp.stack([core, tile // 2, group]).astype(jnp.int32)
+
+    cores = [(i, i ^ 1) for i in range(tiles)]
+    joints = [(2 * z + 1, 2 * z + 2) for z in range(chips - 1)]
+    joints += [(b, a) for a, b in joints]
+
+    def along(k, targets=None):
+        route = []
+        for z in range(chips - k):
+            route += [(2 * z, 2 * z + 2 * k), (2 * z + 2 * k + 1, 2 * z + 1)]
+        return [(a, b) for a, b in route if targets is None or b // 2 in targets]
+
+    def to_tile(block, route):
+        return lax.ppermute(block, "tile", route)
+
+    def to_group(block, route):
+        return lax.ppermute(block, "tm", route)
+
+    def row_of(r):
+        return jnp.concatenate(
+            [lax.dynamic_slice_in_dim(x, r, 1, axis=2)[:, :, 0] for x in (features, aligned)], axis=1
+        )
+
+    rout = to_tile(row_of(core), joints)
+    rin = to_tile(row_of(1 - core), cores)
+    u = jnp.transpose(jnp.concatenate((features, aligned), axis=1), (0, 2, 1, 3))
+    cot = jnp.transpose(cotangent, (0, 2, 1, 3))
+    w3 = weight.reshape(3, 3 * channels, inner)
+    wt = jnp.transpose(weight.reshape(3, 3 * channels, inner)[::-1].reshape(9 * channels, inner))
+    codes = (src_tile * 8 + src_blk).reshape(frames, 1, -1).astype(BF16)
+    tab = jnp.pad(codes, ((0, 0), (0, TABLE_ROWS - 1), (0, columns - codes.shape[2])))
+
+    halo = pltpu.VMEM((2, frames, inner, columns), BF16)
+    msg_shape = jax.ShapeDtypeStruct((2 * channels + TABLE_ROWS, columns), BF16)
+    msg0, msg1, g3, edge = call(
+        forward_kernel,
+        [
+            msg_shape,
+            msg_shape,
+            jax.ShapeDtypeStruct((frames, 2, 3 * channels, columns), BF16),
+            jax.ShapeDtypeStruct((channels, columns), BF16),
+        ],
+        (pos, u, rin, rout, cot, w3, tab),
+        1,
+        [halo],
+        flops=10**9,
+        nbytes=4 << 20,
+    )
+
+    def gathered(block):
+        near = [None] * (chips - 1)
+        for k in (1, 0):
+            near[k] = to_tile(block, along(k + 1))
+        near[2] = to_tile(near[1], along(1, (0, chips - 1)))
+        return near, [to_tile(x, cores) for x in near]
+
+    other1 = to_tile(msg1, cores)
+    own1 = jnp.stack((msg1, other1))
+    near1, far1 = gathered(own1)
+    other0 = to_tile(msg0, cores)
+    zhalo = to_tile(edge, joints)
+    back = [(m + 1, m) for m in range(groups - 1)]
+    own0 = to_group(jnp.stack((msg0, other0)), back)
+    near0, far0 = gathered(own0)
+
+    part_rows = 9 * channels // (2 * groups)
+    half_shape = jax.ShapeDtypeStruct((9 * channels // 2, inner), F32)
+    keep, send = call(
+        taps_kernel,
+        [half_shape, half_shape],
+        (pos, u, rin, rout, g3),
+        1,
+        [halo, pltpu.VMEM((9 * channels, inner), F32)],
+        flops=10**9,
+        nbytes=4 << 20,
+    )
+    got = to_tile(send, cores)
+    part_shape = jax.ShapeDtypeStruct((part_rows, inner), F32)
+    shares = call(shares_kernel, [part_shape] * groups, (pos, keep, got), 1)
+    swaps = [[(i, i ^ k) for i in range(groups)] for k in range(groups)]
+    share = total_over([shares[0]] + [to_group(shares[k], swaps[k]) for k in range(1, groups)])
+    turns = [[(2 * z + c, 2 * (z ^ k) + c) for z in range(chips) for c in range(2)] for k in range(chips)]
+    share = total_over([share] + [to_tile(share, turns[k]) for k in range(1, chips)])
+    pixels = frames * groups * height * tiles * columns
+    share = share * (1.0 / math.sqrt(pixels))
+    mine = jnp.stack([share] + [to_group(share, swaps[k]) for k in range(1, groups)])
+    theirs = to_tile(mine, cores)
+    (grad_weight,) = call(
+        assemble_kernel, [jax.ShapeDtypeStruct((9 * channels, inner), F32)], (pos, mine, theirs), 1
+    )
+
+    bands = 2 * chips
+    sums_shape = (8, channels, 128)
+    work = [
+        pltpu.VMEM((2 * bands + 2, 3 * channels, columns), BF16),
+        pltpu.VMEM((bands, 128), jnp.int32),
+        pltpu.SMEM((bands, 128), jnp.int32),
+        pltpu.VMEM((2 * channels, columns), F32),
+        pltpu.VMEM(sums_shape, F32),
+    ]
+    rows4 = pltpu.VMEM((4, 3 * channels, columns), BF16)
+    local, passed, feat = call(
+        lambda *refs: earlier_kernel(chips, *refs),
+        [
+            jax.ShapeDtypeStruct(sums_shape, F32),
+            jax.ShapeDtypeStruct(sums_shape, BF16),
+            jax.ShapeDtypeStruct((frames, 2, channels, columns), BF16),
+        ],
+        (pos, own1, *near1, *far1, msg0, other0, zhalo, wt),
+        1,
+        work[:1] + [rows4] + work[1:] + [pltpu.SemaphoreType.DMA],
+        flops=3 * 10**9,
+        nbytes=8 << 20,
+    )
+    passed = to_group(passed, back)
+    (prop,) = call(
+        lambda *refs: later_kernel(chips, *refs),
+        [jax.ShapeDtypeStruct((2, 2, channels, columns), BF16)],
+        (pos, own0, *near0, *far0, local, passed, wt),
+        1,
+        work + [pltpu.VMEM(sums_shape, F32), pltpu.SemaphoreType.DMA],
+        flops=3 * 10**9,
+        nbytes=8 << 20,
+    )
+    return (
+        grad_weight.reshape(9, channels, inner),
+        jnp.transpose(feat, (0, 2, 1, 3)),
+        jnp.transpose(prop, (0, 2, 1, 3)),
+    )
 
 
 def with_halo(cells, sides, width):
@@ -31,10 +383,6 @@
 
 def pad_columns(values):
     return jnp.pad(values, ((0, 0), (0, 0), (0, 0), (1, 1)))
-
-
-def act_slope(preact):
-    return 0.1 + 0.9 * jax.nn.sigmoid(preact)
 
 
 def conv_forward(weight, padded_input, height):
@@ -127,7 +475,7 @@
     )
 
 
-def body(features, aligned, cotangent, weight, src_tile, src_blk):
+def many_bands(features, aligned, cotangent, weight, src_tile, src_blk):
     frames, channels, height, columns = features.shape
     inputs = jnp.concatenate((features, aligned), axis=1)
     padded_in = pad_columns(with_halo(inputs, (("tile", 2),), 1))
@@ -165,4 +513,6 @@
         P("tm", "tile", None),
     )
     out_specs = (P(), P("tm", None, "tile", None), P("tm", None, "tile", None))
+    few = mesh.shape["tile"] == 8 and mesh.shape["tm"] == 4
+    body = few_bands if few else many_bands
     return jax.shard_map(body, mesh=mesh, in_specs=in_specs, out_specs=out_specs, check_vma=False)

time: 230 us -> 94.5 us (0.41)
  waiting for transfers between devices: 148 us -> 14.1 us
  Pallas kernels: 0 us -> 23 us
  matrix products: 22.3 us -> 0 us
  starting transfers between devices: 22.8 us -> 42.9 us
  between operations: 14.4 us -> 1.08 us
  other arithmetic: 7.26 us -> 1.31 us
  local copies, waits for them, and re-layouts: 14.1 us -> 11.5 us
    psum x1 -> x0, waiting for transfers between devices: 127 us -> none  [body(): total_weight = lax.psum(local_weight, ('tm', 'tile'))]
    ppermute x5 -> x30, starting transfers between devices: 9.34 us -> 42.9 us  [the longest x22 32.9 us: to_tile(): return lax.ppermute(block, 'tile', route)]
    pallas_call x0 -> x6, Pallas kernels: none -> 23 us  [call(): pl.pallas_call(kernel, out_shape=out_shapes, in_specs=specs, out_specs=[f...]
    dot_general x30 -> x0, matrix products: 22.3 us -> none  [the longest x9 9.24 us: weight_grad(): jnp.einsum('forc,firc->oi', cot_pre, window, preferred_element_type=jnp.f...]
    all_to_all x2 -> x0, waiting for transfers between devices: 18.5 us -> none  [the longest x1 18.5 us: deliver(): lax.all_to_all(payload, 'tile', split_axis=1, concat_axis=1, tiled=True)]
    all_to_all x2 -> x0, starting transfers between devices: 13.2 us -> none  [the longest x1 6.92 us: deliver(): lax.all_to_all(payload, 'tile', split_axis=1, concat_axis=1, tiled=True)]
    ppermute x5 -> x30, waiting for transfers between devices: 2.66 us -> 14.1 us  [the longest x8 11.8 us: to_group(): return lax.ppermute(block, 'tm', route)]
    reshape x3 -> x1, local copies, waits for them, and re-layouts: 4.18 us -> 1.14 us  [few_bands(): weight.reshape(3, 3 * channels, inner)[::-1].reshape(9 * channels, inner)]
  transfers between devices with their start and end apart: 8 -> 30, of which waited for: 3 -> 9; matrix products, arithmetic and copies ran while one was open for 13% -> 5% of each run, Pallas kernels for 0% -> 13%
where the time goes in v1:
time: 94.5 us; the launch traced here: 93.9 us
  starting transfers between devices  42.9 us (45%)
  Pallas kernels  23 us (24%)
  waiting for transfers between devices  14.1 us (15%)
  local copies, waits for them, and re-layouts  11.5 us (12%)
  other arithmetic  1.31 us (1%)
  between operations  1.08 us (1%)
    ppermute x22, starting transfers between devices, to_tile(): return lax.ppermute(block, 'tile', route)  32.9 us
    pallas_call x6, Pallas kernels, call(): pl.pallas_call(kernel, out_shape=out_shapes, in_specs=specs, out_specs=[f...  23 us
    ppermute x8, waiting for transfers between devices, to_group(): return lax.ppermute(block, 'tm', route)  11.8 us
    ppermute x8, starting transfers between devices, to_group(): return lax.ppermute(block, 'tm', route)  10 us
    unnamed x31, local copies, waits for them, and re-layouts  6.6 us
    dynamic_slice x2, local copies, waits for them, and re-layouts, row_of(): lax.dynamic_slice_in_dim(x, r, 1, axis=2)[:, :, 0]  2.83 us
    ppermute x22, waiting for transfers between devices, to_tile(): return lax.ppermute(block, 'tile', route)  2.32 us
  transfers between devices with their start and end apart: 30, of which 9 were waited for; matrix products, arithmetic and copies ran while one was open for 5% of the time, Pallas kernels for 13%

profile of v1, /device:TPU:0, one launch (start us, length us, event | category | flops | bytes accessed | tf_op | source)
XLA Modules:
  0.0 93.9 jit_solution(15522040168705923865)
XLA Ops:
  0.7 2.3 %constant_dynamic-slice_fusion = (bf16[2,128,1,512]{3,2,1,0:T(2,128)(2,1)S(1)}, bf16[2,128,1,512]{3,2,1,0:T(2,128)(2,1)S(1)}) fusion(bf16[2,128,2,512]{3,2,1,0:T(2,128)(2,1)} %param.7, s32[]{:T(128)S(6)} %select_n.22, s32[]{:T(128)S(6)} %select_n.21), kind=kLoop, calls=%fused_computation.14 | loop fusion | bytes 1048584 | tf_op jit(solution)/shard_map/dynamic_slice | solution.py:250
  8.4 2.2 %shard_map.85 = (bf16[144,512]{1,0:T(8,128)(2,1)S(1)}, bf16[144,512]{1,0:T(8,128)(2,1)S(1)}, bf16[2,2,192,512]{3,2,1,0:T(8,128)(2,1)S(1)}, bf16[64,512]{1,0:T(8,128)(2,1)S(1)}) custom-call(s32[3]{0:T(128)S(1)} %pad_add_fusion.pos.refs_0_, bf16[2,2,192,512]{3,2,1,0:T(8,128)(2,1)S(1)} %maximum_bitcast_fusion.u, ...), custom_call_target="tpu_custom_call" | custom-call | flops 1000000000 | bytes 4194304 | tf_op jit(solution)/shard_map/pallas_call | solution.py:27
  10.6 7.0 %collective-permute-start.13 = (bf16[144,512]{1,0:T(8,128)(2,1)S(1)}, bf16[144,512]{1,0:T(8,128)(2,1)S(1)}, u32[]{:S(2)}, u32[]{:S(2)}) collective-permute-start(bf16[144,512]{1,0:T(8,128)(2,1)S(1)} %get-tuple-element.23), channel_id=1, source_target_pairs={{0,1},{1,0},{2,3},{3,2},{4,5},{5,4},{6,7},{7,6},{8,9},{9,8},{10,11... | collective-permute-start | bytes 442376 | tf_op jit(solution)/shard_map/ppermute | solution.py:243
  17.7 1.4 %shard_map.86 = (f32[288,192]{1,0:T(8,128)S(1)}, f32[288,192]{1,0:T(8,128)S(1)}) custom-call(s32[3]{0:T(128)S(1)} %pad_add_fusion.pos.refs_0_, bf16[2,2,192,512]{3,2,1,0:T(8,128)(2,1)S(1)} %maximum_bitcast_fusion.u, bf16[2,192,512]{2,1,0:T(8,128)(2,1)S(1)} %collective-permute-done.rin, bf16[2,192,512]{2,1,0:T(8,128)(2,1)S(1)} %collective-permute-done.1.rout, ...), custom_call_target="tpu_custom_call" | custom-call | flops 1000000000 | bytes 4194304 | tf_op jit(solution)/shard_map/pallas_call | solution.py:27
  19.7 5.0 %collective-permute-start.15 = (bf16[2,144,512]{2,1,0:T(8,128)(2,1)S(1)}, bf16[2,144,512]{2,1,0:T(8,128)(2,1)S(1)}, u32[]{:S(2)}, u32[]{:S(2)}) collective-permute-start(bf16[2,144,512]{2,1,0:T(8,128)(2,1)S(1)} %pad_maximum_fusion.3.refs_1_), channel_id=1, source_target_pairs={{0,4},{5,1},{2,6},{7,3},{8,12},{13,9},{10,14},{15,11},{16,20},{21,... | collective-permute-start | bytes 884744 | tf_op jit(solution)/shard_map/ppermute | solution.py:243
  25.3 2.5 %collective-permute-start.5 = (f32[72,192]{1,0:T(8,128)S(1)}, f32[72,192]{1,0:T(8,128)S(1)}, u32[]{:S(2)}, u32[]{:S(2)}) collective-permute-start(f32[72,192]{1,0:T(8,128)S(1)} %get-tuple-element.22), channel_id=1, source_target_pairs={{0,24},{8,16},{16,8},{24,0},{1,25},{9,17},{17,9},{25,1},{2,26},{10... | collective-permute-start | bytes 165896 | tf_op jit(solution)/shard_map/ppermute | solution.py:246
  28.9 1.3 %collective-permute-start.22 = (bf16[2,144,512]{2,1,0:T(8,128)(2,1)S(1)}, bf16[2,144,512]{2,1,0:T(8,128)(2,1)S(1)}, u32[]{:S(2)}, u32[]{:S(2)}) collective-permute-start(bf16[2,144,512]{2,1,0:T(8,128)(2,1)S(1)} %pad_maximum_fusion.4), channel_id=1, source_target_pairs={{8,0},{16,8},{24,16},{9,1},{17,9},{25,17},{10,2},{18,10},{26,18},{... | collective-permute-start | bytes 884744 | tf_op jit(solution)/shard_map/ppermute | solution.py:246
  31.0 1.2 %collective-permute-done.4 = f32[72,192]{1,0:T(8,128)S(1)} collective-permute-done((f32[72,192]{1,0:T(8,128)S(1)}, f32[72,192]{1,0:T(8,128)S(1)}, u32[]{:S(2)}, u32[]{:S(2)}) %collective-permute-start.4) | collective-permute-done | bytes 55328 | tf_op jit(solution)/shard_map/ppermute | solution.py:246
  32.2 1.4 %collective-permute-done.3 = f32[72,192]{1,0:T(8,128)S(1)} collective-permute-done((f32[72,192]{1,0:T(8,128)S(1)}, f32[72,192]{1,0:T(8,128)S(1)}, u32[]{:S(2)}, u32[]{:S(2)}) %collective-permute-start.3) | collective-permute-done | bytes 55328 | tf_op jit(solution)/shard_map/ppermute | solution.py:246
  33.7 2.6 %collective-permute-start.7 = (f32[72,192]{1,0:T(8,128)S(1)}, f32[72,192]{1,0:T(8,128)S(1)}, u32[]{:S(2)}, u32[]{:S(2)}) collective-permute-start(f32[72,192]{1,0:T(8,128)S(1)} %add_add_fusion), channel_id=1, source_target_pairs={{0,4},{1,5},{2,6},{3,7},{4,0},{5,1},{6,2},{7,3},{8,12},{9,13},{10,... | collective-permute-start | bytes 165896 | tf_op jit(solution)/shard_map/ppermute | solution.py:243
  36.3 1.8 %collective-permute-start.6 = (f32[72,192]{1,0:T(8,128)S(1)}, f32[72,192]{1,0:T(8,128)S(1)}, u32[]{:S(2)}, u32[]{:S(2)}) collective-permute-start(f32[72,192]{1,0:T(8,128)S(1)} %add_add_fusion), channel_id=1, source_target_pairs={{0,2},{1,3},{2,0},{3,1},{4,6},{5,7},{6,4},{7,5},{8,10},{9,11},{10,... | collective-permute-start | bytes 165896 | tf_op jit(solution)/shard_map/ppermute | solution.py:243
  38.0 1.9 %collective-permute-done.8 = f32[72,192]{1,0:T(8,128)S(1)} collective-permute-done((f32[72,192]{1,0:T(8,128)S(1)}, f32[72,192]{1,0:T(8,128)S(1)}, u32[]{:S(2)}, u32[]{:S(2)}) %collective-permute-start.8) | collective-permute-done | bytes 55328 | tf_op jit(solution)/shard_map/ppermute | solution.py:243
  41.0 2.2 %collective-permute-start.14 = (bf16[2,144,512]{2,1,0:T(8,128)(2,1)S(1)}, bf16[2,144,512]{2,1,0:T(8,128)(2,1)S(1)}, u32[]{:S(2)}, u32[]{:S(2)}) collective-permute-start(bf16[2,144,512]{2,1,0:T(8,128)(2,1)S(1)} %pad_maximum_fusion.3.refs_1_), channel_id=1, source_target_pairs={{0,2},{3,1},{2,4},{5,3},{4,6},{7,5},{8,10},{11,9},{10,12},{13,11},... | collective-permute-start | bytes 884744 | tf_op jit(solution)/shard_map/ppermute | solution.py:243
  43.9 5.1 %collective-permute-start.24 = (bf16[2,144,512]{2,1,0:T(8,128)(2,1)S(1)}, bf16[2,144,512]{2,1,0:T(8,128)(2,1)S(1)}, u32[]{:S(2)}, u32[]{:S(2)}) collective-permute-start(bf16[2,144,512]{2,1,0:T(8,128)(2,1)S(1)} %collective-permute-done.22.refs_1_), channel_id=1, source_target_pairs={{0,4},{5,1},{2,6},{7,3},{8,12},{13,9},{10,14},{15,11},{16,20},{21,... | collective-permute-start | bytes 884744 | tf_op jit(solution)/shard_map/ppermute | solution.py:243
  49.0 1.7 %collective-permute-start.11 = (f32[72,192]{1,0:T(8,128)S(1)}, f32[72,192]{1,0:T(8,128)S(1)}, u32[]{:S(2)}, u32[]{:S(2)}) collective-permute-start(f32[72,192]{1,0:T(8,128)S(1)} %add_multiply_fusion), channel_id=1, source_target_pairs={{0,24},{8,16},{16,8},{24,0},{1,25},{9,17},{17,9},{25,1},{2,26},{10... | collective-permute-start | bytes 165896 | tf_op jit(solution)/shard_map/ppermute | solution.py:246
  52.4 2.1 %collective-permute-done.11 = f32[72,192]{1,0:T(8,128)S(1)} collective-permute-done((f32[72,192]{1,0:T(8,128)S(1)}, f32[72,192]{1,0:T(8,128)S(1)}, u32[]{:S(2)}, u32[]{:S(2)}) %collective-permute-start.11) | collective-permute-done | bytes 55328 | tf_op jit(solution)/shard_map/ppermute | solution.py:246
  56.3 2.6 %collective-permute-done.9 = f32[72,192]{1,0:T(8,128)} collective-permute-done((f32[72,192]{1,0:T(8,128)S(1)}, f32[72,192]{1,0:T(8,128)}, u32[]{:S(2)}, u32[]{:S(2)}) %collective-permute-start.9) | collective-permute-done | bytes 55328 | tf_op jit(solution)/shard_map/ppermute | solution.py:246
  58.9 1.3 %collective-permute-start.23 = (bf16[2,144,512]{2,1,0:T(8,128)(2,1)S(1)}, bf16[2,144,512]{2,1,0:T(8,128)(2,1)S(1)}, u32[]{:S(2)}, u32[]{:S(2)}) collective-permute-start(bf16[2,144,512]{2,1,0:T(8,128)(2,1)S(1)} %collective-permute-done.22.refs_1_), channel_id=1, source_target_pairs={{0,2},{3,1},{2,4},{5,3},{4,6},{7,5},{8,10},{11,9},{10,12},{13,11},... | collective-permute-start | bytes 884744 | tf_op jit(solution)/shard_map/ppermute | solution.py:243
  65.0 2.3 %collective-permute-start.28 = (bf16[2,144,512]{2,1,0:T(8,128)(2,1)S(1)}, bf16[2,144,512]{2,1,0:T(8,128)(2,1)S(1)}, u32[]{:S(2)}, u32[]{:S(2)}) collective-permute-start(bf16[2,144,512]{2,1,0:T(8,128)(2,1)S(1)} %collective-permute-done.25.refs_4_), channel_id=1, source_target_pairs={{0,1},{1,0},{2,3},{3,2},{4,5},{5,4},{6,7},{7,6},{8,9},{9,8},{10,11... | collective-permute-start | bytes 884744 | tf_op jit(solution)/shard_map/ppermute | solution.py:243
  68.2 9.0 %shard_map.89 = (f32[8,64,128]{2,1,0:T(8,128)S(1)}, bf16[8,64,128]{2,1,0:T(8,128)(2,1)S(1)}, bf16[2,2,64,512]{3,2,1,0:T(8,128)(2,1)S(1)}) custom-call(s32[3]{0:T(128)S(1)} %pad_add_fusion.pos.refs_0_, bf16[2,144,512]{2,1,0:T(8,128)(2,1)S(1)} %pad_maximum_fusion.3.refs_1_, bf16[2,144,512]{2,1,0:T(8,128)(2,1)S(1)} %collective-permute-done.14.refs_2_, ...), custom_call_target="tpu_custom_call" | custom-call | flops 3000000000 | bytes 8388608 | tf_op jit(solution)/shard_map/pallas_call | solution.py:27
  77.2 1.3 %collective-permute-start.29 = (bf16[8,64,128]{2,1,0:T(8,128)(2,1)S(1)}, bf16[8,64,128]{2,1,0:T(8,128)(2,1)S(1)}, u32[]{:S(2)}, u32[]{:S(2)}) collective-permute-start(bf16[8,64,128]{2,1,0:T(8,128)(2,1)S(1)} %get-tuple-element.28), channel_id=1, source_target_pairs={{8,0},{16,8},{24,16},{9,1},{17,9},{25,17},{10,2},{18,10},{26,18},{... | collective-permute-start | bytes 393224 | tf_op jit(solution)/shard_map/ppermute | solution.py:246
  78.5 1.4 %shard_map.88 = f32[576,192]{1,0:T(8,128)} custom-call(s32[3]{0:T(128)S(1)} %pad_add_fusion.pos.refs_0_, f32[4,72,192]{2,1,0:T(8,128)S(1)} %pad_maximum_fusion.2.mine, f32[4,72,192]{2,1,0:T(8,128)S(1)} %collective-permute-done.12.theirs), custom_call_target="tpu_custom_call" | custom-call | bytes 1048576 | tf_op jit(solution)/shard_map/pallas_call | solution.py:27
  80.9 3.7 %collective-permute-done.29.refs_9_ = bf16[8,64,128]{2,1,0:T(8,128)(2,1)S(1)} collective-permute-done((bf16[8,64,128]{2,1,0:T(8,128)(2,1)S(1)}, bf16[8,64,128]{2,1,0:T(8,128)(2,1)S(1)}, u32[]{:S(2)}, u32[]{:S(2)}) %collective-permute-start.29) | collective-permute-done | bytes 131104 | tf_op jit(solution)/shard_map/ppermute | solution.py:246
  84.5 8.4 %shard_map.90 = bf16[2,2,64,512]{3,2,1,0:T(8,128)(2,1)S(1)} custom-call(s32[3]{0:T(128)S(1)} %pad_add_fusion.pos.refs_0_, bf16[2,144,512]{2,1,0:T(8,128)(2,1)S(1)} %collective-permute-done.22.refs_1_, bf16[2,144,512]{2,1,0:T(8,128)(2,1)S(1)} %collective-permute-done.23.refs_2_, bf16[2,144,512]{2,1,0:T(8,128)(2,1)S(1)} %collective-permute-done.24.refs_3_, ...), custom_call_target="tpu_custom_call" | custom-call | flops 3000000000 | bytes 8388608 | tf_op jit(solution)/shard_map/pallas_call | solution.py:27
  (90 shorter events, 21.2 us)
Async XLA Ops:
  10.6 9.0 %collective-permute-start.13 = (bf16[144,512]{1,0:T(8,128)(2,1)S(1)}, bf16[144,512]{1,0:T(8,128)(2,1)S(1)}, u32[]{:S(2)}, u32[]{:S(2)}) collective-permute-start(bf16[144,512]{1,0:T(8,128)(2,1)S(1)} %get-tuple-element.23), channel_id=1, source_target_pairs={{0,1},{1,0},{2,3},{3,2},{4,5},{5,4},{6,7},{7,6},{8,9},{9,8},{10,11... | collective-permute-start | bytes 442376 | tf_op jit(solution)/shard_map/ppermute | solution.py:243
  19.1 5.7 %collective-permute-start.2 = (f32[288,192]{1,0:T(8,128)S(1)}, f32[288,192]{1,0:T(8,128)S(1)}, u32[]{:S(2)}, u32[]{:S(2)}) collective-permute-start(f32[288,192]{1,0:T(8,128)S(1)} %get-tuple-element.18), channel_id=1, source_target_pairs={{0,1},{1,0},{2,3},{3,2},{4,5},{5,4},{6,7},{7,6},{8,9},{9,8},{10,11... | collective-permute-start | bytes 663560 | tf_op jit(solution)/shard_map/ppermute | solution.py:243
  19.2 9.7 %collective-permute-start.20 = (bf16[144,512]{1,0:T(8,128)(2,1)S(1)}, bf16[144,512]{1,0:T(8,128)(2,1)S(1)}, u32[]{:S(2)}, u32[]{:S(2)}) collective-permute-start(bf16[144,512]{1,0:T(8,128)(2,1)S(1)} %get-tuple-element.24.refs_8_), channel_id=1, source_target_pairs={{0,1},{1,0},{2,3},{3,2},{4,5},{5,4},{6,7},{7,6},{8,9},{9,8},{10,11... | collective-permute-start | bytes 442376 | tf_op jit(solution)/shard_map/ppermute | solution.py:243
  19.7 23.5 %collective-permute-start.15 = (bf16[2,144,512]{2,1,0:T(8,128)(2,1)S(1)}, bf16[2,144,512]{2,1,0:T(8,128)(2,1)S(1)}, u32[]{:S(2)}, u32[]{:S(2)}) collective-permute-start(bf16[2,144,512]{2,1,0:T(8,128)(2,1)S(1)} %pad_maximum_fusion.3.refs_1_), channel_id=1, source_target_pairs={{0,4},{5,1},{2,6},{7,3},{8,12},{13,9},{10,14},{15,11},{16,20},{21,... | collective-permute-start | bytes 884744 | tf_op jit(solution)/shard_map/ppermute | solution.py:243
  25.3 5.7 %collective-permute-start.5 = (f32[72,192]{1,0:T(8,128)S(1)}, f32[72,192]{1,0:T(8,128)S(1)}, u32[]{:S(2)}, u32[]{:S(2)}) collective-permute-start(f32[72,192]{1,0:T(8,128)S(1)} %get-tuple-element.22), channel_id=1, source_target_pairs={{0,24},{8,16},{16,8},{24,0},{1,25},{9,17},{17,9},{25,1},{2,26},{10... | collective-permute-start | bytes 165896 | tf_op jit(solution)/shard_map/ppermute | solution.py:246
  28.4 5.2 %collective-permute-start.3 = (f32[72,192]{1,0:T(8,128)S(1)}, f32[72,192]{1,0:T(8,128)S(1)}, u32[]{:S(2)}, u32[]{:S(2)}) collective-permute-start(f32[72,192]{1,0:T(8,128)S(1)} %get-tuple-element.20), channel_id=1, source_target_pairs={{0,8},{8,0},{16,24},{24,16},{1,9},{9,1},{17,25},{25,17},{2,10},{10... | collective-permute-start | bytes 165896 | tf_op jit(solution)/shard_map/ppermute | solution.py:246
  28.9 14.9 %collective-permute-start.22 = (bf16[2,144,512]{2,1,0:T(8,128)(2,1)S(1)}, bf16[2,144,512]{2,1,0:T(8,128)(2,1)S(1)}, u32[]{:S(2)}, u32[]{:S(2)}) collective-permute-start(bf16[2,144,512]{2,1,0:T(8,128)(2,1)S(1)} %pad_maximum_fusion.4), channel_id=1, source_target_pairs={{8,0},{16,8},{24,16},{9,1},{17,9},{25,17},{10,2},{18,10},{26,18},{... | collective-permute-start | bytes 884744 | tf_op jit(solution)/shard_map/ppermute | solution.py:246
  33.6 6.3 %collective-permute-start.8 = (f32[72,192]{1,0:T(8,128)S(1)}, f32[72,192]{1,0:T(8,128)S(1)}, u32[]{:S(2)}, u32[]{:S(2)}) collective-permute-start(f32[72,192]{1,0:T(8,128)S(1)} %add_add_fusion), channel_id=1, source_target_pairs={{0,6},{1,7},{2,4},{3,5},{4,2},{5,3},{6,0},{7,1},{8,14},{9,15},{10,... | collective-permute-start | bytes 165896 | tf_op jit(solution)/shard_map/ppermute | solution.py:243
  33.7 7.3 %collective-permute-start.7 = (f32[72,192]{1,0:T(8,128)S(1)}, f32[72,192]{1,0:T(8,128)S(1)}, u32[]{:S(2)}, u32[]{:S(2)}) collective-permute-start(f32[72,192]{1,0:T(8,128)S(1)} %add_add_fusion), channel_id=1, source_target_pairs={{0,4},{1,5},{2,6},{3,7},{4,0},{5,1},{6,2},{7,3},{8,12},{9,13},{10,... | collective-permute-start | bytes 165896 | tf_op jit(solution)/shard_map/ppermute | solution.py:243
  36.3 12.7 %collective-permute-start.6 = (f32[72,192]{1,0:T(8,128)S(1)}, f32[72,192]{1,0:T(8,128)S(1)}, u32[]{:S(2)}, u32[]{:S(2)}) collective-permute-start(f32[72,192]{1,0:T(8,128)S(1)} %add_add_fusion), channel_id=1, source_target_pairs={{0,2},{1,3},{2,0},{3,1},{4,6},{5,7},{6,4},{7,5},{8,10},{9,11},{10,... | collective-permute-start | bytes 165896 | tf_op jit(solution)/shard_map/ppermute | solution.py:243
  39.9 10.8 %collective-permute-start.21 = (bf16[64,512]{1,0:T(8,128)(2,1)S(1)}, bf16[64,512]{1,0:T(8,128)(2,1)S(1)}, u32[]{:S(2)}, u32[]{:S(2)}) collective-permute-start(bf16[64,512]{1,0:T(8,128)(2,1)S(1)} %get-tuple-element.25), channel_id=1, source_target_pairs={{1,2},{3,4},{5,6},{2,1},{4,3},{6,5},{9,10},{11,12},{13,14},{10,9},... | collective-permute-start | bytes 196616 | tf_op jit(solution)/shard_map/ppermute | solution.py:243
  41.0 14.6 %collective-permute-start.14 = (bf16[2,144,512]{2,1,0:T(8,128)(2,1)S(1)}, bf16[2,144,512]{2,1,0:T(8,128)(2,1)S(1)}, u32[]{:S(2)}, u32[]{:S(2)}) collective-permute-start(bf16[2,144,512]{2,1,0:T(8,128)(2,1)S(1)} %pad_maximum_fusion.3.refs_1_), channel_id=1, source_target_pairs={{0,2},{3,1},{2,4},{5,3},{4,6},{7,5},{8,10},{11,9},{10,12},{13,11},... | collective-permute-start | bytes 884744 | tf_op jit(solution)/shard_map/ppermute | solution.py:243
  43.2 17.8 %collective-permute-start.16 = (bf16[2,144,512]{2,1,0:T(8,128)(2,1)S(1)}, bf16[2,144,512]{2,1,0:T(8,128)(2,1)S(1)}, u32[]{:S(2)}, u32[]{:S(2)}) collective-permute-start(bf16[2,144,512]{2,1,0:T(8,128)(2,1)S(1)} %collective-permute-done.15.refs_3_), channel_id=1, source_target_pairs={{3,1},{4,6},{11,9},{12,14},{19,17},{20,22},{27,25},{28,30}} | collective-permute-start | bytes 884744 | tf_op jit(solution)/shard_map/ppermute | solution.py:243
  43.9 16.4 %collective-permute-start.24 = (bf16[2,144,512]{2,1,0:T(8,128)(2,1)S(1)}, bf16[2,144,512]{2,1,0:T(8,128)(2,1)S(1)}, u32[]{:S(2)}, u32[]{:S(2)}) collective-permute-start(bf16[2,144,512]{2,1,0:T(8,128)(2,1)S(1)} %collective-permute-done.22.refs_1_), channel_id=1, source_target_pairs={{0,4},{5,1},{2,6},{7,3},{8,12},{13,9},{10,14},{15,11},{16,20},{21,... | collective-permute-start | bytes 884744 | tf_op jit(solution)/shard_map/ppermute | solution.py:243
  49.0 5.5 %collective-permute-start.11 = (f32[72,192]{1,0:T(8,128)S(1)}, f32[72,192]{1,0:T(8,128)S(1)}, u32[]{:S(2)}, u32[]{:S(2)}) collective-permute-start(f32[72,192]{1,0:T(8,128)S(1)} %add_multiply_fusion), channel_id=1, source_target_pairs={{0,24},{8,16},{16,8},{24,0},{1,25},{9,17},{17,9},{25,1},{2,26},{10... | collective-permute-start | bytes 165896 | tf_op jit(solution)/shard_map/ppermute | solution.py:246
  55.6 8.4 %collective-permute-start.17 = (bf16[2,144,512]{2,1,0:T(8,128)(2,1)S(1)}, bf16[2,144,512]{2,1,0:T(8,128)(2,1)S(1)}, u32[]{:S(2)}, u32[]{:S(2)}) collective-permute-start(bf16[2,144,512]{2,1,0:T(8,128)(2,1)S(1)} %collective-permute-done.14.refs_2_), channel_id=1, source_target_pairs={{0,1},{1,0},{2,3},{3,2},{4,5},{5,4},{6,7},{7,6},{8,9},{9,8},{10,11... | collective-permute-start | bytes 884744 | tf_op jit(solution)/shard_map/ppermute | solution.py:243
  55.7 8.8 %collective-permute-start.18 = (bf16[2,144,512]{2,1,0:T(8,128)(2,1)S(1)}, bf16[2,144,512]{2,1,0:T(8,128)(2,1)S(1)}, u32[]{:S(2)}, u32[]{:S(2)}) collective-permute-start(bf16[2,144,512]{2,1,0:T(8,128)(2,1)S(1)} %collective-permute-done.15.refs_3_), channel_id=1, source_target_pairs={{0,1},{1,0},{2,3},{3,2},{4,5},{5,4},{6,7},{7,6},{8,9},{9,8},{10,11... | collective-permute-start | bytes 884744 | tf_op jit(solution)/shard_map/ppermute | solution.py:243
  58.9 5.7 %collective-permute-start.23 = (bf16[2,144,512]{2,1,0:T(8,128)(2,1)S(1)}, bf16[2,144,512]{2,1,0:T(8,128)(2,1)S(1)}, u32[]{:S(2)}, u32[]{:S(2)}) collective-permute-start(bf16[2,144,512]{2,1,0:T(8,128)(2,1)S(1)} %collective-permute-done.22.refs_1_), channel_id=1, source_target_pairs={{0,2},{3,1},{2,4},{5,3},{4,6},{7,5},{8,10},{11,9},{10,12},{13,11},... | collective-permute-start | bytes 884744 | tf_op jit(solution)/shard_map/ppermute | solution.py:243
  61.0 6.4 %collective-permute-start.19 = (bf16[2,144,512]{2,1,0:T(8,128)(2,1)S(1)}, bf16[2,144,512]{2,1,0:T(8,128)(2,1)}, u32[]{:S(2)}, u32[]{:S(2)}) collective-permute-start(bf16[2,144,512]{2,1,0:T(8,128)(2,1)S(1)} %collective-permute-done.16.refs_4_), channel_id=1, source_target_pairs={{0,1},{1,0},{2,3},{3,2},{4,5},{5,4},{6,7},{7,6},{8,9},{9,8},{10,11... | collective-permute-start | bytes 884744 | tf_op jit(solution)/shard_map/ppermute | solution.py:243
  64.0 14.5 %collective-permute-start.12 = (f32[4,72,192]{2,1,0:T(8,128)S(1)}, f32[4,72,192]{2,1,0:T(8,128)S(1)}, u32[]{:S(2)}, u32[]{:S(2)}) collective-permute-start(f32[4,72,192]{2,1,0:T(8,128)S(1)} %pad_maximum_fusion.2.mine), channel_id=1, source_target_pairs={{0,1},{1,0},{2,3},{3,2},{4,5},{5,4},{6,7},{7,6},{8,9},{9,8},{10,11... | collective-permute-start | bytes 663560 | tf_op jit(solution)/shard_map/ppermute | solution.py:243
  64.5 16.4 %collective-permute-start.27 = (bf16[2,144,512]{2,1,0:T(8,128)(2,1)S(1)}, bf16[2,144,512]{2,1,0:T(8,128)(2,1)S(1)}, u32[]{:S(2)}, u32[]{:S(2)}) collective-permute-start(bf16[2,144,512]{2,1,0:T(8,128)(2,1)S(1)} %collective-permute-done.24.refs_3_), channel_id=1, source_target_pairs={{0,1},{1,0},{2,3},{3,2},{4,5},{5,4},{6,7},{7,6},{8,9},{9,8},{10,11... | collective-permute-start | bytes 884744 | tf_op jit(solution)/shard_map/ppermute | solution.py:243
  64.6 16.3 %collective-permute-start.26 = (bf16[2,144,512]{2,1,0:T(8,128)(2,1)S(1)}, bf16[2,144,512]{2,1,0:T(8,128)(2,1)S(1)}, u32[]{:S(2)}, u32[]{:S(2)}) collective-permute-start(bf16[2,144,512]{2,1,0:T(8,128)(2,1)S(1)} %collective-permute-done.23.refs_2_), channel_id=1, source_target_pairs={{0,1},{1,0},{2,3},{3,2},{4,5},{5,4},{6,7},{7,6},{8,9},{9,8},{10,11... | collective-permute-start | bytes 884744 | tf_op jit(solution)/shard_map/ppermute | solution.py:243
  65.0 19.5 %collective-permute-start.28 = (bf16[2,144,512]{2,1,0:T(8,128)(2,1)S(1)}, bf16[2,144,512]{2,1,0:T(8,128)(2,1)S(1)}, u32[]{:S(2)}, u32[]{:S(2)}) collective-permute-start(bf16[2,144,512]{2,1,0:T(8,128)(2,1)S(1)} %collective-permute-done.25.refs_4_), channel_id=1, source_target_pairs={{0,1},{1,0},{2,3},{3,2},{4,5},{5,4},{6,7},{7,6},{8,9},{9,8},{10,11... | collective-permute-start | bytes 884744 | tf_op jit(solution)/shard_map/ppermute | solution.py:243
  77.2 7.3 %collective-permute-start.29 = (bf16[8,64,128]{2,1,0:T(8,128)(2,1)S(1)}, bf16[8,64,128]{2,1,0:T(8,128)(2,1)S(1)}, u32[]{:S(2)}, u32[]{:S(2)}) collective-permute-start(bf16[8,64,128]{2,1,0:T(8,128)(2,1)S(1)} %get-tuple-element.28), channel_id=1, source_target_pairs={{8,0},{16,8},{24,16},{9,1},{17,9},{25,17},{10,2},{18,10},{26,18},{... | collective-permute-start | bytes 393224 | tf_op jit(solution)/shard_map/ppermute | solution.py:246
  (17 other events, 44.7 us)

commit v2 on v0

--- a/solution.py
+++ b/solution.py
@@ -3,7 +3,381 @@
 import jax
 import jax.numpy as jnp
 from jax import lax
+from jax.experimental import pallas as pl
+from jax.experimental.pallas import tpu as pltpu
 from jax.sharding import PartitionSpec as P
+
+F32 = jnp.float32
+BF16 = jnp.bfloat16
+
+
+def act_slope(preact):
+    return 0.1 + 0.9 * jax.nn.sigmoid(preact)
+
+
+TABLE_ROWS = 16
+LANES = 128
+
+
+def full(memory_space=pltpu.VMEM):
+    return pl.BlockSpec(memory_space=memory_space)
+
+
+def call(kernel, out_shapes, args, scalars, scratch=(), micros=1.0):
+    specs = [full(pltpu.SMEM)] * scalars + [full()] * (len(args) - scalars)
+    return pl.pallas_call(
+        kernel,
+        out_shape=out_shapes,
+        in_specs=specs,
+        out_specs=[full()] * len(out_shapes),
+        scratch_shapes=list(scratch),
+        cost_estimate=pl.CostEstimate(flops=int(micros * 1000000000.0), bytes_accessed=0, transcendentals=0),
+        compiler_params=pltpu.CompilerParams(vmem_limit_bytes=24 << 20),
+    )(*args)
+
+
+def after(value, *others):
+    return lax.optimization_barrier((value, *others))[0]
+
+
+def from_left(values):
+    lane = lax.broadcasted_iota(jnp.int32, values.shape, 1)
+    return jnp.where(lane == 0, 0.0, pltpu.roll(values, 1, 1))
+
+
+def from_right(values):
+    columns = values.shape[1]
+    lane = lax.broadcasted_iota(jnp.int32, values.shape, 1)
+    return jnp.where(lane == columns - 1, 0.0, pltpu.roll(values, columns - 1, 1))
+
+
+def taps_of(row):
+    wide = row.astype(F32)
+    return (from_right(wide).astype(BF16), row, from_left(wide).astype(BF16))
+
+
+def forward_kernel(pos, u, rin, rout, cot, w3, tab, msg, g3, halo):
+    core = pos[0]
+    frames, _, ch, columns = cot.shape
+    pieces = columns // LANES
+    halo[core] = rout[...]
+    halo[1 - core] = rin[...]
+    for f in range(frames):
+        rows = (halo.at[0, f], u.at[f, 0], u.at[f, 1], halo.at[1, f])
+        for r in range(2):
+            taps = jnp.dot(w3[0], rows[r][...], preferred_element_type=F32)
+            taps += jnp.dot(w3[1], rows[r + 1][...], preferred_element_type=F32)
+            taps += jnp.dot(w3[2], rows[r + 2][...], preferred_element_type=F32)
+            z = taps[ch : 2 * ch] + from_left(taps[:ch]) + from_right(taps[2 * ch :])
+            g = (cot[f, r].astype(F32) * act_slope(z)).astype(BF16)
+            for j in range(pieces):
+                at = ((2 * f + r) * pieces + j) * ch
+                msg[at : at + ch] = g[:, LANES * j : LANES * (j + 1)]
+            for k, part in enumerate(taps_of(g)):
+                g3[f, r, k * ch : (k + 1) * ch] = part
+    msg[2 * frames * pieces * ch :] = tab[...]
+
+
+def taps_kernel(pos, u, rin, rout, g3, w3, keep, send, wa, wf, halo, total):
+    core = pos[0]
+    size = g3.shape[2]
+    half = keep.shape[0]
+    halo[core] = rout[...]
+    halo[1 - core] = rin[...]
+    for ky in range(3):
+        acc = jnp.zeros((size, u.shape[2]), F32)
+        for f in range(u.shape[0]):
+            rows = (halo.at[0, f], u.at[f, 0], u.at[f, 1], halo.at[1, f])
+            for r in range(2):
+                acc += lax.dot_general(
+                    g3[f, r], rows[r + ky][...], (((1,), (1,)), ((), ())), preferred_element_type=F32
+                )
+        total[ky * size : (ky + 1) * size] = acc
+    keep[...] = total[pl.ds(pl.multiple_of(core * half, 8), half)]
+    send[...] = total[pl.ds(pl.multiple_of((1 - core) * half, 8), half)]
+    ch = size // 3
+    for kx in range(3):
+        rows = [w3[ky, kx * ch : (kx + 1) * ch] for ky in (2, 1, 0)]
+        turned = jnp.transpose(jnp.concatenate(rows, axis=0).astype(F32)).astype(BF16)
+        wf[kx * ch : (kx + 1) * ch] = turned[:ch]
+        wa[2 * kx * ch : 2 * (kx + 1) * ch] = turned[ch:]
+
+
+def shares_kernel(pos, keep, got, own, *others):
+    group = pos[2]
+    part = own.shape[0]
+    for k, out in enumerate((own, *others)):
+        at = pl.ds(pl.multiple_of((group ^ k) * part, 8), part)
+        out[...] = keep[at] + got[at]
+
+
+def assemble_kernel(pos, mine, theirs, out):
+    core, group = pos[0], pos[2]
+    part = mine.shape[1]
+    parts = mine.shape[0]
+    for source, side in ((mine, core), (theirs, 1 - core)):
+        for k in range(parts):
+            at = (side * parts + (group ^ k)) * part
+            out[pl.ds(pl.multiple_of(at, 8), part)] = source[k]
+
+
+def collect(pos, entries, chips, g, tabs):
+    core = pos[0]
+    frames, _, ch, columns = g.shape
+    pieces = columns // LANES
+    for ref, where, first in entries:
+
+        @pl.when((where >= 0) & (where < chips))
+        def _(ref=ref, where=where, first=first):
+            for h in range(2):
+                band = 2 * where + (first if h == 0 else 1 - first)
+                for f in range(frames):
+                    for r in range(2):
+                        for j in range(pieces):
+                            at = ((2 * f + r) * pieces + j) * ch
+                            lanes = slice(LANES * j, LANES * (j + 1))
+                            g[f, 2 * band + r + 1, :, lanes] = ref[h, at : at + ch]
+                codes = ref[h, 2 * frames * pieces * ch :].astype(F32).astype(jnp.int32)
+                tabs[pl.ds(band, 1)] = codes[:1]
+
+
+def convolved(weights, window):
+    taps = jnp.dot(weights[...], window, preferred_element_type=F32)
+    size = taps.shape[0] // 3
+    total = taps[size : 2 * size] + from_right(taps[:size]) + from_left(taps[2 * size :])
+    return total.astype(BF16)
+
+
+def spread(low, high, me, g, weights, codes, hits, gu, sums):
+    frames, _, ch, columns = g.shape
+    pieces = columns // LANES
+
+    def one_row(r, count):
+        for f in range(frames):
+            value = convolved(weights, g[f, pl.ds(r, 3)].reshape(3 * ch, columns))
+            for j in range(pieces):
+                for q in range(2):
+                    gu[f, r, j, q] = value[q * ch : (q + 1) * ch, LANES * j : LANES * (j + 1)]
+            for k in range(2 * pieces):
+                lane = (2 * f + r % 2) * (2 * pieces) + k
+                hits[count] = (r // 2) * LANES + lane
+                count += (lax.shift_right_logical(codes[r // 2, lane], 3) == me).astype(jnp.int32)
+        return count
+
+    count = lax.fori_loop(low, high, one_row, 0)
+
+    def one_hit(k, _):
+        hit = hits[k]
+        band, lane = hit // LANES, hit % LANES
+        f, block, q = lane // (4 * pieces), (lane % (4 * pieces)) // 2, lane % 2
+        target = codes[band, lane] % 8
+        sums[f + 1 - q, target] += gu[f, 2 * band + block // pieces, block % pieces, q].astype(F32)
+        return 0
+
+    lax.fori_loop(0, count, one_hit, 0)
+
+
+def ready_rows(chip, reach, chips):
+    low, high = jnp.maximum(chip - reach, 0), jnp.minimum(chip + reach, chips - 1)
+    return 4 * low + (low > 0).astype(jnp.int32), 4 * high + 4 - (high < chips - 1).astype(jnp.int32)
+
+
+def stage_kernel(reach, chips, pos, *refs):
+    core, chip = pos[0], pos[1]
+    me = 2 * chip + core
+    step = 1 - 2 * core
+    if reach == 1:
+        own, near, far, wa, wf, sums, feat, g, tabs, codes, hits, gu, sem = refs
+        entries = [(own, chip, core)]
+        sums[...] = jnp.zeros(sums.shape, F32)
+    else:
+        near0, far0, near, far, wa, sums_in, sums, g, tabs, codes, hits, gu, sem = refs
+        entries = [(near0, chip - step * (reach - 1), core), (far0, chip + step * (reach - 1), 1 - core)]
+        sums[...] = sums_in[...]
+    entries += [(near, chip - step * reach, core), (far, chip + step * reach, 1 - core)]
+    frames, rows, ch, columns = g.shape
+    zero = jnp.zeros((ch, columns), BF16)
+    for f in range(frames):
+        g[f, 0] = zero
+        g[f, rows - 1] = zero
+    collect(pos, entries, chips, g, tabs)
+    copy = pltpu.make_async_copy(tabs, codes, sem)
+    copy.start()
+    if reach == 1:
+        for f in range(frames):
+            for r in range(2):
+                feat[f, r] = convolved(wf, g[f, pl.ds(2 * me + r, 3)].reshape(3 * ch, columns))
+    copy.wait()
+    low, high = ready_rows(chip, reach, chips)
+    if reach == 1:
+        spread(low, high, me, g, wa, codes, hits, gu, sums)
+    else:
+        old_low, old_high = ready_rows(chip, reach - 1, chips)
+        spread(low, old_low, me, g, wa, codes, hits, gu, sums)
+        spread(old_high, high, me, g, wa, codes, hits, gu, sums)
+
+
+def final_stage_kernel(reach, chips, pos, near0, far0, near, far, wa, sums_in, passed, local, sums, *work):
+    stage_kernel(reach, chips, pos, near0, far0, near, far, wa, sums_in, sums, *work)
+    for s in range(2):
+        passed[s] = sums[s].astype(BF16)
+    local[...] = sums[2]
+
+
+def last_kernel(passed, local, prop):
+    ch = local.shape[1]
+    pieces = prop.shape[3] // LANES
+    for s in range(2):
+        for b in range(2 * pieces):
+            j = b % pieces
+            value = passed[s, b]
+            if s == 0:
+                value = (value.astype(F32) + local[b]).astype(BF16)
+            prop[s, b // pieces, :, LANES * j : LANES * (j + 1)] = value
+
+
+def total_over(parts):
+    first = parts[0]
+    for part in parts[1:]:
+        first = first + part
+    return first
+
+
+def few_bands(features, aligned, cotangent, weight, src_tile, src_blk):
+    frames, channels, height, columns = features.shape
+    inner = channels + aligned.shape[1]
+    tiles = lax.axis_size("tile")
+    groups = lax.axis_size("tm")
+    chips = tiles // 2
+    tile = lax.axis_index("tile")
+    group = lax.axis_index("tm")
+    core = tile % 2
+    pos = jnp.stack([core, tile // 2, group]).astype(jnp.int32)
+
+    cores = [(i, i ^ 1) for i in range(tiles)]
+    joints = [(2 * z + 1, 2 * z + 2) for z in range(chips - 1)]
+    joints += [(b, a) for a, b in joints]
+
+    def hop(k):
+        route = []
+        for z in range(k, chips - 1):
+            route += [(2 * z, 2 * z + 2), (2 * (chips - 1 - z) + 1, 2 * (chips - 1 - z) - 1)]
+        return route
+
+    def to_tile(block, route):
+        return lax.ppermute(block, "tile", route)
+
+    def to_group(block, route):
+        return lax.ppermute(block, "tm", route)
+
+    pieces = columns // LANES
+    u = jnp.transpose(jnp.concatenate((features, aligned), axis=1), (0, 2, 1, 3))
+    u = after(u)
+    rout = to_tile(lax.dynamic_index_in_dim(u, core, 1, keepdims=False), joints)
+    rin = to_tile(lax.dynamic_index_in_dim(u, 1 - core, 1, keepdims=False), cores)
+    cot = jnp.transpose(cotangent, (0, 2, 1, 3))
+    w3 = weight.reshape(3, 3 * channels, inner)
+    codes = (src_tile * 8 + src_blk).reshape(1, -1).astype(BF16)
+    tab = jnp.pad(codes, ((0, TABLE_ROWS - 1), (0, LANES - codes.shape[1])))
+
+    halo = pltpu.VMEM((2, frames, inner, columns), BF16)
+    msg_rows = 2 * frames * pieces * channels + TABLE_ROWS
+    msg, g3 = call(
+        forward_kernel,
+        [
+            jax.ShapeDtypeStruct((msg_rows, LANES), BF16),
+            jax.ShapeDtypeStruct((frames, 2, 3 * channels, columns), BF16),
+        ],
+        (pos, u, rin, rout, cot, w3, tab),
+        1,
+        [halo],
+    )
+
+    half_shapes = [jax.ShapeDtypeStruct((9 * channels // n, inner), F32) for n in (2, 4, 8)]
+    weight_shapes = [
+        jax.ShapeDtypeStruct((3 * n, 3 * channels), BF16) for n in (inner - channels, channels)
+    ]
+    swaps = [[(i, i ^ k) for i in range(groups)] for k in range(groups)]
+    turns = [[(2 * z + c, 2 * (z ^ k) + c) for z in range(chips) for c in range(2)] for k in range(chips)]
+    bands = 2 * chips
+    sums_shape = (3, 2 * pieces, channels, LANES)
+    work = [
+        pltpu.VMEM((frames, 2 * bands + 2, channels, columns), BF16),
+        pltpu.VMEM((bands, LANES), jnp.int32),
+        pltpu.SMEM((bands, LANES), jnp.int32),
+        pltpu.SMEM((4 * pieces * bands + 1,), jnp.int32),
+        pltpu.VMEM((frames, 2 * bands, pieces, 2, channels, LANES), BF16),
+        pltpu.SemaphoreType.DMA,
+    ]
+
+    other = to_tile(msg, cores)
+    own = jnp.stack((msg, other))
+    near1 = to_tile(own, hop(0))
+    keep, send, wa, wf = call(
+        taps_kernel,
+        [half_shapes[0], half_shapes[0], *weight_shapes],
+        (pos, u, rin, rout, after(g3, own), w3),
+        1,
+        [halo, pltpu.VMEM((9 * channels, inner), F32)],
+    )
+    got = to_tile(send, cores)
+    part_rows = 9 * channels // (2 * groups)
+    part_shape = jax.ShapeDtypeStruct((part_rows, inner), F32)
+    shares = call(shares_kernel, [part_shape] * groups, (pos, keep, got), 1, micros=0.6)
+    share = total_over([shares[0]] + [to_group(shares[k], swaps[k]) for k in range(1, groups)])
+    near2 = to_tile(near1, hop(1))
+    far1 = to_tile(near1, cores)
+    share = after(share, far1)
+    sums, feat = call(
+        lambda *refs: stage_kernel(1, chips, *refs),
+        [
+            jax.ShapeDtypeStruct(sums_shape, F32),
+            jax.ShapeDtypeStruct((frames, 2, channels, columns), BF16),
+        ],
+        (pos, own, near1, far1, wa, wf),
+        1,
+        work,
+        micros=6.0,
+    )
+    share = total_over([share] + [to_tile(share, turns[k]) for k in range(1, chips)])
+    pixels = frames * groups * height * tiles * columns
+    share = share * (1.0 / math.sqrt(pixels))
+    near3 = to_tile(near2, hop(2))
+    far2 = to_tile(near2, cores)
+    (sums,) = call(
+        lambda *refs: stage_kernel(2, chips, *refs),
+        [jax.ShapeDtypeStruct(sums_shape, F32)],
+        (pos, near1, far1, near2, far2, wa, sums),
+        1,
+        work,
+        micros=4.0,
+    )
+    share = after(share, far2)
+    mine = jnp.stack([share] + [to_group(share, swaps[k]) for k in range(1, groups)])
+    near3 = after(near3, mine, sums)
+    far3 = to_tile(near3, cores)
+    passed, local = call(
+        lambda *refs: final_stage_kernel(3, chips, *refs),
+        [jax.ShapeDtypeStruct((2, *sums_shape[1:]), BF16), jax.ShapeDtypeStruct(sums_shape[1:], F32)],
+        (pos, near2, far2, near3, far3, wa, sums),
+        1,
+        [pltpu.VMEM(sums_shape, F32)] + work,
+        micros=4.0,
+    )
+    passed = to_group(passed, [(m + 1, m) for m in range(groups - 1)])
+    theirs = to_tile(mine, cores)
+    (grad_weight,) = call(
+        assemble_kernel, [jax.ShapeDtypeStruct((9 * channels, inner), F32)], (pos, mine, theirs), 1
+    )
+
+    (prop,) = call(
+        last_kernel, [jax.ShapeDtypeStruct((2, 2, channels, columns), BF16)], (passed, local), 0
+    )
+    return (
+        grad_weight.reshape(9, channels, inner),
+        jnp.transpose(feat, (0, 2, 1, 3)),
+        jnp.transpose(prop, (0, 2, 1, 3)),
+    )
 
 
 def with_halo(cells, sides, width):
@@ -31,10 +405,6 @@
 
 def pad_columns(values):
     return jnp.pad(values, ((0, 0), (0, 0), (0, 0), (1, 1)))
-
-
-def act_slope(preact):
-    return 0.1 + 0.9 * jax.nn.sigmoid(preact)
 
 
 def conv_forward(weight, padded_input, height):
@@ -127,7 +497,7 @@
     )
 
 
-def body(features, aligned, cotangent, weight, src_tile, src_blk):
+def many_bands(features, aligned, cotangent, weight, src_tile, src_blk):
     frames, channels, height, columns = features.shape
     inputs = jnp.concatenate((features, aligned), axis=1)
     padded_in = pad_columns(with_halo(inputs, (("tile", 2),), 1))
@@ -165,4 +535,6 @@
         P("tm", "tile", None),
     )
     out_specs = (P(), P("tm", None, "tile", None), P("tm", None, "tile", None))
+    few = mesh.shape["tile"] == 8 and mesh.shape["tm"] == 4
+    body = few_bands if few else many_bands
     return jax.shard_map(body, mesh=mesh, in_specs=in_specs, out_specs=out_specs, check_vma=False)

time: 230 us -> 76.8 us (0.33)
  the two profiles are of different devices: /device:TPU:0 before, /device:TPU:16 now
where the time goes in v2:
time: 76.8 us; the launch traced here: 76.5 us
  waiting for transfers between devices  26.5 us (35%)
  starting transfers between devices  25.2 us (33%)
  Pallas kernels  20.1 us (26%)
  local copies, waits for them, and re-layouts  3.43 us (4%)
  between operations  1.03 us (1%)
    pallas_call x8, Pallas kernels, call(): pl.pallas_call(kernel, out_shape=out_shapes, in_specs=specs, out_specs=[f...  20.1 us
    ppermute x14, starting transfers between devices, to_tile(): return lax.ppermute(block, 'tile', route)  16.8 us
    ppermute x14, waiting for transfers between devices, to_tile(): return lax.ppermute(block, 'tile', route)  15.1 us
    ppermute x7, waiting for transfers between devices, to_group(): return lax.ppermute(block, 'tm', route)  11.4 us
    ppermute x7, starting transfers between devices, to_group(): return lax.ppermute(block, 'tm', route)  8.4 us
    unnamed x15, local copies, waits for them, and re-layouts  3.17 us
  transfers between devices with their start and end apart: 21, of which 8 were waited for; matrix products, arithmetic and copies ran while one was open for 2% of the time, Pallas kernels for 24%

profile of v2, /device:TPU:16, one launch (start us, length us, event | category | flops | bytes accessed | tf_op | source)
XLA Modules:
  0.0 76.5 jit_solution(7528886117079800258)
XLA Ops:
  0.7 1.1 %copy.16 = bf16[2,128,2,512]{3,1,2,0:T(8,128)(2,1)S(1)} copy(bf16[2,128,2,512]{3,2,1,0:T(2,128)(2,1)} %param.7) | data formatting | bytes 1048576 | tf_op args[1]
  2.1 2.4 %collective-permute-start.1 = (bf16[2,192,512]{2,1,0:T(8,128)(2,1)S(1)}, bf16[2,192,512]{2,1,0:T(8,128)(2,1)S(1)}, u32[]{:S(2)}, u32[]{:S(2)}) collective-permute-start(bf16[2,192,512]{2,1,0:T(8,128)(2,1)S(1)} %get-tuple-element.45), channel_id=1, source_target_pairs={{1,2},{3,4},{5,6},{2,1},{4,3},{6,5},{9,10},{11,12},{13,14},{10,9},... | collective-permute-start | bytes 1179656 | tf_op jit(solution)/shard_map/ppermute | solution.py:268
  5.0 6.2 %collective-permute-done.1.rout = bf16[2,192,512]{2,1,0:T(8,128)(2,1)S(1)} collective-permute-done((bf16[2,192,512]{2,1,0:T(8,128)(2,1)S(1)}, bf16[2,192,512]{2,1,0:T(8,128)(2,1)S(1)}, u32[]{:S(2)}, u32[]{:S(2)}) %collective-permute-start.1) | collective-permute-done | bytes 393248 | tf_op jit(solution)/shard_map/ppermute | solution.py:268
  11.2 1.6 %shard_map.85 = (bf16[1040,128]{1,0:T(8,128)(2,1)S(1)}, bf16[2,2,192,512]{3,2,1,0:T(8,128)(2,1)S(1)}) custom-call(s32[3]{0:T(128)S(1)} %pad_add_fusion.pos.refs_0_, bf16[2,2,192,512]{3,2,1,0:T(8,128)(2,1)S(1)} %maximum_bitcast_fusion.u, bf16[2,192,512]{2,1,0:T(8,128)(2,1)S(1)} %collective-permute-done.rin, ...), custom_call_target="tpu_custom_call" | custom-call | flops 1000000000 | tf_op jit(solution)/shard_map/pallas_call | solution.py:28
  13.4 1.2 %collective-permute-done.2 = bf16[1040,128]{1,0:T(8,128)(2,1)S(1)} collective-permute-done((bf16[1040,128]{1,0:T(8,128)(2,1)S(1)}, bf16[1040,128]{1,0:T(8,128)(2,1)S(1)}, u32[]{:S(2)}, u32[]{:S(2)}) %collective-permute-start.2) | collective-permute-done | bytes 266272 | tf_op jit(solution)/shard_map/ppermute | solution.py:268
  14.6 3.4 %collective-permute-start.7 = (bf16[2,1040,128]{2,1,0:T(8,128)(2,1)S(1)}, bf16[2,1040,128]{2,1,0:T(8,128)(2,1)S(1)}, u32[]{:S(2)}, u32[]{:S(2)}) collective-permute-start(bf16[2,1040,128]{2,1,0:T(8,128)(2,1)S(1)} %pad_maximum_fusion.refs_1_), channel_id=1, source_target_pairs={{0,2},{7,5},{2,4},{5,3},{4,6},{3,1},{8,10},{15,13},{10,12},{13,11}... | collective-permute-start | bytes 1597448 | tf_op jit(solution)/shard_map/ppermute | solution.py:268
  18.0 1.4 %shard_map.86 = (f32[288,192]{1,0:T(8,128)S(1)}, f32[288,192]{1,0:T(8,128)S(1)}, bf16[384,192]{1,0:T(8,128)(2,1)S(1)}, bf16[192,192]{1,0:T(8,128)(2,1)S(1)}) custom-call(s32[3]{0:T(128)S(1)} %pad_add_fusion.pos.refs_0_, bf16[2,2,192,512]{3,2,1,0:T(8,128)(2,1)S(1)} %maximum_bitcast_fusion.u, bf16[2,192,512]{2,1,0:T(8,128)(2,1)S(1)} %collective-permute-done.rin, ...), custom_call_target="tpu_custom_call" | custom-call | flops 1000000000 | tf_op jit(solution)/shard_map/pallas_call | solution.py:28
  19.5 6.3 %collective-permute-done.7.refs_2_.refs_1_ = bf16[2,1040,128]{2,1,0:T(8,128)(2,1)S(1)} collective-permute-done((bf16[2,1040,128]{2,1,0:T(8,128)(2,1)S(1)}, bf16[2,1040,128]{2,1,0:T(8,128)(2,1)S(1)}, u32[]{:S(2)}, u32[]{:S(2)}) %collective-permute-start.7) | collective-permute-done | bytes 532512 | tf_op jit(solution)/shard_map/ppermute | solution.py:268
  25.7 3.4 %collective-permute-start.12 = (bf16[2,1040,128]{2,1,0:T(8,128)(2,1)S(1)}, bf16[2,1040,128]{2,1,0:T(8,128)(2,1)S(1)}, u32[]{:S(2)}, u32[]{:S(2)}) collective-permute-start(bf16[2,1040,128]{2,1,0:T(8,128)(2,1)S(1)} %collective-permute-done.7.refs_2_.refs_1_), channel_id=1, source_target_pairs={{2,4},{5,3},{4,6},{3,1},{10,12},{13,11},{12,14},{11,9},{18,20},{21... | collective-permute-start | bytes 1597448 | tf_op jit(solution)/shard_map/ppermute | solution.py:268
  29.7 1.6 %collective-permute-start.4 = (f32[72,192]{1,0:T(8,128)S(1)}, f32[72,192]{1,0:T(8,128)S(1)}, u32[]{:S(2)}, u32[]{:S(2)}) collective-permute-start(f32[72,192]{1,0:T(8,128)S(1)} %get-tuple-element.27), channel_id=1, source_target_pairs={{0,8},{8,0},{16,24},{24,16},{1,9},{9,1},{17,25},{25,17},{2,10},{10... | collective-permute-start | bytes 165896 | tf_op jit(solution)/shard_map/ppermute | solution.py:271
  31.3 1.5 %collective-permute-start.5 = (f32[72,192]{1,0:T(8,128)S(1)}, f32[72,192]{1,0:T(8,128)S(1)}, u32[]{:S(2)}, u32[]{:S(2)}) collective-permute-start(f32[72,192]{1,0:T(8,128)S(1)} %get-tuple-element.28), channel_id=1, source_target_pairs={{0,16},{8,24},{16,0},{24,8},{1,17},{9,25},{17,1},{25,9},{2,18},{10... | collective-permute-start | bytes 165896 | tf_op jit(solution)/shard_map/ppermute | solution.py:271
  33.3 1.0 %collective-permute-done.4 = f32[72,192]{1,0:T(8,128)S(1)} collective-permute-done((f32[72,192]{1,0:T(8,128)S(1)}, f32[72,192]{1,0:T(8,128)S(1)}, u32[]{:S(2)}, u32[]{:S(2)}) %collective-permute-start.4) | collective-permute-done | bytes 55328 | tf_op jit(solution)/shard_map/ppermute | solution.py:271
  34.3 2.1 %collective-permute-done.5 = f32[72,192]{1,0:T(8,128)S(1)} collective-permute-done((f32[72,192]{1,0:T(8,128)S(1)}, f32[72,192]{1,0:T(8,128)S(1)}, u32[]{:S(2)}, u32[]{:S(2)}) %collective-permute-start.5) | collective-permute-done | bytes 55328 | tf_op jit(solution)/shard_map/ppermute | solution.py:271
  36.4 1.6 %collective-permute-done.6 = f32[72,192]{1,0:T(8,128)S(1)} collective-permute-done((f32[72,192]{1,0:T(8,128)S(1)}, f32[72,192]{1,0:T(8,128)S(1)}, u32[]{:S(2)}, u32[]{:S(2)}) %collective-permute-start.6) | collective-permute-done | bytes 55328 | tf_op jit(solution)/shard_map/ppermute | solution.py:271
  39.0 3.5 %collective-permute-start.9 = (f32[72,192]{1,0:T(8,128)S(1)}, f32[72,192]{1,0:T(8,128)S(1)}, u32[]{:S(2)}, u32[]{:S(2)}) collective-permute-start(f32[72,192]{1,0:T(8,128)S(1)} %add_add_fusion), channel_id=1, source_target_pairs={{0,2},{1,3},{2,0},{3,1},{4,6},{5,7},{6,4},{7,5},{8,10},{9,11},{10,... | collective-permute-start | bytes 165896 | tf_op jit(solution)/shard_map/ppermute | solution.py:268
  42.5 1.9 %collective-permute-start.18 = (bf16[2,1040,128]{2,1,0:T(8,128)(2,1)S(1)}, bf16[2,1040,128]{2,1,0:T(8,128)(2,1)S(1)}, u32[]{:S(2)}, u32[]{:S(2)}) collective-permute-start(bf16[2,1040,128]{2,1,0:T(8,128)(2,1)S(1)} %collective-permute-done.12.refs_3_.refs_1_), channel_id=1, source_target_pairs={{4,6},{3,1},{12,14},{11,9},{20,22},{19,17},{28,30},{27,25}} | collective-permute-start | bytes 1597448 | tf_op jit(solution)/shard_map/ppermute | solution.py:268
  44.5 8.8 %shard_map.89 = (f32[3,8,64,128]{3,2,1,0:T(8,128)S(1)}, bf16[2,2,64,512]{3,2,1,0:T(8,128)(2,1)S(1)}) custom-call(s32[3]{0:T(128)S(1)} %pad_add_fusion.pos.refs_0_, bf16[2,1040,128]{2,1,0:T(8,128)(2,1)S(1)} %pad_maximum_fusion.refs_1_, bf16[2,1040,128]{2,1,0:T(8,128)(2,1)S(1)} %collective-permute-done.7.refs_2_.refs_1_, ...), custom_call_target="tpu_custom_call" | custom-call | flops 6000000000 | tf_op jit(solution)/shard_map/pallas_call | solution.py:28
  54.6 2.4 %collective-permute-start.16 = (f32[72,192]{1,0:T(8,128)S(1)}, f32[72,192]{1,0:T(8,128)S(1)}, u32[]{:S(2)}, u32[]{:S(2)}) collective-permute-start(f32[72,192]{1,0:T(8,128)S(1)} %add_multiply_fusion), channel_id=1, source_target_pairs={{0,24},{8,16},{16,8},{24,0},{1,25},{9,17},{17,9},{25,1},{2,26},{10... | collective-permute-start | bytes 165896 | tf_op jit(solution)/shard_map/ppermute | solution.py:271
  57.0 4.8 %shard_map.90.refs_6_ = f32[3,8,64,128]{3,2,1,0:T(8,128)S(1)} custom-call(s32[3]{0:T(128)S(1)} %pad_add_fusion.pos.refs_0_, bf16[2,1040,128]{2,1,0:T(8,128)(2,1)S(1)} %collective-permute-done.7.refs_2_.refs_1_, bf16[2,1040,128]{2,1,0:T(8,128)(2,1)S(1)} %collective-permute-done.8.refs_3_.refs_2_, ...), custom_call_target="tpu_custom_call" | custom-call | flops 4000000000 | tf_op jit(solution)/shard_map/pallas_call | solution.py:28
  62.4 1.4 %collective-permute-done.19.refs_4_ = bf16[2,1040,128]{2,1,0:T(8,128)(2,1)S(1)} collective-permute-done((bf16[2,1040,128]{2,1,0:T(8,128)(2,1)S(1)}, bf16[2,1040,128]{2,1,0:T(8,128)(2,1)S(1)}, u32[]{:S(2)}, u32[]{:S(2)}) %collective-permute-start.19) | collective-permute-done | bytes 532512 | tf_op jit(solution)/shard_map/ppermute | solution.py:268
  63.9 1.4 %shard_map.91 = (bf16[2,8,64,128]{3,2,1,0:T(8,128)(2,1)S(1)}, f32[8,64,128]{2,1,0:T(8,128)S(1)}) custom-call(s32[3]{0:T(128)S(1)} %pad_add_fusion.pos.refs_0_, bf16[2,1040,128]{2,1,0:T(8,128)(2,1)S(1)} %collective-permute-done.12.refs_3_.refs_1_, bf16[2,1040,128]{2,1,0:T(8,128)(2,1)S(1)} %collective-permute-done.13.refs_4_.refs_2_, ...), custom_call_target="tpu_custom_call" | custom-call | flops 4000000000 | tf_op jit(solution)/shard_map/pallas_call | solution.py:28
  65.2 1.3 %collective-permute-start.20 = (bf16[2,8,64,128]{3,2,1,0:T(8,128)(2,1)S(1)}, bf16[2,8,64,128]{3,2,1,0:T(8,128)(2,1)S(1)}, u32[]{:S(2)}, u32[]{:S(2)}) collective-permute-start(bf16[2,8,64,128]{3,2,1,0:T(8,128)(2,1)S(1)} %get-tuple-element.37), channel_id=1, source_target_pairs={{8,0},{16,8},{24,16},{9,1},{17,9},{25,17},{10,2},{18,10},{26,18},{... | collective-permute-start | bytes 786440 | tf_op jit(solution)/shard_map/ppermute | solution.py:271
  67.5 1.4 %shard_map.88 = f32[576,192]{1,0:T(8,128)} custom-call(s32[3]{0:T(128)S(1)} %pad_add_fusion.pos.refs_0_, f32[4,72,192]{2,1,0:T(8,128)S(1)} %pad_maximum_fusion.1.mine, f32[4,72,192]{2,1,0:T(8,128)S(1)} %collective-permute-done.17.theirs), custom_call_target="tpu_custom_call" | custom-call | flops 1000000000 | tf_op jit(solution)/shard_map/pallas_call | solution.py:28
  68.9 6.6 %collective-permute-done.20.passed = bf16[2,8,64,128]{3,2,1,0:T(8,128)(2,1)S(1)} collective-permute-done((bf16[2,8,64,128]{3,2,1,0:T(8,128)(2,1)S(1)}, bf16[2,8,64,128]{3,2,1,0:T(8,128)(2,1)S(1)}, u32[]{:S(2)}, u32[]{:S(2)}) %collective-permute-start.20) | collective-permute-done | bytes 262176 | tf_op jit(solution)/shard_map/ppermute | solution.py:271
  (52 shorter events, 7.1 us)
Async XLA Ops:
  1.9 2.7 %copy-start.3 = (s32[2,8,2]{1,2,0:T(2,128)S(1)}, s32[2,8,2]{1,2,0:T(2,128)}, u32[]{:S(2)}) copy-start(s32[2,8,2]{1,2,0:T(2,128)} %param.11) | copy-start | bytes 388
  1.9 2.7 %copy-start.4 = (s32[2,8,2]{1,2,0:T(2,128)S(1)}, s32[2,8,2]{1,2,0:T(2,128)}, u32[]{:S(2)}) copy-start(s32[2,8,2]{1,2,0:T(2,128)} %param.10) | copy-start | bytes 388
  2.0 9.3 %copy-start = (bf16[9,64,192]{2,1,0:T(8,128)(2,1)S(1)}, bf16[9,64,192]{2,1,0:T(8,128)(2,1)}, u32[]{:S(2)}) copy-start(bf16[9,64,192]{2,1,0:T(8,128)(2,1)} %param.9) | copy-start | bytes 663556
  2.0 2.9 %collective-permute-start = (bf16[2,192,512]{2,1,0:T(8,128)(2,1)S(1)}, bf16[2,192,512]{2,1,0:T(8,128)(2,1)S(1)}, u32[]{:S(2)}, u32[]{:S(2)}) collective-permute-start(bf16[2,192,512]{2,1,0:T(8,128)(2,1)S(1)} %get-tuple-element.46), channel_id=1, source_target_pairs={{0,1},{1,0},{2,3},{3,2},{4,5},{5,4},{6,7},{7,6},{8,9},{9,8},{10,11... | collective-permute-start | bytes 1179656 | tf_op jit(solution)/shard_map/ppermute | solution.py:268
  2.1 9.1 %collective-permute-start.1 = (bf16[2,192,512]{2,1,0:T(8,128)(2,1)S(1)}, bf16[2,192,512]{2,1,0:T(8,128)(2,1)S(1)}, u32[]{:S(2)}, u32[]{:S(2)}) collective-permute-start(bf16[2,192,512]{2,1,0:T(8,128)(2,1)S(1)} %get-tuple-element.45), channel_id=1, source_target_pairs={{1,2},{3,4},{5,6},{2,1},{4,3},{6,5},{9,10},{11,12},{13,14},{10,9},... | collective-permute-start | bytes 1179656 | tf_op jit(solution)/shard_map/ppermute | solution.py:268
  12.8 1.7 %collective-permute-start.2 = (bf16[1040,128]{1,0:T(8,128)(2,1)S(1)}, bf16[1040,128]{1,0:T(8,128)(2,1)S(1)}, u32[]{:S(2)}, u32[]{:S(2)}) collective-permute-start(bf16[1040,128]{1,0:T(8,128)(2,1)S(1)} %get-tuple-element.22), channel_id=1, source_target_pairs={{0,1},{1,0},{2,3},{3,2},{4,5},{5,4},{6,7},{7,6},{8,9},{9,8},{10,11... | collective-permute-start | bytes 798728 | tf_op jit(solution)/shard_map/ppermute | solution.py:268
  14.6 11.2 %collective-permute-start.7 = (bf16[2,1040,128]{2,1,0:T(8,128)(2,1)S(1)}, bf16[2,1040,128]{2,1,0:T(8,128)(2,1)S(1)}, u32[]{:S(2)}, u32[]{:S(2)}) collective-permute-start(bf16[2,1040,128]{2,1,0:T(8,128)(2,1)S(1)} %pad_maximum_fusion.refs_1_), channel_id=1, source_target_pairs={{0,2},{7,5},{2,4},{5,3},{4,6},{3,1},{8,10},{15,13},{10,12},{13,11}... | collective-permute-start | bytes 1597448 | tf_op jit(solution)/shard_map/ppermute | solution.py:268
  19.4 9.7 %collective-permute-start.3 = (f32[288,192]{1,0:T(8,128)S(1)}, f32[288,192]{1,0:T(8,128)S(1)}, u32[]{:S(2)}, u32[]{:S(2)}) collective-permute-start(f32[288,192]{1,0:T(8,128)S(1)} %get-tuple-element.25), channel_id=1, source_target_pairs={{0,1},{1,0},{2,3},{3,2},{4,5},{5,4},{6,7},{7,6},{8,9},{9,8},{10,11... | collective-permute-start | bytes 663560 | tf_op jit(solution)/shard_map/ppermute | solution.py:268
  25.7 12.3 %collective-permute-start.8 = (bf16[2,1040,128]{2,1,0:T(8,128)(2,1)S(1)}, bf16[2,1040,128]{2,1,0:T(8,128)(2,1)S(1)}, u32[]{:S(2)}, u32[]{:S(2)}) collective-permute-start(bf16[2,1040,128]{2,1,0:T(8,128)(2,1)S(1)} %collective-permute-done.7.refs_2_.refs_1_), channel_id=1, source_target_pairs={{0,1},{1,0},{2,3},{3,2},{4,5},{5,4},{6,7},{7,6},{8,9},{9,8},{10,11... | collective-permute-start | bytes 1597448 | tf_op jit(solution)/shard_map/ppermute | solution.py:268
  25.7 16.8 %collective-permute-start.12 = (bf16[2,1040,128]{2,1,0:T(8,128)(2,1)S(1)}, bf16[2,1040,128]{2,1,0:T(8,128)(2,1)S(1)}, u32[]{:S(2)}, u32[]{:S(2)}) collective-permute-start(bf16[2,1040,128]{2,1,0:T(8,128)(2,1)S(1)} %collective-permute-done.7.refs_2_.refs_1_), channel_id=1, source_target_pairs={{2,4},{5,3},{4,6},{3,1},{10,12},{13,11},{12,14},{11,9},{18,20},{21... | collective-permute-start | bytes 1597448 | tf_op jit(solution)/shard_map/ppermute | solution.py:268
  29.7 4.6 %collective-permute-start.4 = (f32[72,192]{1,0:T(8,128)S(1)}, f32[72,192]{1,0:T(8,128)S(1)}, u32[]{:S(2)}, u32[]{:S(2)}) collective-permute-start(f32[72,192]{1,0:T(8,128)S(1)} %get-tuple-element.27), channel_id=1, source_target_pairs={{0,8},{8,0},{16,24},{24,16},{1,9},{9,1},{17,25},{25,17},{2,10},{10... | collective-permute-start | bytes 165896 | tf_op jit(solution)/shard_map/ppermute | solution.py:271
  31.3 5.1 %collective-permute-start.5 = (f32[72,192]{1,0:T(8,128)S(1)}, f32[72,192]{1,0:T(8,128)S(1)}, u32[]{:S(2)}, u32[]{:S(2)}) collective-permute-start(f32[72,192]{1,0:T(8,128)S(1)} %get-tuple-element.28), channel_id=1, source_target_pairs={{0,16},{8,24},{16,0},{24,8},{1,17},{9,25},{17,1},{25,9},{2,18},{10... | collective-permute-start | bytes 165896 | tf_op jit(solution)/shard_map/ppermute | solution.py:271
  32.8 5.3 %collective-permute-start.6 = (f32[72,192]{1,0:T(8,128)S(1)}, f32[72,192]{1,0:T(8,128)S(1)}, u32[]{:S(2)}, u32[]{:S(2)}) collective-permute-start(f32[72,192]{1,0:T(8,128)S(1)} %get-tuple-element.29), channel_id=1, source_target_pairs={{0,24},{8,16},{16,8},{24,0},{1,25},{9,17},{17,9},{25,1},{2,26},{10... | collective-permute-start | bytes 165896 | tf_op jit(solution)/shard_map/ppermute | solution.py:271
  38.1 15.2 %collective-permute-start.10 = (f32[72,192]{1,0:T(8,128)S(1)}, f32[72,192]{1,0:T(8,128)S(1)}, u32[]{:S(2)}, u32[]{:S(2)}) collective-permute-start(f32[72,192]{1,0:T(8,128)S(1)} %add_add_fusion), channel_id=1, source_target_pairs={{0,4},{1,5},{2,6},{3,7},{4,0},{5,1},{6,2},{7,3},{8,12},{9,13},{10,... | collective-permute-start | bytes 165896 | tf_op jit(solution)/shard_map/ppermute | solution.py:268
  38.2 15.2 %collective-permute-start.11 = (f32[72,192]{1,0:T(8,128)S(1)}, f32[72,192]{1,0:T(8,128)S(1)}, u32[]{:S(2)}, u32[]{:S(2)}) collective-permute-start(f32[72,192]{1,0:T(8,128)S(1)} %add_add_fusion), channel_id=1, source_target_pairs={{0,6},{1,7},{2,4},{3,5},{4,2},{5,3},{6,0},{7,1},{8,14},{9,15},{10,... | collective-permute-start | bytes 165896 | tf_op jit(solution)/shard_map/ppermute | solution.py:268
  39.0 14.4 %collective-permute-start.9 = (f32[72,192]{1,0:T(8,128)S(1)}, f32[72,192]{1,0:T(8,128)S(1)}, u32[]{:S(2)}, u32[]{:S(2)}) collective-permute-start(f32[72,192]{1,0:T(8,128)S(1)} %add_add_fusion), channel_id=1, source_target_pairs={{0,2},{1,3},{2,0},{3,1},{4,6},{5,7},{6,4},{7,5},{8,10},{9,11},{10,... | collective-permute-start | bytes 165896 | tf_op jit(solution)/shard_map/ppermute | solution.py:268
  42.5 10.8 %collective-permute-start.13 = (bf16[2,1040,128]{2,1,0:T(8,128)(2,1)S(1)}, bf16[2,1040,128]{2,1,0:T(8,128)(2,1)S(1)}, u32[]{:S(2)}, u32[]{:S(2)}) collective-permute-start(bf16[2,1040,128]{2,1,0:T(8,128)(2,1)S(1)} %collective-permute-done.12.refs_3_.refs_1_), channel_id=1, source_target_pairs={{0,1},{1,0},{2,3},{3,2},{4,5},{5,4},{6,7},{7,6},{8,9},{9,8},{10,11... | collective-permute-start | bytes 1597448 | tf_op jit(solution)/shard_map/ppermute | solution.py:268
  42.5 19.3 %collective-permute-start.18 = (bf16[2,1040,128]{2,1,0:T(8,128)(2,1)S(1)}, bf16[2,1040,128]{2,1,0:T(8,128)(2,1)S(1)}, u32[]{:S(2)}, u32[]{:S(2)}) collective-permute-start(bf16[2,1040,128]{2,1,0:T(8,128)(2,1)S(1)} %collective-permute-done.12.refs_3_.refs_1_), channel_id=1, source_target_pairs={{4,6},{3,1},{12,14},{11,9},{20,22},{19,17},{28,30},{27,25}} | collective-permute-start | bytes 1597448 | tf_op jit(solution)/shard_map/ppermute | solution.py:268
  53.4 8.4 %collective-permute-start.14 = (f32[72,192]{1,0:T(8,128)S(1)}, f32[72,192]{1,0:T(8,128)S(1)}, u32[]{:S(2)}, u32[]{:S(2)}) collective-permute-start(f32[72,192]{1,0:T(8,128)S(1)} %add_multiply_fusion), channel_id=1, source_target_pairs={{0,8},{8,0},{16,24},{24,16},{1,9},{9,1},{17,25},{25,17},{2,10},{10... | collective-permute-start | bytes 165896 | tf_op jit(solution)/shard_map/ppermute | solution.py:271
  54.1 7.7 %collective-permute-start.15 = (f32[72,192]{1,0:T(8,128)S(1)}, f32[72,192]{1,0:T(8,128)S(1)}, u32[]{:S(2)}, u32[]{:S(2)}) collective-permute-start(f32[72,192]{1,0:T(8,128)S(1)} %add_multiply_fusion), channel_id=1, source_target_pairs={{0,16},{8,24},{16,0},{24,8},{1,17},{9,25},{17,1},{25,9},{2,18},{10... | collective-permute-start | bytes 165896 | tf_op jit(solution)/shard_map/ppermute | solution.py:271
  54.6 7.2 %collective-permute-start.16 = (f32[72,192]{1,0:T(8,128)S(1)}, f32[72,192]{1,0:T(8,128)S(1)}, u32[]{:S(2)}, u32[]{:S(2)}) collective-permute-start(f32[72,192]{1,0:T(8,128)S(1)} %add_multiply_fusion), channel_id=1, source_target_pairs={{0,24},{8,16},{16,8},{24,0},{1,25},{9,17},{17,9},{25,1},{2,26},{10... | collective-permute-start | bytes 165896 | tf_op jit(solution)/shard_map/ppermute | solution.py:271
  61.9 2.0 %collective-permute-start.19 = (bf16[2,1040,128]{2,1,0:T(8,128)(2,1)S(1)}, bf16[2,1040,128]{2,1,0:T(8,128)(2,1)S(1)}, u32[]{:S(2)}, u32[]{:S(2)}) collective-permute-start(bf16[2,1040,128]{2,1,0:T(8,128)(2,1)S(1)} %collective-permute-done.18.refs_3_), channel_id=1, source_target_pairs={{0,1},{1,0},{2,3},{3,2},{4,5},{5,4},{6,7},{7,6},{8,9},{9,8},{10,11... | collective-permute-start | bytes 1597448 | tf_op jit(solution)/shard_map/ppermute | solution.py:268
  61.9 5.6 %collective-permute-start.17 = (f32[4,72,192]{2,1,0:T(8,128)S(1)}, f32[4,72,192]{2,1,0:T(8,128)S(1)}, u32[]{:S(2)}, u32[]{:S(2)}) collective-permute-start(f32[4,72,192]{2,1,0:T(8,128)S(1)} %pad_maximum_fusion.1.mine), channel_id=1, source_target_pairs={{0,1},{1,0},{2,3},{3,2},{4,5},{5,4},{6,7},{7,6},{8,9},{9,8},{10,11... | collective-permute-start | bytes 663560 | tf_op jit(solution)/shard_map/ppermute | solution.py:268
  65.2 10.2 %collective-permute-start.20 = (bf16[2,8,64,128]{3,2,1,0:T(8,128)(2,1)S(1)}, bf16[2,8,64,128]{3,2,1,0:T(8,128)(2,1)S(1)}, u32[]{:S(2)}, u32[]{:S(2)}) collective-permute-start(bf16[2,8,64,128]{3,2,1,0:T(8,128)(2,1)S(1)} %get-tuple-element.37), channel_id=1, source_target_pairs={{8,0},{16,8},{24,16},{9,1},{17,9},{25,17},{10,2},{18,10},{26,18},{... | collective-permute-start | bytes 786440 | tf_op jit(solution)/shard_map/ppermute | solution.py:271
  (2 other events, 3.8 us)

commit v3 on v2

--- a/solution.py
+++ b/solution.py
@@ -23,7 +23,7 @@
     return pl.BlockSpec(memory_space=memory_space)
 
 
-def call(kernel, out_shapes, args, scalars, scratch=(), micros=1.0):
+def call(kernel, out_shapes, args, scalars, scratch=(), micros=0.0):
     specs = [full(pltpu.SMEM)] * scalars + [full()] * (len(args) - scalars)
     return pl.pallas_call(
         kernel,
@@ -31,7 +31,7 @@
         in_specs=specs,
         out_specs=[full()] * len(out_shapes),
         scratch_shapes=list(scratch),
-        cost_estimate=pl.CostEstimate(flops=int(micros * 1000000000.0), bytes_accessed=0, transcendentals=0),
+        cost_estimate=pl.CostEstimate(flops=int(micros * 1e9), bytes_accessed=0, transcendentals=0),
         compiler_params=pltpu.CompilerParams(vmem_limit_bytes=24 << 20),
     )(*args)
 
@@ -121,8 +121,18 @@
             out[pl.ds(pl.multiple_of(at, 8), part)] = source[k]
 
 
-def collect(pos, entries, chips, g, tabs):
-    core = pos[0]
+def collect_codes(entries, chips, tabs):
+    for ref, where, first in entries:
+
+        @pl.when((where >= 0) & (where < chips))
+        def _(ref=ref, where=where, first=first):
+            for h in range(2):
+                band = 2 * where + (first if h == 0 else 1 - first)
+                codes = ref[h, ref.shape[1] - TABLE_ROWS :].astype(F32).astype(jnp.int32)
+                tabs[pl.ds(band, 1)] = codes[:1]
+
+
+def collect(entries, chips, g):
     frames, _, ch, columns = g.shape
     pieces = columns // LANES
     for ref, where, first in entries:
@@ -137,8 +147,6 @@
                             at = ((2 * f + r) * pieces + j) * ch
                             lanes = slice(LANES * j, LANES * (j + 1))
                             g[f, 2 * band + r + 1, :, lanes] = ref[h, at : at + ch]
-                codes = ref[h, 2 * frames * pieces * ch :].astype(F32).astype(jnp.int32)
-                tabs[pl.ds(band, 1)] = codes[:1]
 
 
 def convolved(weights, window):
@@ -148,23 +156,27 @@
     return total.astype(BF16)
 
 
-def spread(low, high, me, g, weights, codes, hits, gu, sums):
-    frames, _, ch, columns = g.shape
+def spread(count_rows, row_at, me, g, weights, codes, hits, gu, sums):
+    frames, rows, ch, columns = g.shape
     pieces = columns // LANES
 
-    def one_row(r, count):
-        for f in range(frames):
-            value = convolved(weights, g[f, pl.ds(r, 3)].reshape(3 * ch, columns))
-            for j in range(pieces):
-                for q in range(2):
-                    gu[f, r, j, q] = value[q * ch : (q + 1) * ch, LANES * j : LANES * (j + 1)]
-            for k in range(2 * pieces):
-                lane = (2 * f + r % 2) * (2 * pieces) + k
-                hits[count] = (r // 2) * LANES + lane
-                count += (lax.shift_right_logical(codes[r // 2, lane], 3) == me).astype(jnp.int32)
+    def two_rows(p, count):
+        for i in range(2):
+            known = 2 * p + i < count_rows
+            r = jnp.minimum(row_at(2 * p + i), rows - 3)
+            for f in range(frames):
+                value = convolved(weights, g[f, pl.ds(r, 3)].reshape(3 * ch, columns))
+                for j in range(pieces):
+                    for q in range(2):
+                        gu[f, r, j, q] = value[q * ch : (q + 1) * ch, LANES * j : LANES * (j + 1)]
+                for k in range(2 * pieces):
+                    lane = (2 * f + r % 2) * (2 * pieces) + k
+                    hits[count] = (r // 2) * LANES + lane
+                    named = lax.shift_right_logical(codes[r // 2, lane], 3) == me
+                    count += (known & named).astype(jnp.int32)
         return count
 
-    count = lax.fori_loop(low, high, one_row, 0)
+    count = lax.fori_loop(0, (count_rows + 1) // 2, two_rows, 0)
 
     def one_hit(k, _):
         hit = hits[k]
@@ -182,46 +194,77 @@
     return 4 * low + (low > 0).astype(jnp.int32), 4 * high + 4 - (high < chips - 1).astype(jnp.int32)
 
 
-def stage_kernel(reach, chips, pos, *refs):
+def side(ref, reach, pos, away):
+    core, chip = pos[0], pos[1]
+    step = (1 - 2 * core) * reach
+    return (ref, chip + step, 1 - core) if away else (ref, chip - step, core)
+
+
+def stage(old, reach, chips, entries, pos, weights, sums, g, tabs, codes, hits, gu, sem):
     core, chip = pos[0], pos[1]
     me = 2 * chip + core
-    step = 1 - 2 * core
-    if reach == 1:
-        own, near, far, wa, wf, sums, feat, g, tabs, codes, hits, gu, sem = refs
-        entries = [(own, chip, core)]
-        sums[...] = jnp.zeros(sums.shape, F32)
-    else:
-        near0, far0, near, far, wa, sums_in, sums, g, tabs, codes, hits, gu, sem = refs
-        entries = [(near0, chip - step * (reach - 1), core), (far0, chip + step * (reach - 1), 1 - core)]
-        sums[...] = sums_in[...]
-    entries += [(near, chip - step * reach, core), (far, chip + step * reach, 1 - core)]
+    collect_codes(entries, chips, tabs)
+    copy = pltpu.make_async_copy(tabs, codes, sem)
+    copy.start()
     frames, rows, ch, columns = g.shape
     zero = jnp.zeros((ch, columns), BF16)
     for f in range(frames):
         g[f, 0] = zero
         g[f, rows - 1] = zero
-    collect(pos, entries, chips, g, tabs)
-    copy = pltpu.make_async_copy(tabs, codes, sem)
-    copy.start()
-    if reach == 1:
-        for f in range(frames):
-            for r in range(2):
-                feat[f, r] = convolved(wf, g[f, pl.ds(2 * me + r, 3)].reshape(3 * ch, columns))
+    collect(entries, chips, g)
     copy.wait()
     low, high = ready_rows(chip, reach, chips)
-    if reach == 1:
-        spread(low, high, me, g, wa, codes, hits, gu, sums)
+    if old is None:
+        spread(high - low, lambda i: low + i, me, g, weights, codes, hits, gu, sums)
     else:
-        old_low, old_high = ready_rows(chip, reach - 1, chips)
-        spread(low, old_low, me, g, wa, codes, hits, gu, sums)
-        spread(old_high, high, me, g, wa, codes, hits, gu, sums)
-
-
-def final_stage_kernel(reach, chips, pos, near0, far0, near, far, wa, sums_in, passed, local, sums, *work):
-    stage_kernel(reach, chips, pos, near0, far0, near, far, wa, sums_in, sums, *work)
+        old_low, old_high = ready_rows(chip, old, chips)
+        below = old_low - low
+        spread(
+            below + high - old_high,
+            lambda i: jnp.where(i < below, low + i, old_high + i - below),
+            me, g, weights, codes, hits, gu, sums,
+        )
+
+
+def first_stage_kernel(chips, pos, own, wa, sums, *work):
+    sums[...] = jnp.zeros(sums.shape, F32)
+    stage(None, 0, chips, [side(own, 0, pos, False)], pos, wa, sums, *work)
+
+
+def middle_stage_kernel(chips, pos, own, near1, near2, far, wa, sums_in, sums, *work):
+    sums[...] = sums_in[...]
+    entries = [side(own, 0, pos, False), side(near1, 1, pos, False), side(near2, 2, pos, False)]
+    entries += [side(far.at[0], 1, pos, True), side(far.at[1], 2, pos, True)]
+    stage(0, 2, chips, entries, pos, wa, sums, *work)
+
+
+def final_stage_kernel(chips, pos, near2, far, near3, far3, wa, sums_in, passed, local, sums, *work):
+    sums[...] = sums_in[...]
+    entries = [side(near2, 2, pos, False), side(far.at[1], 2, pos, True)]
+    entries += [side(near3, 3, pos, False), side(far3, 3, pos, True)]
+    stage(2, 3, chips, entries, pos, wa, sums, *work)
     for s in range(2):
         passed[s] = sums[s].astype(BF16)
     local[...] = sums[2]
+
+
+def features_kernel(pos, own, near, wf, feat, rows4):
+    core = pos[0]
+    frames, _, ch, columns = feat.shape
+    pieces = columns // LANES
+    for f in range(frames):
+        for j in range(pieces):
+            lanes = slice(LANES * j, LANES * (j + 1))
+
+            def at(r):
+                return pl.ds(pl.multiple_of(((2 * f + r) * pieces + j) * ch, ch), ch)
+
+            rows4[3 * core, :, lanes] = near[1, at(1 - core)]
+            rows4[3 * (1 - core), :, lanes] = own[1, at(core)]
+            for r in range(2):
+                rows4[1 + r, :, lanes] = own[0, at(r)]
+        for r in range(2):
+            feat[f, r] = convolved(wf, rows4[r : r + 3].reshape(3 * ch, columns))
 
 
 def last_kernel(passed, local, prop):
@@ -293,7 +336,7 @@
         [halo],
     )
 
-    half_shapes = [jax.ShapeDtypeStruct((9 * channels // n, inner), F32) for n in (2, 4, 8)]
+    half_shape = jax.ShapeDtypeStruct((9 * channels // 2, inner), F32)
     weight_shapes = [
         jax.ShapeDtypeStruct((3 * n, 3 * channels), BF16) for n in (inner - channels, channels)
     ]
@@ -315,54 +358,61 @@
     near1 = to_tile(own, hop(0))
     keep, send, wa, wf = call(
         taps_kernel,
-        [half_shapes[0], half_shapes[0], *weight_shapes],
+        [half_shape, half_shape, *weight_shapes],
         (pos, u, rin, rout, after(g3, own), w3),
         1,
         [halo, pltpu.VMEM((9 * channels, inner), F32)],
+        micros=0.0,
     )
     got = to_tile(send, cores)
     part_rows = 9 * channels // (2 * groups)
     part_shape = jax.ShapeDtypeStruct((part_rows, inner), F32)
-    shares = call(shares_kernel, [part_shape] * groups, (pos, keep, got), 1, micros=0.6)
-    share = total_over([shares[0]] + [to_group(shares[k], swaps[k]) for k in range(1, groups)])
-    near2 = to_tile(near1, hop(1))
-    far1 = to_tile(near1, cores)
-    share = after(share, far1)
-    sums, feat = call(
-        lambda *refs: stage_kernel(1, chips, *refs),
-        [
-            jax.ShapeDtypeStruct(sums_shape, F32),
-            jax.ShapeDtypeStruct((frames, 2, channels, columns), BF16),
-        ],
-        (pos, own, near1, far1, wa, wf),
+    shares = call(shares_kernel, [part_shape] * groups, (pos, keep, got), 1, micros=0.0)
+
+    (sums,) = call(
+        lambda *refs: first_stage_kernel(chips, *refs),
+        [jax.ShapeDtypeStruct(sums_shape, F32)],
+        (pos, own, wa),
         1,
         work,
-        micros=6.0,
-    )
+        micros=0.0,
+    )
+    near1 = after(near1, sums, *shares)
+    near2 = to_tile(near1, hop(1))
+    share = total_over([shares[0]] + [to_group(shares[k], swaps[k]) for k in range(1, groups)])
+    pixels = frames * groups * height * tiles * columns
+    near2 = after(near2, share)
+    near3 = to_tile(near2, hop(2))
+    far = to_tile(jnp.stack((near1, near2)), cores)
+    share = after(share, far)
     share = total_over([share] + [to_tile(share, turns[k]) for k in range(1, chips)])
-    pixels = frames * groups * height * tiles * columns
     share = share * (1.0 / math.sqrt(pixels))
-    near3 = to_tile(near2, hop(2))
-    far2 = to_tile(near2, cores)
     (sums,) = call(
-        lambda *refs: stage_kernel(2, chips, *refs),
+        lambda *refs: middle_stage_kernel(chips, *refs),
         [jax.ShapeDtypeStruct(sums_shape, F32)],
-        (pos, near1, far1, near2, far2, wa, sums),
+        (pos, own, near1, near2, far, wa, sums),
         1,
         work,
-        micros=4.0,
-    )
-    share = after(share, far2)
-    mine = jnp.stack([share] + [to_group(share, swaps[k]) for k in range(1, groups)])
-    near3 = after(near3, mine, sums)
+        micros=2.0,
+    )
+    share = after(share, sums)
+    near3 = after(near3, share, sums)
     far3 = to_tile(near3, cores)
     passed, local = call(
-        lambda *refs: final_stage_kernel(3, chips, *refs),
+        lambda *refs: final_stage_kernel(chips, *refs),
         [jax.ShapeDtypeStruct((2, *sums_shape[1:]), BF16), jax.ShapeDtypeStruct(sums_shape[1:], F32)],
-        (pos, near2, far2, near3, far3, wa, sums),
+        (pos, near2, far, near3, far3, wa, sums),
         1,
         [pltpu.VMEM(sums_shape, F32)] + work,
-        micros=4.0,
+        micros=0.0,
+    )
+    mine = jnp.stack([share] + [to_group(share, swaps[k]) for k in range(1, groups)])
+    (feat,) = call(
+        features_kernel,
+        [jax.ShapeDtypeStruct((frames, 2, channels, columns), BF16)],
+        (pos, after(own, passed), near1, wf),
+        1,
+        [pltpu.VMEM((4, channels, columns), BF16)],
     )
     passed = to_group(passed, [(m + 1, m) for m in range(groups - 1)])
     theirs = to_tile(mine, cores)

time: 76.8 us -> 72.5 us (0.944)
  the two profiles are of different devices: /device:TPU:16 before, /device:TPU:0 now
where the time goes in v3:
time: 72.5 us; the launch traced here: 71.5 us
  starting transfers between devices  33.7 us (46%)
  Pallas kernels  18.3 us (25%)
  waiting for transfers between devices  14.7 us (20%)
  local copies, waits for them, and re-layouts  3.43 us (5%)
  between operations  1.01 us (1%)
    ppermute x13, starting transfers between devices, to_tile(): return lax.ppermute(block, 'tile', route)  25.3 us
    pallas_call x9, Pallas kernels, call(): pl.pallas_call(kernel, out_shape=out_shapes, in_specs=specs, out_specs=[f...  18.3 us
    ppermute x7, starting transfers between devices, to_group(): return lax.ppermute(block, 'tm', route)  8.33 us
    ppermute x13, waiting for transfers between devices, to_tile(): return lax.ppermute(block, 'tile', route)  7.36 us
    ppermute x7, waiting for transfers between devices, to_group(): return lax.ppermute(block, 'tm', route)  7.36 us
    unnamed x15, local copies, waits for them, and re-layouts  3.17 us
  transfers between devices with their start and end apart: 20, of which 10 were waited for; matrix products, arithmetic and copies ran while one was open for 2% of the time, Pallas kernels for 23%

profile of v3, /device:TPU:0, one launch (start us, length us, event | category | flops | bytes accessed | tf_op | source)
XLA Modules:
  0.0 71.5 jit_solution(16364085921608815907)
XLA Ops:
  3.9 1.6 %shard_map.85 = (bf16[1040,128]{1,0:T(8,128)(2,1)S(1)}, bf16[2,2,192,512]{3,2,1,0:T(8,128)(2,1)S(1)}) custom-call(s32[3]{0:T(128)S(1)} %pad_add_fusion.pos.refs_0_, bf16[2,2,192,512]{3,2,1,0:T(8,128)(2,1)S(1)} %maximum_bitcast_fusion.u, bf16[2,192,512]{2,1,0:T(8,128)(2,1)S(1)} %collective-permute-done.rin, ...), custom_call_target="tpu_custom_call" | custom-call | tf_op jit(solution)/shard_map/pallas_call | solution.py:28
  5.5 8.8 %collective-permute-start.2 = (bf16[1040,128]{1,0:T(8,128)(2,1)S(1)}, bf16[1040,128]{1,0:T(8,128)(2,1)S(1)}, u32[]{:S(2)}, u32[]{:S(2)}) collective-permute-start(bf16[1040,128]{1,0:T(8,128)(2,1)S(1)} %get-tuple-element.23), channel_id=1, source_target_pairs={{0,1},{1,0},{2,3},{3,2},{4,5},{5,4},{6,7},{7,6},{8,9},{9,8},{10,11... | collective-permute-start | bytes 798728 | tf_op jit(solution)/shard_map/ppermute | solution.py:311
  15.5 4.0 %collective-permute-start.7 = (bf16[2,1040,128]{2,1,0:T(8,128)(2,1)S(1)}, bf16[2,1040,128]{2,1,0:T(8,128)(2,1)S(1)}, u32[]{:S(2)}, u32[]{:S(2)}) collective-permute-start(bf16[2,1040,128]{2,1,0:T(8,128)(2,1)S(1)} %pad_maximum_fusion.1.refs_1_.own), channel_id=1, source_target_pairs={{0,2},{7,5},{2,4},{5,3},{4,6},{3,1},{8,10},{15,13},{10,12},{13,11}... | collective-permute-start | bytes 1597448 | tf_op jit(solution)/shard_map/ppermute | solution.py:311
  19.6 1.4 %shard_map.86 = (f32[288,192]{1,0:T(8,128)S(1)}, f32[288,192]{1,0:T(8,128)S(1)}, bf16[384,192]{1,0:T(8,128)(2,1)S(1)}, bf16[192,192]{1,0:T(8,128)(2,1)S(1)}) custom-call(s32[3]{0:T(128)S(1)} %pad_add_fusion.pos.refs_0_, bf16[2,2,192,512]{3,2,1,0:T(8,128)(2,1)S(1)} %maximum_bitcast_fusion.u, bf16[2,192,512]{2,1,0:T(8,128)(2,1)S(1)} %collective-permute-done.rin, ...), custom_call_target="tpu_custom_call" | custom-call | tf_op jit(solution)/shard_map/pallas_call | solution.py:28
  21.1 3.1 %shard_map.88.refs_6_ = f32[3,8,64,128]{3,2,1,0:T(8,128)S(1)} custom-call(s32[3]{0:T(128)S(1)} %pad_add_fusion.pos.refs_0_, bf16[2,1040,128]{2,1,0:T(8,128)(2,1)S(1)} %pad_maximum_fusion.1.refs_1_.own, bf16[384,192]{1,0:T(8,128)(2,1)S(1)} %get-tuple-element.31.refs_2_.refs_5_), custom_call_target="tpu_custom_call" | custom-call | tf_op jit(solution)/shard_map/pallas_call | solution.py:28
  24.8 1.5 %collective-permute-done.7.refs_2_.near = bf16[2,1040,128]{2,1,0:T(8,128)(2,1)S(1)} collective-permute-done((bf16[2,1040,128]{2,1,0:T(8,128)(2,1)S(1)}, bf16[2,1040,128]{2,1,0:T(8,128)(2,1)S(1)}, u32[]{:S(2)}, u32[]{:S(2)}) %collective-permute-start.7) | collective-permute-done | bytes 532512 | tf_op jit(solution)/shard_map/ppermute | solution.py:311
  27.0 1.6 %collective-permute-start.4 = (f32[72,192]{1,0:T(8,128)S(1)}, f32[72,192]{1,0:T(8,128)S(1)}, u32[]{:S(2)}, u32[]{:S(2)}) collective-permute-start(f32[72,192]{1,0:T(8,128)S(1)} %get-tuple-element.28), channel_id=1, source_target_pairs={{0,8},{8,0},{16,24},{24,16},{1,9},{9,1},{17,25},{25,17},{2,10},{10... | collective-permute-start | bytes 165896 | tf_op jit(solution)/shard_map/ppermute | solution.py:314
  28.5 1.5 %collective-permute-start.5 = (f32[72,192]{1,0:T(8,128)S(1)}, f32[72,192]{1,0:T(8,128)S(1)}, u32[]{:S(2)}, u32[]{:S(2)}) collective-permute-start(f32[72,192]{1,0:T(8,128)S(1)} %get-tuple-element.29), channel_id=1, source_target_pairs={{0,16},{8,24},{16,0},{24,8},{1,17},{9,25},{17,1},{25,9},{2,18},{10... | collective-permute-start | bytes 165896 | tf_op jit(solution)/shard_map/ppermute | solution.py:314
  30.5 1.3 %collective-permute-done.4 = f32[72,192]{1,0:T(8,128)S(1)} collective-permute-done((f32[72,192]{1,0:T(8,128)S(1)}, f32[72,192]{1,0:T(8,128)S(1)}, u32[]{:S(2)}, u32[]{:S(2)}) %collective-permute-start.4) | collective-permute-done | bytes 55328 | tf_op jit(solution)/shard_map/ppermute | solution.py:314
  31.8 2.0 %collective-permute-done.5 = f32[72,192]{1,0:T(8,128)S(1)} collective-permute-done((f32[72,192]{1,0:T(8,128)S(1)}, f32[72,192]{1,0:T(8,128)S(1)}, u32[]{:S(2)}, u32[]{:S(2)}) %collective-permute-start.5) | collective-permute-done | bytes 55328 | tf_op jit(solution)/shard_map/ppermute | solution.py:314
  33.8 1.5 %collective-permute-done.6 = f32[72,192]{1,0:T(8,128)S(1)} collective-permute-done((f32[72,192]{1,0:T(8,128)S(1)}, f32[72,192]{1,0:T(8,128)S(1)}, u32[]{:S(2)}, u32[]{:S(2)}) %collective-permute-start.6) | collective-permute-done | bytes 55328 | tf_op jit(solution)/shard_map/ppermute | solution.py:314
  35.5 1.3 %collective-permute-start.9 = (bf16[2,2,1040,128]{3,2,1,0:T(8,128)(2,1)S(1)}, bf16[2,2,1040,128]{3,2,1,0:T(8,128)(2,1)S(1)}, u32[]{:S(2)}, u32[]{:S(2)}) collective-permute-start(bf16[2,2,1040,128]{3,2,1,0:T(8,128)(2,1)S(1)} %pad_maximum_fusion), channel_id=1, source_target_pairs={{0,1},{1,0},{2,3},{3,2},{4,5},{5,4},{6,7},{7,6},{8,9},{9,8},{10,11... | collective-permute-start | bytes 3194888 | tf_op jit(solution)/shard_map/ppermute | solution.py:311
  37.4 1.6 %collective-permute-done.9.refs_4_.refs_2_ = bf16[2,2,1040,128]{3,2,1,0:T(8,128)(2,1)S(1)} collective-permute-done((bf16[2,2,1040,128]{3,2,1,0:T(8,128)(2,1)S(1)}, bf16[2,2,1040,128]{3,2,1,0:T(8,128)(2,1)S(1)}, u32[]{:S(2)}, u32[]{:S(2)}) %collective-permute-start.9) | collective-permute-done | bytes 1064992 | tf_op jit(solution)/shard_map/ppermute | solution.py:311
  39.0 4.5 %collective-permute-start.10 = (f32[72,192]{1,0:T(8,128)S(1)}, f32[72,192]{1,0:T(8,128)S(1)}, u32[]{:S(2)}, u32[]{:S(2)}) collective-permute-start(f32[72,192]{1,0:T(8,128)S(1)} %add_add_fusion), channel_id=1, source_target_pairs={{0,2},{1,3},{2,0},{3,1},{4,6},{5,7},{6,4},{7,5},{8,10},{9,11},{10,... | collective-permute-start | bytes 165896 | tf_op jit(solution)/shard_map/ppermute | solution.py:311
  43.5 1.7 %collective-permute-start.11 = (f32[72,192]{1,0:T(8,128)S(1)}, f32[72,192]{1,0:T(8,128)S(1)}, u32[]{:S(2)}, u32[]{:S(2)}) collective-permute-start(f32[72,192]{1,0:T(8,128)S(1)} %add_add_fusion), channel_id=1, source_target_pairs={{0,4},{1,5},{2,6},{3,7},{4,0},{5,1},{6,2},{7,3},{8,12},{9,13},{10,... | collective-permute-start | bytes 165896 | tf_op jit(solution)/shard_map/ppermute | solution.py:311
  46.1 5.0 %shard_map.89.refs_6_ = f32[3,8,64,128]{3,2,1,0:T(8,128)S(1)} custom-call(s32[3]{0:T(128)S(1)} %pad_add_fusion.pos.refs_0_, bf16[2,1040,128]{2,1,0:T(8,128)(2,1)S(1)} %pad_maximum_fusion.1.refs_1_.own, bf16[2,1040,128]{2,1,0:T(8,128)(2,1)S(1)} %collective-permute-done.7.refs_2_.near, bf16[2,1040,128]{2,1,0:T(8,128)(2,1)S(1)} %collective-permute-done.8.refs_3_.refs_1_, ...), custom_call_target="tpu_custom_call" | custom-call | flops 2000000000 | tf_op jit(solution)/shard_map/pallas_call | solution.py:28
  51.1 1.2 %collective-permute-done.11 = f32[72,192]{1,0:T(8,128)S(1)} collective-permute-done((f32[72,192]{1,0:T(8,128)S(1)}, f32[72,192]{1,0:T(8,128)S(1)}, u32[]{:S(2)}, u32[]{:S(2)}) %collective-permute-start.11) | collective-permute-done | bytes 55328 | tf_op jit(solution)/shard_map/ppermute | solution.py:311
  52.3 1.5 %collective-permute-start.18 = (bf16[2,1040,128]{2,1,0:T(8,128)(2,1)S(1)}, bf16[2,1040,128]{2,1,0:T(8,128)(2,1)S(1)}, u32[]{:S(2)}, u32[]{:S(2)}) collective-permute-start(bf16[2,1040,128]{2,1,0:T(8,128)(2,1)S(1)} %collective-permute-done.17.refs_3_), channel_id=1, source_target_pairs={{0,1},{1,0},{2,3},{3,2},{4,5},{5,4},{6,7},{7,6},{8,9},{9,8},{10,11... | collective-permute-start | bytes 1597448 | tf_op jit(solution)/shard_map/ppermute | solution.py:311
  55.2 2.1 %collective-permute-start.15 = (f32[72,192]{1,0:T(8,128)S(1)}, f32[72,192]{1,0:T(8,128)S(1)}, u32[]{:S(2)}, u32[]{:S(2)}) collective-permute-start(f32[72,192]{1,0:T(8,128)S(1)} %add_multiply_fusion), channel_id=1, source_target_pairs={{0,24},{8,16},{16,8},{24,0},{1,25},{9,17},{17,9},{25,1},{2,26},{10... | collective-permute-start | bytes 165896 | tf_op jit(solution)/shard_map/ppermute | solution.py:314
  57.3 4.1 %shard_map.91 = (bf16[2,8,64,128]{3,2,1,0:T(8,128)(2,1)S(1)}, f32[8,64,128]{2,1,0:T(8,128)S(1)}) custom-call(s32[3]{0:T(128)S(1)} %pad_add_fusion.pos.refs_0_, bf16[2,1040,128]{2,1,0:T(8,128)(2,1)S(1)} %collective-permute-done.8.refs_3_.refs_1_, bf16[2,2,1040,128]{3,2,1,0:T(8,128)(2,1)S(1)} %collective-permute-done.9.refs_4_.refs_2_, ...), custom_call_target="tpu_custom_call" | custom-call | tf_op jit(solution)/shard_map/pallas_call | solution.py:28
  61.4 1.3 %collective-permute-start.19 = (bf16[2,8,64,128]{3,2,1,0:T(8,128)(2,1)S(1)}, bf16[2,8,64,128]{3,2,1,0:T(8,128)(2,1)S(1)}, u32[]{:S(2)}, u32[]{:S(2)}) collective-permute-start(bf16[2,8,64,128]{3,2,1,0:T(8,128)(2,1)S(1)} %get-tuple-element.37), channel_id=1, source_target_pairs={{8,0},{16,8},{24,16},{9,1},{17,9},{25,17},{10,2},{18,10},{26,18},{... | collective-permute-start | bytes 786440 | tf_op jit(solution)/shard_map/ppermute | solution.py:314
  62.9 1.6 %collective-permute-done.16.theirs = f32[4,72,192]{2,1,0:T(8,128)S(1)} collective-permute-done((f32[4,72,192]{2,1,0:T(8,128)S(1)}, f32[4,72,192]{2,1,0:T(8,128)S(1)}, u32[]{:S(2)}, u32[]{:S(2)}) %collective-permute-start.16) | collective-permute-done | bytes 221216 | tf_op jit(solution)/shard_map/ppermute | solution.py:311
  64.4 1.4 %shard_map.90 = f32[576,192]{1,0:T(8,128)} custom-call(s32[3]{0:T(128)S(1)} %pad_add_fusion.pos.refs_0_, f32[4,72,192]{2,1,0:T(8,128)S(1)} %pad_maximum_fusion.2.mine, f32[4,72,192]{2,1,0:T(8,128)S(1)} %collective-permute-done.16.theirs), custom_call_target="tpu_custom_call" | custom-call | tf_op jit(solution)/shard_map/pallas_call | solution.py:28
  67.9 2.6 %collective-permute-done.19.passed = bf16[2,8,64,128]{3,2,1,0:T(8,128)(2,1)S(1)} collective-permute-done((bf16[2,8,64,128]{3,2,1,0:T(8,128)(2,1)S(1)}, bf16[2,8,64,128]{3,2,1,0:T(8,128)(2,1)S(1)}, u32[]{:S(2)}, u32[]{:S(2)}) %collective-permute-start.19) | collective-permute-done | bytes 262176 | tf_op jit(solution)/shard_map/ppermute | solution.py:314
  (52 shorter events, 12.4 us)
Async XLA Ops:
  1.9 1.3 %copy-start.2 = (bf16[2,64,2,512]{3,2,1,0:T(2,128)(2,1)S(1)}, bf16[2,64,2,512]{3,2,1,0:T(2,128)(2,1)}, u32[]{:S(2)}) copy-start(bf16[2,64,2,512]{3,2,1,0:T(2,128)(2,1)} %param.8) | copy-start | bytes 786436
  1.9 1.4 %copy-start.3 = (s32[2,8,2]{1,2,0:T(2,128)S(1)}, s32[2,8,2]{1,2,0:T(2,128)}, u32[]{:S(2)}) copy-start(s32[2,8,2]{1,2,0:T(2,128)} %param.11) | copy-start | bytes 388
  1.9 1.4 %copy-start.4 = (s32[2,8,2]{1,2,0:T(2,128)S(1)}, s32[2,8,2]{1,2,0:T(2,128)}, u32[]{:S(2)}) copy-start(s32[2,8,2]{1,2,0:T(2,128)} %param.10) | copy-start | bytes 388
  2.0 2.0 %copy-start = (bf16[9,64,192]{2,1,0:T(8,128)(2,1)S(1)}, bf16[9,64,192]{2,1,0:T(8,128)(2,1)}, u32[]{:S(2)}) copy-start(bf16[9,64,192]{2,1,0:T(8,128)(2,1)} %param.9) | copy-start | bytes 663556
  2.0 1.9 %collective-permute-start = (bf16[2,192,512]{2,1,0:T(8,128)(2,1)S(1)}, bf16[2,192,512]{2,1,0:T(8,128)(2,1)S(1)}, u32[]{:S(2)}, u32[]{:S(2)}) collective-permute-start(bf16[2,192,512]{2,1,0:T(8,128)(2,1)S(1)} %get-tuple-element.48), channel_id=1, source_target_pairs={{0,1},{1,0},{2,3},{3,2},{4,5},{5,4},{6,7},{7,6},{8,9},{9,8},{10,11... | collective-permute-start | bytes 1179656 | tf_op jit(solution)/shard_map/ppermute | solution.py:311
  2.6 1.4 %collective-permute-start.1 = (bf16[2,192,512]{2,1,0:T(8,128)(2,1)S(1)}, bf16[2,192,512]{2,1,0:T(8,128)(2,1)S(1)}, u32[]{:S(2)}, u32[]{:S(2)}) collective-permute-start(bf16[2,192,512]{2,1,0:T(8,128)(2,1)S(1)} %get-tuple-element.47), channel_id=1, source_target_pairs={{1,2},{3,4},{5,6},{2,1},{4,3},{6,5},{9,10},{11,12},{13,14},{10,9},... | collective-permute-start | bytes 1179656 | tf_op jit(solution)/shard_map/ppermute | solution.py:311
  5.5 9.9 %collective-permute-start.2 = (bf16[1040,128]{1,0:T(8,128)(2,1)S(1)}, bf16[1040,128]{1,0:T(8,128)(2,1)S(1)}, u32[]{:S(2)}, u32[]{:S(2)}) collective-permute-start(bf16[1040,128]{1,0:T(8,128)(2,1)S(1)} %get-tuple-element.23), channel_id=1, source_target_pairs={{0,1},{1,0},{2,3},{3,2},{4,5},{5,4},{6,7},{7,6},{8,9},{9,8},{10,11... | collective-permute-start | bytes 798728 | tf_op jit(solution)/shard_map/ppermute | solution.py:311
  15.5 10.8 %collective-permute-start.7 = (bf16[2,1040,128]{2,1,0:T(8,128)(2,1)S(1)}, bf16[2,1040,128]{2,1,0:T(8,128)(2,1)S(1)}, u32[]{:S(2)}, u32[]{:S(2)}) collective-permute-start(bf16[2,1040,128]{2,1,0:T(8,128)(2,1)S(1)} %pad_maximum_fusion.1.refs_1_.own), channel_id=1, source_target_pairs={{0,2},{7,5},{2,4},{5,3},{4,6},{3,1},{8,10},{15,13},{10,12},{13,11}... | collective-permute-start | bytes 1597448 | tf_op jit(solution)/shard_map/ppermute | solution.py:311
  21.0 3.2 %collective-permute-start.3 = (f32[288,192]{1,0:T(8,128)S(1)}, f32[288,192]{1,0:T(8,128)S(1)}, u32[]{:S(2)}, u32[]{:S(2)}) collective-permute-start(f32[288,192]{1,0:T(8,128)S(1)} %get-tuple-element.26), channel_id=1, source_target_pairs={{0,1},{1,0},{2,3},{3,2},{4,5},{5,4},{6,7},{7,6},{8,9},{9,8},{10,11... | collective-permute-start | bytes 663560 | tf_op jit(solution)/shard_map/ppermute | solution.py:311
  26.3 9.1 %collective-permute-start.8 = (bf16[2,1040,128]{2,1,0:T(8,128)(2,1)S(1)}, bf16[2,1040,128]{2,1,0:T(8,128)(2,1)S(1)}, u32[]{:S(2)}, u32[]{:S(2)}) collective-permute-start(bf16[2,1040,128]{2,1,0:T(8,128)(2,1)S(1)} %collective-permute-done.7.refs_2_.near), channel_id=1, source_target_pairs={{2,4},{5,3},{4,6},{3,1},{10,12},{13,11},{12,14},{11,9},{18,20},{21... | collective-permute-start | bytes 1597448 | tf_op jit(solution)/shard_map/ppermute | solution.py:311
  27.0 4.8 %collective-permute-start.4 = (f32[72,192]{1,0:T(8,128)S(1)}, f32[72,192]{1,0:T(8,128)S(1)}, u32[]{:S(2)}, u32[]{:S(2)}) collective-permute-start(f32[72,192]{1,0:T(8,128)S(1)} %get-tuple-element.28), channel_id=1, source_target_pairs={{0,8},{8,0},{16,24},{24,16},{1,9},{9,1},{17,25},{25,17},{2,10},{10... | collective-permute-start | bytes 165896 | tf_op jit(solution)/shard_map/ppermute | solution.py:314
  28.5 5.3 %collective-permute-start.5 = (f32[72,192]{1,0:T(8,128)S(1)}, f32[72,192]{1,0:T(8,128)S(1)}, u32[]{:S(2)}, u32[]{:S(2)}) collective-permute-start(f32[72,192]{1,0:T(8,128)S(1)} %get-tuple-element.29), channel_id=1, source_target_pairs={{0,16},{8,24},{16,0},{24,8},{1,17},{9,25},{17,1},{25,9},{2,18},{10... | collective-permute-start | bytes 165896 | tf_op jit(solution)/shard_map/ppermute | solution.py:314
  30.1 5.3 %collective-permute-start.6 = (f32[72,192]{1,0:T(8,128)S(1)}, f32[72,192]{1,0:T(8,128)S(1)}, u32[]{:S(2)}, u32[]{:S(2)}) collective-permute-start(f32[72,192]{1,0:T(8,128)S(1)} %get-tuple-element.30), channel_id=1, source_target_pairs={{0,24},{8,16},{16,8},{24,0},{1,25},{9,17},{17,9},{25,1},{2,26},{10... | collective-permute-start | bytes 165896 | tf_op jit(solution)/shard_map/ppermute | solution.py:314
  35.5 3.6 %collective-permute-start.9 = (bf16[2,2,1040,128]{3,2,1,0:T(8,128)(2,1)S(1)}, bf16[2,2,1040,128]{3,2,1,0:T(8,128)(2,1)S(1)}, u32[]{:S(2)}, u32[]{:S(2)}) collective-permute-start(bf16[2,2,1040,128]{3,2,1,0:T(8,128)(2,1)S(1)} %pad_maximum_fusion), channel_id=1, source_target_pairs={{0,1},{1,0},{2,3},{3,2},{4,5},{5,4},{6,7},{7,6},{8,9},{9,8},{10,11... | collective-permute-start | bytes 3194888 | tf_op jit(solution)/shard_map/ppermute | solution.py:311
  36.7 15.6 %collective-permute-start.17 = (bf16[2,1040,128]{2,1,0:T(8,128)(2,1)S(1)}, bf16[2,1040,128]{2,1,0:T(8,128)(2,1)S(1)}, u32[]{:S(2)}, u32[]{:S(2)}) collective-permute-start(bf16[2,1040,128]{2,1,0:T(8,128)(2,1)S(1)} %collective-permute-done.8.refs_3_.refs_1_), channel_id=1, source_target_pairs={{4,6},{3,1},{12,14},{11,9},{20,22},{19,17},{28,30},{27,25}} | collective-permute-start | bytes 1597448 | tf_op jit(solution)/shard_map/ppermute | solution.py:311
  39.0 12.0 %collective-permute-start.10 = (f32[72,192]{1,0:T(8,128)S(1)}, f32[72,192]{1,0:T(8,128)S(1)}, u32[]{:S(2)}, u32[]{:S(2)}) collective-permute-start(f32[72,192]{1,0:T(8,128)S(1)} %add_add_fusion), channel_id=1, source_target_pairs={{0,2},{1,3},{2,0},{3,1},{4,6},{5,7},{6,4},{7,5},{8,10},{9,11},{10,... | collective-permute-start | bytes 165896 | tf_op jit(solution)/shard_map/ppermute | solution.py:311
  43.5 8.8 %collective-permute-start.11 = (f32[72,192]{1,0:T(8,128)S(1)}, f32[72,192]{1,0:T(8,128)S(1)}, u32[]{:S(2)}, u32[]{:S(2)}) collective-permute-start(f32[72,192]{1,0:T(8,128)S(1)} %add_add_fusion), channel_id=1, source_target_pairs={{0,4},{1,5},{2,6},{3,7},{4,0},{5,1},{6,2},{7,3},{8,12},{9,13},{10,... | collective-permute-start | bytes 165896 | tf_op jit(solution)/shard_map/ppermute | solution.py:311
  45.3 7.0 %collective-permute-start.12 = (f32[72,192]{1,0:T(8,128)S(1)}, f32[72,192]{1,0:T(8,128)S(1)}, u32[]{:S(2)}, u32[]{:S(2)}) collective-permute-start(f32[72,192]{1,0:T(8,128)S(1)} %add_add_fusion), channel_id=1, source_target_pairs={{0,6},{1,7},{2,4},{3,5},{4,2},{5,3},{6,0},{7,1},{8,14},{9,15},{10,... | collective-permute-start | bytes 165896 | tf_op jit(solution)/shard_map/ppermute | solution.py:311
  52.3 5.0 %collective-permute-start.18 = (bf16[2,1040,128]{2,1,0:T(8,128)(2,1)S(1)}, bf16[2,1040,128]{2,1,0:T(8,128)(2,1)S(1)}, u32[]{:S(2)}, u32[]{:S(2)}) collective-permute-start(bf16[2,1040,128]{2,1,0:T(8,128)(2,1)S(1)} %collective-permute-done.17.refs_3_), channel_id=1, source_target_pairs={{0,1},{1,0},{2,3},{3,2},{4,5},{5,4},{6,7},{7,6},{8,9},{9,8},{10,11... | collective-permute-start | bytes 1597448 | tf_op jit(solution)/shard_map/ppermute | solution.py:311
  53.8 8.9 %collective-permute-start.13 = (f32[72,192]{1,0:T(8,128)S(1)}, f32[72,192]{1,0:T(8,128)S(1)}, u32[]{:S(2)}, u32[]{:S(2)}) collective-permute-start(f32[72,192]{1,0:T(8,128)S(1)} %add_multiply_fusion), channel_id=1, source_target_pairs={{0,8},{8,0},{16,24},{24,16},{1,9},{9,1},{17,25},{25,17},{2,10},{10... | collective-permute-start | bytes 165896 | tf_op jit(solution)/shard_map/ppermute | solution.py:314
  54.4 8.4 %collective-permute-start.14 = (f32[72,192]{1,0:T(8,128)S(1)}, f32[72,192]{1,0:T(8,128)S(1)}, u32[]{:S(2)}, u32[]{:S(2)}) collective-permute-start(f32[72,192]{1,0:T(8,128)S(1)} %add_multiply_fusion), channel_id=1, source_target_pairs={{0,16},{8,24},{16,0},{24,8},{1,17},{9,25},{17,1},{25,9},{2,18},{10... | collective-permute-start | bytes 165896 | tf_op jit(solution)/shard_map/ppermute | solution.py:314
  55.2 7.5 %collective-permute-start.15 = (f32[72,192]{1,0:T(8,128)S(1)}, f32[72,192]{1,0:T(8,128)S(1)}, u32[]{:S(2)}, u32[]{:S(2)}) collective-permute-start(f32[72,192]{1,0:T(8,128)S(1)} %add_multiply_fusion), channel_id=1, source_target_pairs={{0,24},{8,16},{16,8},{24,0},{1,25},{9,17},{17,9},{25,1},{2,26},{10... | collective-permute-start | bytes 165896 | tf_op jit(solution)/shard_map/ppermute | solution.py:314
  61.4 9.1 %collective-permute-start.19 = (bf16[2,8,64,128]{3,2,1,0:T(8,128)(2,1)S(1)}, bf16[2,8,64,128]{3,2,1,0:T(8,128)(2,1)S(1)}, u32[]{:S(2)}, u32[]{:S(2)}) collective-permute-start(bf16[2,8,64,128]{3,2,1,0:T(8,128)(2,1)S(1)} %get-tuple-element.37), channel_id=1, source_target_pairs={{8,0},{16,8},{24,16},{9,1},{17,9},{25,17},{10,2},{18,10},{26,18},{... | collective-permute-start | bytes 786440 | tf_op jit(solution)/shard_map/ppermute | solution.py:314
  62.8 1.6 %collective-permute-start.16 = (f32[4,72,192]{2,1,0:T(8,128)S(1)}, f32[4,72,192]{2,1,0:T(8,128)S(1)}, u32[]{:S(2)}, u32[]{:S(2)}) collective-permute-start(f32[4,72,192]{2,1,0:T(8,128)S(1)} %pad_maximum_fusion.2.mine), channel_id=1, source_target_pairs={{0,1},{1,0},{2,3},{3,2},{4,5},{5,4},{6,7},{7,6},{8,9},{9,8},{10,11... | collective-permute-start | bytes 663560 | tf_op jit(solution)/shard_map/ppermute | solution.py:311
  (1 other events, 1.2 us)

commit v4 on v3

--- a/solution.py
+++ b/solution.py
@@ -56,7 +56,7 @@
     return (from_right(wide).astype(BF16), row, from_left(wide).astype(BF16))
 
 
-def forward_kernel(pos, u, rin, rout, cot, w3, tab, msg, g3, halo):
+def forward_kernel(pos, u, rin, rout, cot, w3, tab, msg, halo):
     core = pos[0]
     frames, _, ch, columns = cot.shape
     pieces = columns // LANES
@@ -73,17 +73,23 @@
             for j in range(pieces):
                 at = ((2 * f + r) * pieces + j) * ch
                 msg[at : at + ch] = g[:, LANES * j : LANES * (j + 1)]
-            for k, part in enumerate(taps_of(g)):
-                g3[f, r, k * ch : (k + 1) * ch] = part
     msg[2 * frames * pieces * ch :] = tab[...]
 
 
-def taps_kernel(pos, u, rin, rout, g3, w3, keep, send, wa, wf, halo, total):
+def taps_kernel(pos, u, rin, rout, msg, w3, keep, send, wa, wf, halo, total, g3):
     core = pos[0]
-    size = g3.shape[2]
+    frames, _, size, columns = g3.shape
+    ch = size // 3
+    pieces = columns // LANES
     half = keep.shape[0]
     halo[core] = rout[...]
     halo[1 - core] = rin[...]
+    for f in range(frames):
+        for r in range(2):
+            at = (2 * f + r) * pieces * ch
+            row = jnp.concatenate([msg[at + j * ch : at + (j + 1) * ch] for j in range(pieces)], axis=1)
+            for k, part in enumerate(taps_of(row)):
+                g3[f, r, k * ch : (k + 1) * ch] = part
     for ky in range(3):
         acc = jnp.zeros((size, u.shape[2]), F32)
         for f in range(u.shape[0]):
@@ -95,7 +101,6 @@
         total[ky * size : (ky + 1) * size] = acc
     keep[...] = total[pl.ds(pl.multiple_of(core * half, 8), half)]
     send[...] = total[pl.ds(pl.multiple_of((1 - core) * half, 8), half)]
-    ch = size // 3
     for kx in range(3):
         rows = [w3[ky, kx * ch : (kx + 1) * ch] for ky in (2, 1, 0)]
         turned = jnp.transpose(jnp.concatenate(rows, axis=0).astype(F32)).astype(BF16)
@@ -157,26 +162,25 @@
 
 
 def spread(count_rows, row_at, me, g, weights, codes, hits, gu, sums):
-    frames, rows, ch, columns = g.shape
+    frames, _, ch, columns = g.shape
     pieces = columns // LANES
 
-    def two_rows(p, count):
-        for i in range(2):
-            known = 2 * p + i < count_rows
-            r = jnp.minimum(row_at(2 * p + i), rows - 3)
-            for f in range(frames):
-                value = convolved(weights, g[f, pl.ds(r, 3)].reshape(3 * ch, columns))
-                for j in range(pieces):
-                    for q in range(2):
-                        gu[f, r, j, q] = value[q * ch : (q + 1) * ch, LANES * j : LANES * (j + 1)]
-                for k in range(2 * pieces):
-                    lane = (2 * f + r % 2) * (2 * pieces) + k
-                    hits[count] = (r // 2) * LANES + lane
-                    named = lax.shift_right_logical(codes[r // 2, lane], 3) == me
-                    count += (known & named).astype(jnp.int32)
+    def one_row(i, count):
+        r = row_at(i)
+        for f in range(frames):
+            value = convolved(weights, g[f, pl.ds(r, 3)].reshape(3 * ch, columns))
+            for j in range(pieces):
+                for q in range(2):
+                    gu[f, r, j, q] = value[q * ch : (q + 1) * ch, LANES * j : LANES * (j + 1)]
+            for k in range(2 * pieces):
+                lane = (2 * f + r % 2) * (2 * pieces) + k
+                hits[count] = (r // 2) * LANES + lane
+                count += (lax.shift_right_logical(codes[r // 2, lane], 3) == me).astype(jnp.int32)
         return count
 
-    count = lax.fori_loop(0, (count_rows + 1) // 2, two_rows, 0)
+    pairs = count_rows // 2
+    count = lax.fori_loop(0, pairs, lambda p, n: one_row(2 * p + 1, one_row(2 * p, n)), 0)
+    count = lax.fori_loop(2 * pairs, count_rows, one_row, count)
 
     def one_hit(k, _):
         hit = hits[k]
@@ -231,16 +235,16 @@
     stage(None, 0, chips, [side(own, 0, pos, False)], pos, wa, sums, *work)
 
 
-def middle_stage_kernel(chips, pos, own, near1, near2, far, wa, sums_in, sums, *work):
+def middle_stage_kernel(chips, pos, own, near1, near2, far1, far2, wa, sums_in, sums, *work):
     sums[...] = sums_in[...]
     entries = [side(own, 0, pos, False), side(near1, 1, pos, False), side(near2, 2, pos, False)]
-    entries += [side(far.at[0], 1, pos, True), side(far.at[1], 2, pos, True)]
+    entries += [side(far1, 1, pos, True), side(far2, 2, pos, True)]
     stage(0, 2, chips, entries, pos, wa, sums, *work)
 
 
-def final_stage_kernel(chips, pos, near2, far, near3, far3, wa, sums_in, passed, local, sums, *work):
+def final_stage_kernel(chips, pos, near2, far2, near3, far3, wa, sums_in, passed, local, sums, *work):
     sums[...] = sums_in[...]
-    entries = [side(near2, 2, pos, False), side(far.at[1], 2, pos, True)]
+    entries = [side(near2, 2, pos, False), side(far2, 2, pos, True)]
     entries += [side(near3, 3, pos, False), side(far3, 3, pos, True)]
     stage(2, 3, chips, entries, pos, wa, sums, *work)
     for s in range(2):
@@ -325,12 +329,9 @@
 
     halo = pltpu.VMEM((2, frames, inner, columns), BF16)
     msg_rows = 2 * frames * pieces * channels + TABLE_ROWS
-    msg, g3 = call(
+    (msg,) = call(
         forward_kernel,
-        [
-            jax.ShapeDtypeStruct((msg_rows, LANES), BF16),
-            jax.ShapeDtypeStruct((frames, 2, 3 * channels, columns), BF16),
-        ],
+        [jax.ShapeDtypeStruct((msg_rows, LANES), BF16)],
         (pos, u, rin, rout, cot, w3, tab),
         1,
         [halo],
@@ -359,9 +360,13 @@
     keep, send, wa, wf = call(
         taps_kernel,
         [half_shape, half_shape, *weight_shapes],
-        (pos, u, rin, rout, after(g3, own), w3),
+        (pos, u, rin, rout, after(msg, own), w3),
         1,
-        [halo, pltpu.VMEM((9 * channels, inner), F32)],
+        [
+            halo,
+            pltpu.VMEM((9 * channels, inner), F32),
+            pltpu.VMEM((frames, 2, 3 * channels, columns), BF16),
+        ],
         micros=0.0,
     )
     got = to_tile(send, cores)
@@ -379,18 +384,20 @@
     )
     near1 = after(near1, sums, *shares)
     near2 = to_tile(near1, hop(1))
+    far1 = to_tile(near1, cores)
+    shares = [after(x, far1) for x in shares]
     share = total_over([shares[0]] + [to_group(shares[k], swaps[k]) for k in range(1, groups)])
     pixels = frames * groups * height * tiles * columns
     near2 = after(near2, share)
     near3 = to_tile(near2, hop(2))
-    far = to_tile(jnp.stack((near1, near2)), cores)
-    share = after(share, far)
+    far = [far1, to_tile(near2, cores)]
+    share = after(share, *far)
     share = total_over([share] + [to_tile(share, turns[k]) for k in range(1, chips)])
     share = share * (1.0 / math.sqrt(pixels))
     (sums,) = call(
         lambda *refs: middle_stage_kernel(chips, *refs),
         [jax.ShapeDtypeStruct(sums_shape, F32)],
-        (pos, own, near1, near2, far, wa, sums),
+        (pos, own, near1, near2, *far, wa, sums),
         1,
         work,
         micros=2.0,
@@ -401,7 +408,7 @@
     passed, local = call(
         lambda *refs: final_stage_kernel(chips, *refs),
         [jax.ShapeDtypeStruct((2, *sums_shape[1:]), BF16), jax.ShapeDtypeStruct(sums_shape[1:], F32)],
-        (pos, near2, far, near3, far3, wa, sums),
+        (pos, near2, far[1], near3, far3, wa, sums),
         1,
         [pltpu.VMEM(sums_shape, F32)] + work,
         micros=0.0,

time: 72.5 us -> 71.4 us (0.985)
    pallas_call x9, Pallas kernels: 18.3 us -> 17.6 us  [call(): pl.pallas_call(kernel, out_shape=out_shapes, in_specs=specs, out_specs=[f...]
    ppermute x13 -> x14, starting transfers between devices: 25.3 us -> 25.7 us  [to_tile(): return lax.ppermute(block, 'tile', route)]
    ppermute x13 -> x14, waiting for transfers between devices: 7.36 us -> 7.33 us  [to_tile(): return lax.ppermute(block, 'tile', route)]
  transfers between devices with their start and end apart: 20 -> 21, of which waited for: 10 -> 11; matrix products, arithmetic and copies ran while one was open for 2% -> 2% of each run, Pallas kernels for 23% -> 23%
where the time goes in v4:
time: 71.4 us; the launch traced here: 71 us
  starting transfers between devices  34 us (48%)
  Pallas kernels  17.6 us (25%)
  waiting for transfers between devices  14.7 us (21%)
  local copies, waits for them, and re-layouts  3.43 us (5%)
  between operations  1.01 us (1%)
    ppermute x14, starting transfers between devices, to_tile(): return lax.ppermute(block, 'tile', route)  25.7 us
    pallas_call x9, Pallas kernels, call(): pl.pallas_call(kernel, out_shape=out_shapes, in_specs=specs, out_specs=[f...  17.6 us
    ppermute x7, starting transfers between devices, to_group(): return lax.ppermute(block, 'tm', route)  8.27 us
    ppermute x7, waiting for transfers between devices, to_group(): return lax.ppermute(block, 'tm', route)  7.38 us
    ppermute x14, waiting for transfers between devices, to_tile(): return lax.ppermute(block, 'tile', route)  7.33 us
    unnamed x15, local copies, waits for them, and re-layouts  3.17 us
  transfers between devices with their start and end apart: 21, of which 11 were waited for; matrix products, arithmetic and copies ran while one was open for 2% of the time, Pallas kernels for 23%

profile of v4, /device:TPU:0, one launch (start us, length us, event | category | flops | bytes accessed | tf_op | source)
XLA Modules:
  0.0 71.0 jit_solution(8416219920973192636)
XLA Ops:
  3.9 1.4 %shard_map.85.msg = bf16[1040,128]{1,0:T(8,128)(2,1)S(1)} custom-call(s32[3]{0:T(128)S(1)} %pad_add_fusion.pos.refs_0_, bf16[2,2,192,512]{3,2,1,0:T(8,128)(2,1)S(1)} %maximum_bitcast_fusion.u, bf16[2,192,512]{2,1,0:T(8,128)(2,1)S(1)} %collective-permute-done.rin, bf16[2,192,512]{2,1,0:T(8,128)(2,1)S(1)} %collective-permute-done.1.rout, ...), custom_call_target="tpu_custom_call" | custom-call | tf_op jit(solution)/shard_map/pallas_call | solution.py:28
  5.4 8.8 %collective-permute-start.2 = (bf16[1040,128]{1,0:T(8,128)(2,1)S(1)}, bf16[1040,128]{1,0:T(8,128)(2,1)S(1)}, u32[]{:S(2)}, u32[]{:S(2)}) collective-permute-start(bf16[1040,128]{1,0:T(8,128)(2,1)S(1)} %shard_map.85.msg), channel_id=1, source_target_pairs={{0,1},{1,0},{2,3},{3,2},{4,5},{5,4},{6,7},{7,6},{8,9},{9,8},{10,11... | collective-permute-start | bytes 798728 | tf_op jit(solution)/shard_map/ppermute | solution.py:315
  14.1 1.2 %collective-permute-done.2 = bf16[1040,128]{1,0:T(8,128)(2,1)S(1)} collective-permute-done((bf16[1040,128]{1,0:T(8,128)(2,1)S(1)}, bf16[1040,128]{1,0:T(8,128)(2,1)S(1)}, u32[]{:S(2)}, u32[]{:S(2)}) %collective-permute-start.2) | collective-permute-done | bytes 266272 | tf_op jit(solution)/shard_map/ppermute | solution.py:315
  15.4 4.0 %collective-permute-start.4 = (bf16[2,1040,128]{2,1,0:T(8,128)(2,1)S(1)}, bf16[2,1040,128]{2,1,0:T(8,128)(2,1)S(1)}, u32[]{:S(2)}, u32[]{:S(2)}) collective-permute-start(bf16[2,1040,128]{2,1,0:T(8,128)(2,1)S(1)} %pad_maximum_fusion.refs_1_.own), channel_id=1, source_target_pairs={{0,2},{7,5},{2,4},{5,3},{4,6},{3,1},{8,10},{15,13},{10,12},{13,11}... | collective-permute-start | bytes 1597448 | tf_op jit(solution)/shard_map/ppermute | solution.py:315
  19.4 1.5 %shard_map.86 = (f32[288,192]{1,0:T(8,128)S(1)}, f32[288,192]{1,0:T(8,128)S(1)}, bf16[384,192]{1,0:T(8,128)(2,1)S(1)}, bf16[192,192]{1,0:T(8,128)(2,1)S(1)}) custom-call(s32[3]{0:T(128)S(1)} %pad_add_fusion.pos.refs_0_, bf16[2,2,192,512]{3,2,1,0:T(8,128)(2,1)S(1)} %maximum_bitcast_fusion.u, bf16[2,192,512]{2,1,0:T(8,128)(2,1)S(1)} %collective-permute-done.rin, ...), custom_call_target="tpu_custom_call" | custom-call | tf_op jit(solution)/shard_map/pallas_call | solution.py:28
  21.0 2.7 %shard_map.88.refs_7_ = f32[3,8,64,128]{3,2,1,0:T(8,128)S(1)} custom-call(s32[3]{0:T(128)S(1)} %pad_add_fusion.pos.refs_0_, bf16[2,1040,128]{2,1,0:T(8,128)(2,1)S(1)} %pad_maximum_fusion.refs_1_.own, bf16[384,192]{1,0:T(8,128)(2,1)S(1)} %get-tuple-element.28.refs_2_.refs_6_.refs_5_), custom_call_target="tpu_custom_call" | custom-call | tf_op jit(solution)/shard_map/pallas_call | solution.py:28
  24.3 1.9 %collective-permute-done.4.refs_2_.near = bf16[2,1040,128]{2,1,0:T(8,128)(2,1)S(1)} collective-permute-done((bf16[2,1040,128]{2,1,0:T(8,128)(2,1)S(1)}, bf16[2,1040,128]{2,1,0:T(8,128)(2,1)S(1)}, u32[]{:S(2)}, u32[]{:S(2)}) %collective-permute-start.4) | collective-permute-done | bytes 532512 | tf_op jit(solution)/shard_map/ppermute | solution.py:315
  26.8 1.2 %collective-permute-done.5.refs_4_ = bf16[2,1040,128]{2,1,0:T(8,128)(2,1)S(1)} collective-permute-done((bf16[2,1040,128]{2,1,0:T(8,128)(2,1)S(1)}, bf16[2,1040,128]{2,1,0:T(8,128)(2,1)S(1)}, u32[]{:S(2)}, u32[]{:S(2)}) %collective-permute-start.5) | collective-permute-done | bytes 532512 | tf_op jit(solution)/shard_map/ppermute | solution.py:315
  28.1 1.5 %collective-permute-start.6 = (f32[72,192]{1,0:T(8,128)S(1)}, f32[72,192]{1,0:T(8,128)S(1)}, u32[]{:S(2)}, u32[]{:S(2)}) collective-permute-start(f32[72,192]{1,0:T(8,128)S(1)} %get-tuple-element.34), channel_id=1, source_target_pairs={{0,8},{8,0},{16,24},{24,16},{1,9},{9,1},{17,25},{25,17},{2,10},{10... | collective-permute-start | bytes 165896 | tf_op jit(solution)/shard_map/ppermute | solution.py:318
  29.6 1.5 %collective-permute-start.7 = (f32[72,192]{1,0:T(8,128)S(1)}, f32[72,192]{1,0:T(8,128)S(1)}, u32[]{:S(2)}, u32[]{:S(2)}) collective-permute-start(f32[72,192]{1,0:T(8,128)S(1)} %get-tuple-element.35), channel_id=1, source_target_pairs={{0,16},{8,24},{16,0},{24,8},{1,17},{9,25},{17,1},{25,9},{2,18},{10... | collective-permute-start | bytes 165896 | tf_op jit(solution)/shard_map/ppermute | solution.py:318
  32.4 1.5 %collective-permute-done.7 = f32[72,192]{1,0:T(8,128)S(1)} collective-permute-done((f32[72,192]{1,0:T(8,128)S(1)}, f32[72,192]{1,0:T(8,128)S(1)}, u32[]{:S(2)}, u32[]{:S(2)}) %collective-permute-start.7) | collective-permute-done | bytes 55328 | tf_op jit(solution)/shard_map/ppermute | solution.py:318
  33.9 2.4 %collective-permute-done.8 = f32[72,192]{1,0:T(8,128)S(1)} collective-permute-done((f32[72,192]{1,0:T(8,128)S(1)}, f32[72,192]{1,0:T(8,128)S(1)}, u32[]{:S(2)}, u32[]{:S(2)}) %collective-permute-start.8) | collective-permute-done | bytes 55328 | tf_op jit(solution)/shard_map/ppermute | solution.py:318
  38.9 3.6 %collective-permute-start.11 = (f32[72,192]{1,0:T(8,128)S(1)}, f32[72,192]{1,0:T(8,128)S(1)}, u32[]{:S(2)}, u32[]{:S(2)}) collective-permute-start(f32[72,192]{1,0:T(8,128)S(1)} %add_add_fusion), channel_id=1, source_target_pairs={{0,2},{1,3},{2,0},{3,1},{4,6},{5,7},{6,4},{7,5},{8,10},{9,11},{10,... | collective-permute-start | bytes 165896 | tf_op jit(solution)/shard_map/ppermute | solution.py:315
  42.5 1.8 %collective-permute-start.12 = (f32[72,192]{1,0:T(8,128)S(1)}, f32[72,192]{1,0:T(8,128)S(1)}, u32[]{:S(2)}, u32[]{:S(2)}) collective-permute-start(f32[72,192]{1,0:T(8,128)S(1)} %add_add_fusion), channel_id=1, source_target_pairs={{0,4},{1,5},{2,6},{3,7},{4,0},{5,1},{6,2},{7,3},{8,12},{9,13},{10,... | collective-permute-start | bytes 165896 | tf_op jit(solution)/shard_map/ppermute | solution.py:315
  44.3 1.4 %collective-permute-start.13 = (f32[72,192]{1,0:T(8,128)S(1)}, f32[72,192]{1,0:T(8,128)S(1)}, u32[]{:S(2)}, u32[]{:S(2)}) collective-permute-start(f32[72,192]{1,0:T(8,128)S(1)} %add_add_fusion), channel_id=1, source_target_pairs={{0,6},{1,7},{2,4},{3,5},{4,2},{5,3},{6,0},{7,1},{8,14},{9,15},{10,... | collective-permute-start | bytes 165896 | tf_op jit(solution)/shard_map/ppermute | solution.py:315
  45.7 5.1 %shard_map.89.refs_6_ = f32[3,8,64,128]{3,2,1,0:T(8,128)S(1)} custom-call(s32[3]{0:T(128)S(1)} %pad_add_fusion.pos.refs_0_, bf16[2,1040,128]{2,1,0:T(8,128)(2,1)S(1)} %pad_maximum_fusion.refs_1_.own, bf16[2,1040,128]{2,1,0:T(8,128)(2,1)S(1)} %collective-permute-done.4.refs_2_.near, bf16[2,1040,128]{2,1,0:T(8,128)(2,1)S(1)} %collective-permute-done.9.refs_3_.refs_1_, ...), custom_call_target="tpu_custom_call" | custom-call | flops 2000000000 | tf_op jit(solution)/shard_map/pallas_call | solution.py:28
  51.2 2.4 %collective-permute-start.19 = (bf16[2,1040,128]{2,1,0:T(8,128)(2,1)S(1)}, bf16[2,1040,128]{2,1,0:T(8,128)(2,1)S(1)}, u32[]{:S(2)}, u32[]{:S(2)}) collective-permute-start(bf16[2,1040,128]{2,1,0:T(8,128)(2,1)S(1)} %collective-permute-done.18.refs_3_), channel_id=1, source_target_pairs={{0,1},{1,0},{2,3},{3,2},{4,5},{5,4},{6,7},{7,6},{8,9},{9,8},{10,11... | collective-permute-start | bytes 1597448 | tf_op jit(solution)/shard_map/ppermute | solution.py:315
  54.1 1.2 %collective-permute-start.15 = (f32[72,192]{1,0:T(8,128)S(1)}, f32[72,192]{1,0:T(8,128)S(1)}, u32[]{:S(2)}, u32[]{:S(2)}) collective-permute-start(f32[72,192]{1,0:T(8,128)S(1)} %add_multiply_fusion), channel_id=1, source_target_pairs={{0,16},{8,24},{16,0},{24,8},{1,17},{9,25},{17,1},{25,9},{2,18},{10... | collective-permute-start | bytes 165896 | tf_op jit(solution)/shard_map/ppermute | solution.py:318
  55.3 1.8 %collective-permute-start.16 = (f32[72,192]{1,0:T(8,128)S(1)}, f32[72,192]{1,0:T(8,128)S(1)}, u32[]{:S(2)}, u32[]{:S(2)}) collective-permute-start(f32[72,192]{1,0:T(8,128)S(1)} %add_multiply_fusion), channel_id=1, source_target_pairs={{0,24},{8,16},{16,8},{24,0},{1,25},{9,17},{17,9},{25,1},{2,26},{10... | collective-permute-start | bytes 165896 | tf_op jit(solution)/shard_map/ppermute | solution.py:318
  57.1 3.8 %shard_map.91 = (bf16[2,8,64,128]{3,2,1,0:T(8,128)(2,1)S(1)}, f32[8,64,128]{2,1,0:T(8,128)S(1)}) custom-call(s32[3]{0:T(128)S(1)} %pad_add_fusion.pos.refs_0_, bf16[2,1040,128]{2,1,0:T(8,128)(2,1)S(1)} %collective-permute-done.9.refs_3_.refs_1_, bf16[2,1040,128]{2,1,0:T(8,128)(2,1)S(1)} %collective-permute-done.10.refs_5_.refs_2_, ...), custom_call_target="tpu_custom_call" | custom-call | tf_op jit(solution)/shard_map/pallas_call | solution.py:28
  60.8 1.3 %collective-permute-start.20 = (bf16[2,8,64,128]{3,2,1,0:T(8,128)(2,1)S(1)}, bf16[2,8,64,128]{3,2,1,0:T(8,128)(2,1)S(1)}, u32[]{:S(2)}, u32[]{:S(2)}) collective-permute-start(bf16[2,8,64,128]{3,2,1,0:T(8,128)(2,1)S(1)} %get-tuple-element.41), channel_id=1, source_target_pairs={{8,0},{16,8},{24,16},{9,1},{17,9},{25,17},{10,2},{18,10},{26,18},{... | collective-permute-start | bytes 786440 | tf_op jit(solution)/shard_map/ppermute | solution.py:318
  62.3 1.6 %collective-permute-done.17.theirs = f32[4,72,192]{2,1,0:T(8,128)S(1)} collective-permute-done((f32[4,72,192]{2,1,0:T(8,128)S(1)}, f32[4,72,192]{2,1,0:T(8,128)S(1)}, u32[]{:S(2)}, u32[]{:S(2)}) %collective-permute-start.17) | collective-permute-done | bytes 221216 | tf_op jit(solution)/shard_map/ppermute | solution.py:315
  63.8 1.4 %shard_map.90 = f32[576,192]{1,0:T(8,128)} custom-call(s32[3]{0:T(128)S(1)} %pad_add_fusion.pos.refs_0_, f32[4,72,192]{2,1,0:T(8,128)S(1)} %pad_maximum_fusion.1.mine, f32[4,72,192]{2,1,0:T(8,128)S(1)} %collective-permute-done.17.theirs), custom_call_target="tpu_custom_call" | custom-call | tf_op jit(solution)/shard_map/pallas_call | solution.py:28
  67.3 2.6 %collective-permute-done.20.passed = bf16[2,8,64,128]{3,2,1,0:T(8,128)(2,1)S(1)} collective-permute-done((bf16[2,8,64,128]{3,2,1,0:T(8,128)(2,1)S(1)}, bf16[2,8,64,128]{3,2,1,0:T(8,128)(2,1)S(1)}, u32[]{:S(2)}, u32[]{:S(2)}) %collective-permute-start.20) | collective-permute-done | bytes 262176 | tf_op jit(solution)/shard_map/ppermute | solution.py:318
  (53 shorter events, 12.5 us)
Async XLA Ops:
  1.9 1.4 %copy-start.3 = (s32[2,8,2]{1,2,0:T(2,128)S(1)}, s32[2,8,2]{1,2,0:T(2,128)}, u32[]{:S(2)}) copy-start(s32[2,8,2]{1,2,0:T(2,128)} %param.11) | copy-start | bytes 388
  1.9 1.4 %copy-start.4 = (s32[2,8,2]{1,2,0:T(2,128)S(1)}, s32[2,8,2]{1,2,0:T(2,128)}, u32[]{:S(2)}) copy-start(s32[2,8,2]{1,2,0:T(2,128)} %param.10) | copy-start | bytes 388
  2.0 2.0 %copy-start = (bf16[9,64,192]{2,1,0:T(8,128)(2,1)S(1)}, bf16[9,64,192]{2,1,0:T(8,128)(2,1)}, u32[]{:S(2)}) copy-start(bf16[9,64,192]{2,1,0:T(8,128)(2,1)} %param.9) | copy-start | bytes 663556
  2.0 1.9 %collective-permute-start = (bf16[2,192,512]{2,1,0:T(8,128)(2,1)S(1)}, bf16[2,192,512]{2,1,0:T(8,128)(2,1)S(1)}, u32[]{:S(2)}, u32[]{:S(2)}) collective-permute-start(bf16[2,192,512]{2,1,0:T(8,128)(2,1)S(1)} %get-tuple-element.52), channel_id=1, source_target_pairs={{0,1},{1,0},{2,3},{3,2},{4,5},{5,4},{6,7},{7,6},{8,9},{9,8},{10,11... | collective-permute-start | bytes 1179656 | tf_op jit(solution)/shard_map/ppermute | solution.py:315
  2.6 1.4 %collective-permute-start.1 = (bf16[2,192,512]{2,1,0:T(8,128)(2,1)S(1)}, bf16[2,192,512]{2,1,0:T(8,128)(2,1)S(1)}, u32[]{:S(2)}, u32[]{:S(2)}) collective-permute-start(bf16[2,192,512]{2,1,0:T(8,128)(2,1)S(1)} %get-tuple-element.51), channel_id=1, source_target_pairs={{1,2},{3,4},{5,6},{2,1},{4,3},{6,5},{9,10},{11,12},{13,14},{10,9},... | collective-permute-start | bytes 1179656 | tf_op jit(solution)/shard_map/ppermute | solution.py:315
  5.4 9.9 %collective-permute-start.2 = (bf16[1040,128]{1,0:T(8,128)(2,1)S(1)}, bf16[1040,128]{1,0:T(8,128)(2,1)S(1)}, u32[]{:S(2)}, u32[]{:S(2)}) collective-permute-start(bf16[1040,128]{1,0:T(8,128)(2,1)S(1)} %shard_map.85.msg), channel_id=1, source_target_pairs={{0,1},{1,0},{2,3},{3,2},{4,5},{5,4},{6,7},{7,6},{8,9},{9,8},{10,11... | collective-permute-start | bytes 798728 | tf_op jit(solution)/shard_map/ppermute | solution.py:315
  15.4 10.8 %collective-permute-start.4 = (bf16[2,1040,128]{2,1,0:T(8,128)(2,1)S(1)}, bf16[2,1040,128]{2,1,0:T(8,128)(2,1)S(1)}, u32[]{:S(2)}, u32[]{:S(2)}) collective-permute-start(bf16[2,1040,128]{2,1,0:T(8,128)(2,1)S(1)} %pad_maximum_fusion.refs_1_.own), channel_id=1, source_target_pairs={{0,2},{7,5},{2,4},{5,3},{4,6},{3,1},{8,10},{15,13},{10,12},{13,11}... | collective-permute-start | bytes 1597448 | tf_op jit(solution)/shard_map/ppermute | solution.py:315
  20.9 2.8 %collective-permute-start.3 = (f32[288,192]{1,0:T(8,128)S(1)}, f32[288,192]{1,0:T(8,128)S(1)}, u32[]{:S(2)}, u32[]{:S(2)}) collective-permute-start(f32[288,192]{1,0:T(8,128)S(1)} %get-tuple-element.26), channel_id=1, source_target_pairs={{0,1},{1,0},{2,3},{3,2},{4,5},{5,4},{6,7},{7,6},{8,9},{9,8},{10,11... | collective-permute-start | bytes 663560 | tf_op jit(solution)/shard_map/ppermute | solution.py:315
  26.1 1.9 %collective-permute-start.5 = (bf16[2,1040,128]{2,1,0:T(8,128)(2,1)S(1)}, bf16[2,1040,128]{2,1,0:T(8,128)(2,1)S(1)}, u32[]{:S(2)}, u32[]{:S(2)}) collective-permute-start(bf16[2,1040,128]{2,1,0:T(8,128)(2,1)S(1)} %collective-permute-done.4.refs_2_.near), channel_id=1, source_target_pairs={{0,1},{1,0},{2,3},{3,2},{4,5},{5,4},{6,7},{7,6},{8,9},{9,8},{10,11... | collective-permute-start | bytes 1597448 | tf_op jit(solution)/shard_map/ppermute | solution.py:315
  26.1 10.2 %collective-permute-start.9 = (bf16[2,1040,128]{2,1,0:T(8,128)(2,1)S(1)}, bf16[2,1040,128]{2,1,0:T(8,128)(2,1)S(1)}, u32[]{:S(2)}, u32[]{:S(2)}) collective-permute-start(bf16[2,1040,128]{2,1,0:T(8,128)(2,1)S(1)} %collective-permute-done.4.refs_2_.near), channel_id=1, source_target_pairs={{2,4},{5,3},{4,6},{3,1},{10,12},{13,11},{12,14},{11,9},{18,20},{21... | collective-permute-start | bytes 1597448 | tf_op jit(solution)/shard_map/ppermute | solution.py:315
  28.1 4.4 %collective-permute-start.6 = (f32[72,192]{1,0:T(8,128)S(1)}, f32[72,192]{1,0:T(8,128)S(1)}, u32[]{:S(2)}, u32[]{:S(2)}) collective-permute-start(f32[72,192]{1,0:T(8,128)S(1)} %get-tuple-element.34), channel_id=1, source_target_pairs={{0,8},{8,0},{16,24},{24,16},{1,9},{9,1},{17,25},{25,17},{2,10},{10... | collective-permute-start | bytes 165896 | tf_op jit(solution)/shard_map/ppermute | solution.py:318
  29.6 4.4 %collective-permute-start.7 = (f32[72,192]{1,0:T(8,128)S(1)}, f32[72,192]{1,0:T(8,128)S(1)}, u32[]{:S(2)}, u32[]{:S(2)}) collective-permute-start(f32[72,192]{1,0:T(8,128)S(1)} %get-tuple-element.35), channel_id=1, source_target_pairs={{0,16},{8,24},{16,0},{24,8},{1,17},{9,25},{17,1},{25,9},{2,18},{10... | collective-permute-start | bytes 165896 | tf_op jit(solution)/shard_map/ppermute | solution.py:318
  31.1 5.3 %collective-permute-start.8 = (f32[72,192]{1,0:T(8,128)S(1)}, f32[72,192]{1,0:T(8,128)S(1)}, u32[]{:S(2)}, u32[]{:S(2)}) collective-permute-start(f32[72,192]{1,0:T(8,128)S(1)} %get-tuple-element.36), channel_id=1, source_target_pairs={{0,24},{8,16},{16,8},{24,0},{1,25},{9,17},{17,9},{25,1},{2,26},{10... | collective-permute-start | bytes 165896 | tf_op jit(solution)/shard_map/ppermute | solution.py:318
  36.4 2.6 %collective-permute-start.10 = (bf16[2,1040,128]{2,1,0:T(8,128)(2,1)S(1)}, bf16[2,1040,128]{2,1,0:T(8,128)(2,1)S(1)}, u32[]{:S(2)}, u32[]{:S(2)}) collective-permute-start(bf16[2,1040,128]{2,1,0:T(8,128)(2,1)S(1)} %collective-permute-done.9.refs_3_.refs_1_), channel_id=1, source_target_pairs={{0,1},{1,0},{2,3},{3,2},{4,5},{5,4},{6,7},{7,6},{8,9},{9,8},{10,11... | collective-permute-start | bytes 1597448 | tf_op jit(solution)/shard_map/ppermute | solution.py:315
  37.4 13.8 %collective-permute-start.18 = (bf16[2,1040,128]{2,1,0:T(8,128)(2,1)S(1)}, bf16[2,1040,128]{2,1,0:T(8,128)(2,1)S(1)}, u32[]{:S(2)}, u32[]{:S(2)}) collective-permute-start(bf16[2,1040,128]{2,1,0:T(8,128)(2,1)S(1)} %collective-permute-done.9.refs_3_.refs_1_), channel_id=1, source_target_pairs={{4,6},{3,1},{12,14},{11,9},{20,22},{19,17},{28,30},{27,25}} | collective-permute-start | bytes 1597448 | tf_op jit(solution)/shard_map/ppermute | solution.py:315
  38.9 11.9 %collective-permute-start.11 = (f32[72,192]{1,0:T(8,128)S(1)}, f32[72,192]{1,0:T(8,128)S(1)}, u32[]{:S(2)}, u32[]{:S(2)}) collective-permute-start(f32[72,192]{1,0:T(8,128)S(1)} %add_add_fusion), channel_id=1, source_target_pairs={{0,2},{1,3},{2,0},{3,1},{4,6},{5,7},{6,4},{7,5},{8,10},{9,11},{10,... | collective-permute-start | bytes 165896 | tf_op jit(solution)/shard_map/ppermute | solution.py:315
  42.5 8.7 %collective-permute-start.12 = (f32[72,192]{1,0:T(8,128)S(1)}, f32[72,192]{1,0:T(8,128)S(1)}, u32[]{:S(2)}, u32[]{:S(2)}) collective-permute-start(f32[72,192]{1,0:T(8,128)S(1)} %add_add_fusion), channel_id=1, source_target_pairs={{0,4},{1,5},{2,6},{3,7},{4,0},{5,1},{6,2},{7,3},{8,12},{9,13},{10,... | collective-permute-start | bytes 165896 | tf_op jit(solution)/shard_map/ppermute | solution.py:315
  44.3 6.8 %collective-permute-start.13 = (f32[72,192]{1,0:T(8,128)S(1)}, f32[72,192]{1,0:T(8,128)S(1)}, u32[]{:S(2)}, u32[]{:S(2)}) collective-permute-start(f32[72,192]{1,0:T(8,128)S(1)} %add_add_fusion), channel_id=1, source_target_pairs={{0,6},{1,7},{2,4},{3,5},{4,2},{5,3},{6,0},{7,1},{8,14},{9,15},{10,... | collective-permute-start | bytes 165896 | tf_op jit(solution)/shard_map/ppermute | solution.py:315
  51.2 5.9 %collective-permute-start.19 = (bf16[2,1040,128]{2,1,0:T(8,128)(2,1)S(1)}, bf16[2,1040,128]{2,1,0:T(8,128)(2,1)S(1)}, u32[]{:S(2)}, u32[]{:S(2)}) collective-permute-start(bf16[2,1040,128]{2,1,0:T(8,128)(2,1)S(1)} %collective-permute-done.18.refs_3_), channel_id=1, source_target_pairs={{0,1},{1,0},{2,3},{3,2},{4,5},{5,4},{6,7},{7,6},{8,9},{9,8},{10,11... | collective-permute-start | bytes 1597448 | tf_op jit(solution)/shard_map/ppermute | solution.py:315
  53.6 8.6 %collective-permute-start.14 = (f32[72,192]{1,0:T(8,128)S(1)}, f32[72,192]{1,0:T(8,128)S(1)}, u32[]{:S(2)}, u32[]{:S(2)}) collective-permute-start(f32[72,192]{1,0:T(8,128)S(1)} %add_multiply_fusion), channel_id=1, source_target_pairs={{0,8},{8,0},{16,24},{24,16},{1,9},{9,1},{17,25},{25,17},{2,10},{10... | collective-permute-start | bytes 165896 | tf_op jit(solution)/shard_map/ppermute | solution.py:318
  54.1 8.0 %collective-permute-start.15 = (f32[72,192]{1,0:T(8,128)S(1)}, f32[72,192]{1,0:T(8,128)S(1)}, u32[]{:S(2)}, u32[]{:S(2)}) collective-permute-start(f32[72,192]{1,0:T(8,128)S(1)} %add_multiply_fusion), channel_id=1, source_target_pairs={{0,16},{8,24},{16,0},{24,8},{1,17},{9,25},{17,1},{25,9},{2,18},{10... | collective-permute-start | bytes 165896 | tf_op jit(solution)/shard_map/ppermute | solution.py:318
  55.3 6.9 %collective-permute-start.16 = (f32[72,192]{1,0:T(8,128)S(1)}, f32[72,192]{1,0:T(8,128)S(1)}, u32[]{:S(2)}, u32[]{:S(2)}) collective-permute-start(f32[72,192]{1,0:T(8,128)S(1)} %add_multiply_fusion), channel_id=1, source_target_pairs={{0,24},{8,16},{16,8},{24,0},{1,25},{9,17},{17,9},{25,1},{2,26},{10... | collective-permute-start | bytes 165896 | tf_op jit(solution)/shard_map/ppermute | solution.py:318
  60.8 9.1 %collective-permute-start.20 = (bf16[2,8,64,128]{3,2,1,0:T(8,128)(2,1)S(1)}, bf16[2,8,64,128]{3,2,1,0:T(8,128)(2,1)S(1)}, u32[]{:S(2)}, u32[]{:S(2)}) collective-permute-start(bf16[2,8,64,128]{3,2,1,0:T(8,128)(2,1)S(1)} %get-tuple-element.41), channel_id=1, source_target_pairs={{8,0},{16,8},{24,16},{9,1},{17,9},{25,17},{10,2},{18,10},{26,18},{... | collective-permute-start | bytes 786440 | tf_op jit(solution)/shard_map/ppermute | solution.py:318
  62.2 1.6 %collective-permute-start.17 = (f32[4,72,192]{2,1,0:T(8,128)S(1)}, f32[4,72,192]{2,1,0:T(8,128)S(1)}, u32[]{:S(2)}, u32[]{:S(2)}) collective-permute-start(f32[4,72,192]{2,1,0:T(8,128)S(1)} %pad_maximum_fusion.1.mine), channel_id=1, source_target_pairs={{0,1},{1,0},{2,3},{3,2},{4,5},{5,4},{6,7},{7,6},{8,9},{9,8},{10,11... | collective-permute-start | bytes 663560 | tf_op jit(solution)/shard_map/ppermute | solution.py:315
  (2 other events, 2.5 us)

commit v5 on v4

--- a/solution.py
+++ b/solution.py
@@ -56,7 +56,7 @@
     return (from_right(wide).astype(BF16), row, from_left(wide).astype(BF16))
 
 
-def forward_kernel(pos, u, rin, rout, cot, w3, tab, msg, halo):
+def forward_kernel(pos, u, rin, rout, cot, wide, tab, msg, halo):
     core = pos[0]
     frames, _, ch, columns = cot.shape
     pieces = columns // LANES
@@ -65,9 +65,8 @@
     for f in range(frames):
         rows = (halo.at[0, f], u.at[f, 0], u.at[f, 1], halo.at[1, f])
         for r in range(2):
-            taps = jnp.dot(w3[0], rows[r][...], preferred_element_type=F32)
-            taps += jnp.dot(w3[1], rows[r + 1][...], preferred_element_type=F32)
-            taps += jnp.dot(w3[2], rows[r + 2][...], preferred_element_type=F32)
+            window = jnp.concatenate([row[...] for row in rows[r : r + 3]], axis=0)
+            taps = jnp.dot(wide[...], window, preferred_element_type=F32)
             z = taps[ch : 2 * ch] + from_left(taps[:ch]) + from_right(taps[2 * ch :])
             g = (cot[f, r].astype(F32) * act_slope(z)).astype(BF16)
             for j in range(pieces):
@@ -324,6 +323,7 @@
     rin = to_tile(lax.dynamic_index_in_dim(u, 1 - core, 1, keepdims=False), cores)
     cot = jnp.transpose(cotangent, (0, 2, 1, 3))
     w3 = weight.reshape(3, 3 * channels, inner)
+    wide = jnp.transpose(w3, (1, 0, 2)).reshape(3 * channels, 3 * inner)
     codes = (src_tile * 8 + src_blk).reshape(1, -1).astype(BF16)
     tab = jnp.pad(codes, ((0, TABLE_ROWS - 1), (0, LANES - codes.shape[1])))
 
@@ -332,7 +332,7 @@
     (msg,) = call(
         forward_kernel,
         [jax.ShapeDtypeStruct((msg_rows, LANES), BF16)],
-        (pos, u, rin, rout, cot, w3, tab),
+        (pos, u, rin, rout, cot, wide, tab),
         1,
         [halo],
     )

time: 71.4 us -> 71.4 us (level)
  transfers between devices with their start and end apart: 21 -> 21, of which waited for: 11 -> 10; matrix products, arithmetic and copies ran while one was open for 2% -> 2% of each run, Pallas kernels for 23% -> 23%
where the time goes in v5:
time: 71.4 us; the launch traced here: 71.1 us
  starting transfers between devices  33.6 us (47%)
  Pallas kernels  17.6 us (25%)
  waiting for transfers between devices  14.5 us (20%)
  local copies, waits for them, and re-layouts  4.05 us (6%)
  between operations  1 us (1%)
    ppermute x14, starting transfers between devices, to_tile(): return lax.ppermute(block, 'tile', route)  25.3 us
    pallas_call x9, Pallas kernels, call(): pl.pallas_call(kernel, out_shape=out_shapes, in_specs=specs, out_specs=[f...  17.6 us
    ppermute x7, starting transfers between devices, to_group(): return lax.ppermute(block, 'tm', route)  8.27 us
    ppermute x7, waiting for transfers between devices, to_group(): return lax.ppermute(block, 'tm', route)  7.53 us
    ppermute x14, waiting for transfers between devices, to_tile(): return lax.ppermute(block, 'tile', route)  6.99 us
    unnamed x15, local copies, waits for them, and re-layouts  3.44 us
  transfers between devices with their start and end apart: 21, of which 10 were waited for; matrix products, arithmetic and copies ran while one was open for 2% of the time, Pallas kernels for 23%

profile of v5, /device:TPU:0, one launch (start us, length us, event | category | flops | bytes accessed | tf_op | source)
XLA Modules:
  0.0 71.1 jit_solution(2595374680665569040)
XLA Ops:
  4.3 1.5 %shard_map.85.msg = bf16[1040,128]{1,0:T(8,128)(2,1)S(1)} custom-call(s32[3]{0:T(128)S(1)} %pad_add_fusion.pos.refs_0_, bf16[2,2,192,512]{3,2,1,0:T(8,128)(2,1)S(1)} %maximum_bitcast_fusion.u, bf16[2,192,512]{2,1,0:T(8,128)(2,1)S(1)} %collective-permute-done.rin, bf16[2,192,512]{2,1,0:T(8,128)(2,1)S(1)} %collective-permute-done.1.rout, ...), custom_call_target="tpu_custom_call" | custom-call | tf_op jit(solution)/shard_map/pallas_call | solution.py:28
  5.7 8.4 %collective-permute-start.2 = (bf16[1040,128]{1,0:T(8,128)(2,1)S(1)}, bf16[1040,128]{1,0:T(8,128)(2,1)S(1)}, u32[]{:S(2)}, u32[]{:S(2)}) collective-permute-start(bf16[1040,128]{1,0:T(8,128)(2,1)S(1)} %shard_map.85.msg), channel_id=1, source_target_pairs={{0,1},{1,0},{2,3},{3,2},{4,5},{5,4},{6,7},{7,6},{8,9},{9,8},{10,11... | collective-permute-start | bytes 798728 | tf_op jit(solution)/shard_map/ppermute | solution.py:314
  14.1 1.2 %collective-permute-done.2 = bf16[1040,128]{1,0:T(8,128)(2,1)S(1)} collective-permute-done((bf16[1040,128]{1,0:T(8,128)(2,1)S(1)}, bf16[1040,128]{1,0:T(8,128)(2,1)S(1)}, u32[]{:S(2)}, u32[]{:S(2)}) %collective-permute-start.2) | collective-permute-done | bytes 266272 | tf_op jit(solution)/shard_map/ppermute | solution.py:314
  15.4 4.0 %collective-permute-start.4 = (bf16[2,1040,128]{2,1,0:T(8,128)(2,1)S(1)}, bf16[2,1040,128]{2,1,0:T(8,128)(2,1)S(1)}, u32[]{:S(2)}, u32[]{:S(2)}) collective-permute-start(bf16[2,1040,128]{2,1,0:T(8,128)(2,1)S(1)} %pad_maximum_fusion.refs_1_.own), channel_id=1, source_target_pairs={{0,2},{7,5},{2,4},{5,3},{4,6},{3,1},{8,10},{15,13},{10,12},{13,11}... | collective-permute-start | bytes 1597448 | tf_op jit(solution)/shard_map/ppermute | solution.py:314
  19.4 1.5 %shard_map.86 = (f32[288,192]{1,0:T(8,128)S(1)}, f32[288,192]{1,0:T(8,128)S(1)}, bf16[384,192]{1,0:T(8,128)(2,1)S(1)}, bf16[192,192]{1,0:T(8,128)(2,1)S(1)}) custom-call(s32[3]{0:T(128)S(1)} %pad_add_fusion.pos.refs_0_, bf16[2,2,192,512]{3,2,1,0:T(8,128)(2,1)S(1)} %maximum_bitcast_fusion.u, bf16[2,192,512]{2,1,0:T(8,128)(2,1)S(1)} %collective-permute-done.rin, ...), custom_call_target="tpu_custom_call" | custom-call | tf_op jit(solution)/shard_map/pallas_call | solution.py:28
  21.0 2.8 %shard_map.88.refs_7_ = f32[3,8,64,128]{3,2,1,0:T(8,128)S(1)} custom-call(s32[3]{0:T(128)S(1)} %pad_add_fusion.pos.refs_0_, bf16[2,1040,128]{2,1,0:T(8,128)(2,1)S(1)} %pad_maximum_fusion.refs_1_.own, bf16[384,192]{1,0:T(8,128)(2,1)S(1)} %get-tuple-element.28.refs_2_.refs_6_.refs_5_), custom_call_target="tpu_custom_call" | custom-call | tf_op jit(solution)/shard_map/pallas_call | solution.py:28
  24.4 1.8 %collective-permute-done.4.refs_2_.near = bf16[2,1040,128]{2,1,0:T(8,128)(2,1)S(1)} collective-permute-done((bf16[2,1040,128]{2,1,0:T(8,128)(2,1)S(1)}, bf16[2,1040,128]{2,1,0:T(8,128)(2,1)S(1)}, u32[]{:S(2)}, u32[]{:S(2)}) %collective-permute-start.4) | collective-permute-done | bytes 532512 | tf_op jit(solution)/shard_map/ppermute | solution.py:314
  26.9 1.2 %collective-permute-done.5.refs_4_ = bf16[2,1040,128]{2,1,0:T(8,128)(2,1)S(1)} collective-permute-done((bf16[2,1040,128]{2,1,0:T(8,128)(2,1)S(1)}, bf16[2,1040,128]{2,1,0:T(8,128)(2,1)S(1)}, u32[]{:S(2)}, u32[]{:S(2)}) %collective-permute-start.5) | collective-permute-done | bytes 532512 | tf_op jit(solution)/shard_map/ppermute | solution.py:314
  28.1 1.5 %collective-permute-start.6 = (f32[72,192]{1,0:T(8,128)S(1)}, f32[72,192]{1,0:T(8,128)S(1)}, u32[]{:S(2)}, u32[]{:S(2)}) collective-permute-start(f32[72,192]{1,0:T(8,128)S(1)} %get-tuple-element.34), channel_id=1, source_target_pairs={{0,8},{8,0},{16,24},{24,16},{1,9},{9,1},{17,25},{25,17},{2,10},{10... | collective-permute-start | bytes 165896 | tf_op jit(solution)/shard_map/ppermute | solution.py:317
  29.6 1.5 %collective-permute-start.7 = (f32[72,192]{1,0:T(8,128)S(1)}, f32[72,192]{1,0:T(8,128)S(1)}, u32[]{:S(2)}, u32[]{:S(2)}) collective-permute-start(f32[72,192]{1,0:T(8,128)S(1)} %get-tuple-element.35), channel_id=1, source_target_pairs={{0,16},{8,24},{16,0},{24,8},{1,17},{9,25},{17,1},{25,9},{2,18},{10... | collective-permute-start | bytes 165896 | tf_op jit(solution)/shard_map/ppermute | solution.py:317
  32.4 1.5 %collective-permute-done.7 = f32[72,192]{1,0:T(8,128)S(1)} collective-permute-done((f32[72,192]{1,0:T(8,128)S(1)}, f32[72,192]{1,0:T(8,128)S(1)}, u32[]{:S(2)}, u32[]{:S(2)}) %collective-permute-start.7) | collective-permute-done | bytes 55328 | tf_op jit(solution)/shard_map/ppermute | solution.py:317
  33.9 2.4 %collective-permute-done.8 = f32[72,192]{1,0:T(8,128)S(1)} collective-permute-done((f32[72,192]{1,0:T(8,128)S(1)}, f32[72,192]{1,0:T(8,128)S(1)}, u32[]{:S(2)}, u32[]{:S(2)}) %collective-permute-start.8) | collective-permute-done | bytes 55328 | tf_op jit(solution)/shard_map/ppermute | solution.py:317
  39.0 3.5 %collective-permute-start.11 = (f32[72,192]{1,0:T(8,128)S(1)}, f32[72,192]{1,0:T(8,128)S(1)}, u32[]{:S(2)}, u32[]{:S(2)}) collective-permute-start(f32[72,192]{1,0:T(8,128)S(1)} %add_add_fusion), channel_id=1, source_target_pairs={{0,2},{1,3},{2,0},{3,1},{4,6},{5,7},{6,4},{7,5},{8,10},{9,11},{10,... | collective-permute-start | bytes 165896 | tf_op jit(solution)/shard_map/ppermute | solution.py:314
  42.5 1.9 %collective-permute-start.12 = (f32[72,192]{1,0:T(8,128)S(1)}, f32[72,192]{1,0:T(8,128)S(1)}, u32[]{:S(2)}, u32[]{:S(2)}) collective-permute-start(f32[72,192]{1,0:T(8,128)S(1)} %add_add_fusion), channel_id=1, source_target_pairs={{0,4},{1,5},{2,6},{3,7},{4,0},{5,1},{6,2},{7,3},{8,12},{9,13},{10,... | collective-permute-start | bytes 165896 | tf_op jit(solution)/shard_map/ppermute | solution.py:314
  44.4 1.4 %collective-permute-start.13 = (f32[72,192]{1,0:T(8,128)S(1)}, f32[72,192]{1,0:T(8,128)S(1)}, u32[]{:S(2)}, u32[]{:S(2)}) collective-permute-start(f32[72,192]{1,0:T(8,128)S(1)} %add_add_fusion), channel_id=1, source_target_pairs={{0,6},{1,7},{2,4},{3,5},{4,2},{5,3},{6,0},{7,1},{8,14},{9,15},{10,... | collective-permute-start | bytes 165896 | tf_op jit(solution)/shard_map/ppermute | solution.py:314
  45.7 5.0 %shard_map.89.refs_6_ = f32[3,8,64,128]{3,2,1,0:T(8,128)S(1)} custom-call(s32[3]{0:T(128)S(1)} %pad_add_fusion.pos.refs_0_, bf16[2,1040,128]{2,1,0:T(8,128)(2,1)S(1)} %pad_maximum_fusion.refs_1_.own, bf16[2,1040,128]{2,1,0:T(8,128)(2,1)S(1)} %collective-permute-done.4.refs_2_.near, bf16[2,1040,128]{2,1,0:T(8,128)(2,1)S(1)} %collective-permute-done.9.refs_3_.refs_1_, ...), custom_call_target="tpu_custom_call" | custom-call | flops 2000000000 | tf_op jit(solution)/shard_map/pallas_call | solution.py:28
  51.2 2.4 %collective-permute-start.19 = (bf16[2,1040,128]{2,1,0:T(8,128)(2,1)S(1)}, bf16[2,1040,128]{2,1,0:T(8,128)(2,1)S(1)}, u32[]{:S(2)}, u32[]{:S(2)}) collective-permute-start(bf16[2,1040,128]{2,1,0:T(8,128)(2,1)S(1)} %collective-permute-done.18.refs_3_), channel_id=1, source_target_pairs={{0,1},{1,0},{2,3},{3,2},{4,5},{5,4},{6,7},{7,6},{8,9},{9,8},{10,11... | collective-permute-start | bytes 1597448 | tf_op jit(solution)/shard_map/ppermute | solution.py:314
  54.1 1.2 %collective-permute-start.15 = (f32[72,192]{1,0:T(8,128)S(1)}, f32[72,192]{1,0:T(8,128)S(1)}, u32[]{:S(2)}, u32[]{:S(2)}) collective-permute-start(f32[72,192]{1,0:T(8,128)S(1)} %add_multiply_fusion), channel_id=1, source_target_pairs={{0,16},{8,24},{16,0},{24,8},{1,17},{9,25},{17,1},{25,9},{2,18},{10... | collective-permute-start | bytes 165896 | tf_op jit(solution)/shard_map/ppermute | solution.py:317
  55.3 1.8 %collective-permute-start.16 = (f32[72,192]{1,0:T(8,128)S(1)}, f32[72,192]{1,0:T(8,128)S(1)}, u32[]{:S(2)}, u32[]{:S(2)}) collective-permute-start(f32[72,192]{1,0:T(8,128)S(1)} %add_multiply_fusion), channel_id=1, source_target_pairs={{0,24},{8,16},{16,8},{24,0},{1,25},{9,17},{17,9},{25,1},{2,26},{10... | collective-permute-start | bytes 165896 | tf_op jit(solution)/shard_map/ppermute | solution.py:317
  57.1 3.7 %shard_map.91 = (bf16[2,8,64,128]{3,2,1,0:T(8,128)(2,1)S(1)}, f32[8,64,128]{2,1,0:T(8,128)S(1)}) custom-call(s32[3]{0:T(128)S(1)} %pad_add_fusion.pos.refs_0_, bf16[2,1040,128]{2,1,0:T(8,128)(2,1)S(1)} %collective-permute-done.9.refs_3_.refs_1_, bf16[2,1040,128]{2,1,0:T(8,128)(2,1)S(1)} %collective-permute-done.10.refs_5_.refs_2_, ...), custom_call_target="tpu_custom_call" | custom-call | tf_op jit(solution)/shard_map/pallas_call | solution.py:28
  60.8 1.3 %collective-permute-start.20 = (bf16[2,8,64,128]{3,2,1,0:T(8,128)(2,1)S(1)}, bf16[2,8,64,128]{3,2,1,0:T(8,128)(2,1)S(1)}, u32[]{:S(2)}, u32[]{:S(2)}) collective-permute-start(bf16[2,8,64,128]{3,2,1,0:T(8,128)(2,1)S(1)} %get-tuple-element.41), channel_id=1, source_target_pairs={{8,0},{16,8},{24,16},{9,1},{17,9},{25,17},{10,2},{18,10},{26,18},{... | collective-permute-start | bytes 786440 | tf_op jit(solution)/shard_map/ppermute | solution.py:317
  62.2 1.6 %collective-permute-done.17.theirs = f32[4,72,192]{2,1,0:T(8,128)S(1)} collective-permute-done((f32[4,72,192]{2,1,0:T(8,128)S(1)}, f32[4,72,192]{2,1,0:T(8,128)S(1)}, u32[]{:S(2)}, u32[]{:S(2)}) %collective-permute-start.17) | collective-permute-done | bytes 221216 | tf_op jit(solution)/shard_map/ppermute | solution.py:314
  63.8 1.4 %shard_map.90 = f32[576,192]{1,0:T(8,128)} custom-call(s32[3]{0:T(128)S(1)} %pad_add_fusion.pos.refs_0_, f32[4,72,192]{2,1,0:T(8,128)S(1)} %pad_maximum_fusion.1.mine, f32[4,72,192]{2,1,0:T(8,128)S(1)} %collective-permute-done.17.theirs), custom_call_target="tpu_custom_call" | custom-call | tf_op jit(solution)/shard_map/pallas_call | solution.py:28
  67.3 2.8 %collective-permute-done.20.passed = bf16[2,8,64,128]{3,2,1,0:T(8,128)(2,1)S(1)} collective-permute-done((bf16[2,8,64,128]{3,2,1,0:T(8,128)(2,1)S(1)}, bf16[2,8,64,128]{3,2,1,0:T(8,128)(2,1)S(1)}, u32[]{:S(2)}, u32[]{:S(2)}) %collective-permute-start.20) | collective-permute-done | bytes 262176 | tf_op jit(solution)/shard_map/ppermute | solution.py:317
  (55 shorter events, 13.0 us)
Async XLA Ops:
  0.6 1.2 %copy-start.1 = (bf16[2,64,2,512]{3,2,1,0:T(2,128)(2,1)S(1)}, bf16[2,64,2,512]{3,2,1,0:T(2,128)(2,1)}, u32[]{:S(2)}) copy-start(bf16[2,64,2,512]{3,2,1,0:T(2,128)(2,1)} %param.6) | copy-start | bytes 786436
  1.9 1.3 %copy-start = (bf16[9,64,192]{2,1,0:T(8,128)(2,1)S(1)}, bf16[9,64,192]{2,1,0:T(8,128)(2,1)}, u32[]{:S(2)}) copy-start(bf16[9,64,192]{2,1,0:T(8,128)(2,1)} %param.9) | copy-start | bytes 663556
  2.0 1.6 %copy-start.2 = (bf16[2,64,2,512]{3,2,1,0:T(2,128)(2,1)S(1)}, bf16[2,64,2,512]{3,2,1,0:T(2,128)(2,1)}, u32[]{:S(2)}) copy-start(bf16[2,64,2,512]{3,2,1,0:T(2,128)(2,1)} %param.8) | copy-start | bytes 786436
  2.0 2.2 %collective-permute-start = (bf16[2,192,512]{2,1,0:T(8,128)(2,1)S(1)}, bf16[2,192,512]{2,1,0:T(8,128)(2,1)S(1)}, u32[]{:S(2)}, u32[]{:S(2)}) collective-permute-start(bf16[2,192,512]{2,1,0:T(8,128)(2,1)S(1)} %get-tuple-element.52), channel_id=1, source_target_pairs={{0,1},{1,0},{2,3},{3,2},{4,5},{5,4},{6,7},{7,6},{8,9},{9,8},{10,11... | collective-permute-start | bytes 1179656 | tf_op jit(solution)/shard_map/ppermute | solution.py:314
  2.5 1.7 %collective-permute-start.1 = (bf16[2,192,512]{2,1,0:T(8,128)(2,1)S(1)}, bf16[2,192,512]{2,1,0:T(8,128)(2,1)S(1)}, u32[]{:S(2)}, u32[]{:S(2)}) collective-permute-start(bf16[2,192,512]{2,1,0:T(8,128)(2,1)S(1)} %get-tuple-element.51), channel_id=1, source_target_pairs={{1,2},{3,4},{5,6},{2,1},{4,3},{6,5},{9,10},{11,12},{13,14},{10,9},... | collective-permute-start | bytes 1179656 | tf_op jit(solution)/shard_map/ppermute | solution.py:314
  5.7 9.6 %collective-permute-start.2 = (bf16[1040,128]{1,0:T(8,128)(2,1)S(1)}, bf16[1040,128]{1,0:T(8,128)(2,1)S(1)}, u32[]{:S(2)}, u32[]{:S(2)}) collective-permute-start(bf16[1040,128]{1,0:T(8,128)(2,1)S(1)} %shard_map.85.msg), channel_id=1, source_target_pairs={{0,1},{1,0},{2,3},{3,2},{4,5},{5,4},{6,7},{7,6},{8,9},{9,8},{10,11... | collective-permute-start | bytes 798728 | tf_op jit(solution)/shard_map/ppermute | solution.py:314
  15.4 10.8 %collective-permute-start.4 = (bf16[2,1040,128]{2,1,0:T(8,128)(2,1)S(1)}, bf16[2,1040,128]{2,1,0:T(8,128)(2,1)S(1)}, u32[]{:S(2)}, u32[]{:S(2)}) collective-permute-start(bf16[2,1040,128]{2,1,0:T(8,128)(2,1)S(1)} %pad_maximum_fusion.refs_1_.own), channel_id=1, source_target_pairs={{0,2},{7,5},{2,4},{5,3},{4,6},{3,1},{8,10},{15,13},{10,12},{13,11}... | collective-permute-start | bytes 1597448 | tf_op jit(solution)/shard_map/ppermute | solution.py:314
  20.9 2.9 %collective-permute-start.3 = (f32[288,192]{1,0:T(8,128)S(1)}, f32[288,192]{1,0:T(8,128)S(1)}, u32[]{:S(2)}, u32[]{:S(2)}) collective-permute-start(f32[288,192]{1,0:T(8,128)S(1)} %get-tuple-element.26), channel_id=1, source_target_pairs={{0,1},{1,0},{2,3},{3,2},{4,5},{5,4},{6,7},{7,6},{8,9},{9,8},{10,11... | collective-permute-start | bytes 663560 | tf_op jit(solution)/shard_map/ppermute | solution.py:314
  26.2 1.9 %collective-permute-start.5 = (bf16[2,1040,128]{2,1,0:T(8,128)(2,1)S(1)}, bf16[2,1040,128]{2,1,0:T(8,128)(2,1)S(1)}, u32[]{:S(2)}, u32[]{:S(2)}) collective-permute-start(bf16[2,1040,128]{2,1,0:T(8,128)(2,1)S(1)} %collective-permute-done.4.refs_2_.near), channel_id=1, source_target_pairs={{0,1},{1,0},{2,3},{3,2},{4,5},{5,4},{6,7},{7,6},{8,9},{9,8},{10,11... | collective-permute-start | bytes 1597448 | tf_op jit(solution)/shard_map/ppermute | solution.py:314
  26.2 10.2 %collective-permute-start.9 = (bf16[2,1040,128]{2,1,0:T(8,128)(2,1)S(1)}, bf16[2,1040,128]{2,1,0:T(8,128)(2,1)S(1)}, u32[]{:S(2)}, u32[]{:S(2)}) collective-permute-start(bf16[2,1040,128]{2,1,0:T(8,128)(2,1)S(1)} %collective-permute-done.4.refs_2_.near), channel_id=1, source_target_pairs={{2,4},{5,3},{4,6},{3,1},{10,12},{13,11},{12,14},{11,9},{18,20},{21... | collective-permute-start | bytes 1597448 | tf_op jit(solution)/shard_map/ppermute | solution.py:314
  28.1 4.4 %collective-permute-start.6 = (f32[72,192]{1,0:T(8,128)S(1)}, f32[72,192]{1,0:T(8,128)S(1)}, u32[]{:S(2)}, u32[]{:S(2)}) collective-permute-start(f32[72,192]{1,0:T(8,128)S(1)} %get-tuple-element.34), channel_id=1, source_target_pairs={{0,8},{8,0},{16,24},{24,16},{1,9},{9,1},{17,25},{25,17},{2,10},{10... | collective-permute-start | bytes 165896 | tf_op jit(solution)/shard_map/ppermute | solution.py:317
  29.6 4.4 %collective-permute-start.7 = (f32[72,192]{1,0:T(8,128)S(1)}, f32[72,192]{1,0:T(8,128)S(1)}, u32[]{:S(2)}, u32[]{:S(2)}) collective-permute-start(f32[72,192]{1,0:T(8,128)S(1)} %get-tuple-element.35), channel_id=1, source_target_pairs={{0,16},{8,24},{16,0},{24,8},{1,17},{9,25},{17,1},{25,9},{2,18},{10... | collective-permute-start | bytes 165896 | tf_op jit(solution)/shard_map/ppermute | solution.py:317
  31.1 5.3 %collective-permute-start.8 = (f32[72,192]{1,0:T(8,128)S(1)}, f32[72,192]{1,0:T(8,128)S(1)}, u32[]{:S(2)}, u32[]{:S(2)}) collective-permute-start(f32[72,192]{1,0:T(8,128)S(1)} %get-tuple-element.36), channel_id=1, source_target_pairs={{0,24},{8,16},{16,8},{24,0},{1,25},{9,17},{17,9},{25,1},{2,26},{10... | collective-permute-start | bytes 165896 | tf_op jit(solution)/shard_map/ppermute | solution.py:317
  36.4 2.6 %collective-permute-start.10 = (bf16[2,1040,128]{2,1,0:T(8,128)(2,1)S(1)}, bf16[2,1040,128]{2,1,0:T(8,128)(2,1)S(1)}, u32[]{:S(2)}, u32[]{:S(2)}) collective-permute-start(bf16[2,1040,128]{2,1,0:T(8,128)(2,1)S(1)} %collective-permute-done.9.refs_3_.refs_1_), channel_id=1, source_target_pairs={{0,1},{1,0},{2,3},{3,2},{4,5},{5,4},{6,7},{7,6},{8,9},{9,8},{10,11... | collective-permute-start | bytes 1597448 | tf_op jit(solution)/shard_map/ppermute | solution.py:314
  37.4 13.8 %collective-permute-start.18 = (bf16[2,1040,128]{2,1,0:T(8,128)(2,1)S(1)}, bf16[2,1040,128]{2,1,0:T(8,128)(2,1)S(1)}, u32[]{:S(2)}, u32[]{:S(2)}) collective-permute-start(bf16[2,1040,128]{2,1,0:T(8,128)(2,1)S(1)} %collective-permute-done.9.refs_3_.refs_1_), channel_id=1, source_target_pairs={{4,6},{3,1},{12,14},{11,9},{20,22},{19,17},{28,30},{27,25}} | collective-permute-start | bytes 1597448 | tf_op jit(solution)/shard_map/ppermute | solution.py:314
  39.0 11.8 %collective-permute-start.11 = (f32[72,192]{1,0:T(8,128)S(1)}, f32[72,192]{1,0:T(8,128)S(1)}, u32[]{:S(2)}, u32[]{:S(2)}) collective-permute-start(f32[72,192]{1,0:T(8,128)S(1)} %add_add_fusion), channel_id=1, source_target_pairs={{0,2},{1,3},{2,0},{3,1},{4,6},{5,7},{6,4},{7,5},{8,10},{9,11},{10,... | collective-permute-start | bytes 165896 | tf_op jit(solution)/shard_map/ppermute | solution.py:314
  42.5 8.7 %collective-permute-start.12 = (f32[72,192]{1,0:T(8,128)S(1)}, f32[72,192]{1,0:T(8,128)S(1)}, u32[]{:S(2)}, u32[]{:S(2)}) collective-permute-start(f32[72,192]{1,0:T(8,128)S(1)} %add_add_fusion), channel_id=1, source_target_pairs={{0,4},{1,5},{2,6},{3,7},{4,0},{5,1},{6,2},{7,3},{8,12},{9,13},{10,... | collective-permute-start | bytes 165896 | tf_op jit(solution)/shard_map/ppermute | solution.py:314
  44.4 6.8 %collective-permute-start.13 = (f32[72,192]{1,0:T(8,128)S(1)}, f32[72,192]{1,0:T(8,128)S(1)}, u32[]{:S(2)}, u32[]{:S(2)}) collective-permute-start(f32[72,192]{1,0:T(8,128)S(1)} %add_add_fusion), channel_id=1, source_target_pairs={{0,6},{1,7},{2,4},{3,5},{4,2},{5,3},{6,0},{7,1},{8,14},{9,15},{10,... | collective-permute-start | bytes 165896 | tf_op jit(solution)/shard_map/ppermute | solution.py:314
  51.2 5.9 %collective-permute-start.19 = (bf16[2,1040,128]{2,1,0:T(8,128)(2,1)S(1)}, bf16[2,1040,128]{2,1,0:T(8,128)(2,1)S(1)}, u32[]{:S(2)}, u32[]{:S(2)}) collective-permute-start(bf16[2,1040,128]{2,1,0:T(8,128)(2,1)S(1)} %collective-permute-done.18.refs_3_), channel_id=1, source_target_pairs={{0,1},{1,0},{2,3},{3,2},{4,5},{5,4},{6,7},{7,6},{8,9},{9,8},{10,11... | collective-permute-start | bytes 1597448 | tf_op jit(solution)/shard_map/ppermute | solution.py:314
  53.6 8.5 %collective-permute-start.14 = (f32[72,192]{1,0:T(8,128)S(1)}, f32[72,192]{1,0:T(8,128)S(1)}, u32[]{:S(2)}, u32[]{:S(2)}) collective-permute-start(f32[72,192]{1,0:T(8,128)S(1)} %add_multiply_fusion), channel_id=1, source_target_pairs={{0,8},{8,0},{16,24},{24,16},{1,9},{9,1},{17,25},{25,17},{2,10},{10... | collective-permute-start | bytes 165896 | tf_op jit(solution)/shard_map/ppermute | solution.py:317
  54.1 8.0 %collective-permute-start.15 = (f32[72,192]{1,0:T(8,128)S(1)}, f32[72,192]{1,0:T(8,128)S(1)}, u32[]{:S(2)}, u32[]{:S(2)}) collective-permute-start(f32[72,192]{1,0:T(8,128)S(1)} %add_multiply_fusion), channel_id=1, source_target_pairs={{0,16},{8,24},{16,0},{24,8},{1,17},{9,25},{17,1},{25,9},{2,18},{10... | collective-permute-start | bytes 165896 | tf_op jit(solution)/shard_map/ppermute | solution.py:317
  55.3 6.8 %collective-permute-start.16 = (f32[72,192]{1,0:T(8,128)S(1)}, f32[72,192]{1,0:T(8,128)S(1)}, u32[]{:S(2)}, u32[]{:S(2)}) collective-permute-start(f32[72,192]{1,0:T(8,128)S(1)} %add_multiply_fusion), channel_id=1, source_target_pairs={{0,24},{8,16},{16,8},{24,0},{1,25},{9,17},{17,9},{25,1},{2,26},{10... | collective-permute-start | bytes 165896 | tf_op jit(solution)/shard_map/ppermute | solution.py:317
  60.8 9.3 %collective-permute-start.20 = (bf16[2,8,64,128]{3,2,1,0:T(8,128)(2,1)S(1)}, bf16[2,8,64,128]{3,2,1,0:T(8,128)(2,1)S(1)}, u32[]{:S(2)}, u32[]{:S(2)}) collective-permute-start(bf16[2,8,64,128]{3,2,1,0:T(8,128)(2,1)S(1)} %get-tuple-element.41), channel_id=1, source_target_pairs={{8,0},{16,8},{24,16},{9,1},{17,9},{25,17},{10,2},{18,10},{26,18},{... | collective-permute-start | bytes 786440 | tf_op jit(solution)/shard_map/ppermute | solution.py:317
  62.1 1.6 %collective-permute-start.17 = (f32[4,72,192]{2,1,0:T(8,128)S(1)}, f32[4,72,192]{2,1,0:T(8,128)S(1)}, u32[]{:S(2)}, u32[]{:S(2)}) collective-permute-start(f32[4,72,192]{2,1,0:T(8,128)S(1)} %pad_maximum_fusion.1.mine), channel_id=1, source_target_pairs={{0,1},{1,0},{2,3},{3,2},{4,5},{5,4},{6,7},{7,6},{8,9},{9,8},{10,11... | collective-permute-start | bytes 663560 | tf_op jit(solution)/shard_map/ppermute | solution.py:314
  (2 other events, 1.4 us)
